TPU v7x, 32 devices: a whole 2x2x4 slice. The times are simulated.
32 devices in a mesh: replica: 4 (over y, x), shard: 8 (over z, core).
Axes of the slice: x: 2, y: 2, z: 4, core: 2. Of those that a mesh axis runs over, the one named last changes fastest.
Arguments:
- inputs: bfloat16 [8192, 6144], P(('replica', 'shard')), may hold values from -6 to 6
- doc_ids: int32 [32, 256], P(('replica', 'shard')), may hold values from 0 to 7, never falling along the last dimension, each value on 1 to 64 neighbouring positions
- values: bfloat16 [8192, 128], P(('replica', 'shard')), may hold values from -6 to 6
- cotangent: bfloat16 [8192, 128], P(('replica', 'shard')), may hold values from -24 to 24
- weights: float32 [24576, 256], P(('replica', 'shard')), may hold values from -6 to 6
- moment1: float32 [24576, 256], P(('replica', 'shard')), may hold values from -3 to 3
- moment2: float32 [24576, 256], P(('replica', 'shard')), may hold values from 0.05 to 2
- frag_local: bfloat16 [4, 16, 8, 6144], P('replica', None, 'shard'), may hold values from -6 to 6
- frag_global: float32 [16, 8, 6144], P(None, 'shard'), may hold values from -6 to 6
- frag_moment: float32 [16, 8, 6144], P(None, 'shard'), may hold values from -3 to 3
- frag_index: int32 [1], replicated, may hold values from 0 to 15
Outputs:
- new_weights: float32 [24576, 256], P(('replica', 'shard'))
- new_moment1: float32 [24576, 256], P(('replica', 'shard'))
- new_moment2: float32 [24576, 256], P(('replica', 'shard'))
- new_global: float32 [8, 6144], P('shard')
- new_moment: float32 [8, 6144], P('shard')
Inputs may be any that keep to these rules, and one draw needn't show every extreme that they name: `doc_ids`: within each row document numbers start at 0, never fall, and each document has 1 to 64 tokens; some document has exactly 64.
All inputs are finite; a program needn't handle non-finite values.
Results may differ from a plain program's by a relative error of at most 0.008.
Values may be sent and summed in bfloat16 or wider, within the bound.
No kernel may reach another device: no remote copies, remote signals or barrier semaphores. Data moves between devices by JAX's collectives and lax.ppermute only.
A program may use at most 64 MiB of HBM per device.

v0:
```python
import math

import jax
import jax.numpy as jnp
from jax import lax
from jax.sharding import PartitionSpec as P

ADAM_STEP = 100


epsilon = 1e-06
beta_one = 0.9
beta_two = 0.95
learn_rate = 0.01
decay_rate = 0.1
outer_momentum = 0.9
outer_rate = 0.7


def head_grads(inputs, doc_ids, values, cotangent, projected):
    model_width = inputs.shape[1]
    head_size = values.shape[1]
    input_scale = 1.0 / math.sqrt(model_width)
    score_scale = 1.0 / math.sqrt(head_size)
    scaled = projected * input_scale
    queries = scaled[:, :head_size]
    keys_part = scaled[:, head_size:]
    q_rate = lax.rsqrt(jnp.mean(queries * queries, axis=1, keepdims=True) + epsilon)
    k_rate = lax.rsqrt(jnp.mean(keys_part * keys_part, axis=1, keepdims=True) + epsilon)
    q_unit = queries * q_rate
    k_unit = keys_part * k_rate
    scores = jnp.dot(q_unit, k_unit.T, precision=lax.Precision.HIGHEST) * score_scale
    position = jnp.arange(doc_ids.shape[0])
    allowed = (doc_ids[:, None] == doc_ids[None, :]) & (position[None, :] <= position[:, None])
    raised = jnp.where(allowed, jnp.exp(scores), jnp.float32(0.0))
    attention = raised / jnp.sum(raised, axis=1, keepdims=True)
    grad_attention = jnp.dot(cotangent, values.T, preferred_element_type=jnp.float32)
    grad_scores = (
        attention
        * (grad_attention - jnp.sum(attention * grad_attention, axis=1, keepdims=True))
        * score_scale
    )
    grad_qunit = jnp.dot(grad_scores, k_unit, precision=lax.Precision.HIGHEST)
    grad_kunit = jnp.dot(grad_scores.T, q_unit, precision=lax.Precision.HIGHEST)
    grad_query = q_rate * (
        grad_qunit - q_unit * jnp.mean(grad_qunit * q_unit, axis=1, keepdims=True)
    )
    grad_keys = k_rate * (
        grad_kunit - k_unit * jnp.mean(grad_kunit * k_unit, axis=1, keepdims=True)
    )
    return (jnp.concatenate([grad_query, grad_keys], axis=1) * input_scale).astype(jnp.bfloat16)


def inner_step(inputs, doc_ids, values, cotangent, weights, moment1, moment2):
    lowered = weights.astype(jnp.bfloat16)
    gathered = lax.all_gather(lowered, "shard", axis=0, tiled=True)
    projected = jnp.dot(inputs, gathered, preferred_element_type=jnp.float32)
    grad_projected = head_grads(inputs, doc_ids[0], values, cotangent, projected)
    grad_term = lax.dot_general(
        inputs, grad_projected, (((0,), (0,)), ((), ())), preferred_element_type=jnp.float32
    )
    gradient = lax.psum_scatter(
        grad_term.astype(jnp.bfloat16), "shard", scatter_dimension=0, tiled=True
    ).astype(jnp.float32)
    first_new = beta_one * moment1 + (1.0 - beta_one) * gradient
    second_new = beta_two * moment2 + (1.0 - beta_two) * gradient * gradient
    first_hat = first_new / (1.0 - beta_one**ADAM_STEP)
    second_hat = second_new / (1.0 - beta_two**ADAM_STEP)
    weight_new = weights - learn_rate * (
        first_hat / (jnp.sqrt(second_hat) + 1e-08) + decay_rate * weights
    )
    return (weight_new, first_new, second_new)


def outer_step(frag_local, frag_global, frag_moment, frag_index):
    chosen = frag_index[0]
    current = lax.dynamic_index_in_dim(frag_global, chosen, 0, keepdims=False)
    moment_now = lax.dynamic_index_in_dim(frag_moment, chosen, 0, keepdims=False)
    local_copy = lax.dynamic_index_in_dim(frag_local[0], chosen, 0, keepdims=False)
    lowered_drift = lax.optimization_barrier(
        (current - local_copy.astype(jnp.float32)).astype(jnp.bfloat16)
    )
    drift = lowered_drift.astype(jnp.float32)
    replicas = lax.axis_size("replica")
    drift_mean = lax.psum(drift, "replica") / replicas
    new_moment = outer_momentum * moment_now + drift_mean
    new_global = current - outer_rate * (drift_mean + outer_momentum * new_moment)
    return (new_global, new_moment)


def on_device(
    inputs,
    doc_ids,
    values,
    cotangent,
    weights,
    moment1,
    moment2,
    frag_local,
    frag_global,
    frag_moment,
    frag_index,
):
    new_weights, new_moment1, new_moment2 = inner_step(
        inputs, doc_ids, values, cotangent, weights, moment1, moment2
    )
    new_global, new_moment = outer_step(frag_local, frag_global, frag_moment, frag_index)
    return (new_weights, new_moment1, new_moment2, new_global, new_moment)


def solution(mesh):
    placed = (
        P(("replica", "shard"), None),
        P(("replica", "shard"), None),
        P(("replica", "shard"), None),
        P(("replica", "shard"), None),
        P(("replica", "shard"), None),
        P(("replica", "shard"), None),
        P(("replica", "shard"), None),
        P("replica", None, "shard", None),
        P(None, "shard", None),
        P(None, "shard", None),
        P(),
    )
    return jax.shard_map(
        on_device,
        mesh=mesh,
        in_specs=placed,
        out_specs=(
            P(("replica", "shard"), None),
            P(("replica", "shard"), None),
            P(("replica", "shard"), None),
            P("shard", None),
            P("shard", None),
        ),
        check_vma=False,
    )
```

profile of v0, /device:TPU:0, one launch (start us, length us, event | category | flops | bytes accessed | tf_op | source)
XLA Modules:
  0.0 115.3 jit_solution(11375689508416129361)
XLA Ops:
  7.2 0.0 all-gather.2.cloned.1.call-start
  7.2 2.1 %convert_element_type.43 = bf16[768,256]{1,0:T(8,128)(2,1)} convert(f32[768,256]{1,0:T(8,128)} %param.15) | non-fusion elementwise | flops 196608 | bytes 1179648 | tf_op jit(solution)/shard_map/convert_element_type | solution.py:55
  9.3 0.0 all-gather.2.cloned.1.call-update
  9.4 0.0 reduce-scatter.2.cloned.1.call-start
  9.4 41.8 %all-gather.2.cloned.1.call-done = bf16[6144,256]{1,0:T(8,128)(2,1)} async-done(((bf16[768,256]{1,0:T(8,128)(2,1)}), bf16[6144,256]{1,0:T(8,128)(2,1)}) %all-gather.2.cloned.1.call-update) | async-done | bytes 3145744 | tf_op jit(solution)/shard_map/all_gather | solution.py:56
  51.2 3.2 %convolution_multiply_fusion.1 = f32[256,256]{0,1:T(8,128)S(1)} fusion(bf16[256,6144]{1,0:T(8,128)(2,1)S(1)} %copy-done, bf16[6144,256]{1,0:T(8,128)(2,1)} %all-gather.2.cloned.1.call-done), kind=kOutput, calls=%fused_computation.6 | convolution fusion | flops 805371904 | bytes 6553600 | tf_op jit(solution)/shard_map/dot_general | solution.py:57
  54.5 0.4 fusion.20
  55.0 0.2 multiply_reduce_fusion
  55.2 0.4 fusion.9
  55.7 0.3 multiply_reduce_fusion.2
  56.0 0.1 subtract_multiply_fusion.1
  56.1 2.7 %fusion = bf16[6144,256]{0,1:T(8,128)(2,1)} fusion(bf16[256,6144]{1,0:T(8,128)(2,1)S(1)} %copy-done, f32[256,128]{0,1:T(8,128)S(1)} %get-tuple-element.20, f32[256,128]{0,1:T(8,128)S(1)} %get-tuple-element.19), kind=kOutput, calls=%fused_computation.1 | convolution fusion | flops 807075840 | bytes 6553600 | tf_op jit(solution)/shard_map/dot_general | solution.py:59
  58.8 0.0 reduce-scatter.2.cloned.1.call-update
  58.8 2.3 %copy.19 = f32[768,256]{0,1:T(8,128)} copy(f32[768,256]{1,0:T(8,128)} %param.15) | data formatting | bytes 1572864 | tf_op args[4]
  61.1 2.3 %copy.16 = f32[768,256]{0,1:T(8,128)} copy(f32[768,256]{1,0:T(8,128)} %param.16) | data formatting | bytes 1572864 | tf_op args[5]
  63.4 2.3 %copy.17 = f32[768,256]{0,1:T(8,128)} copy(f32[768,256]{1,0:T(8,128)} %param.17) | data formatting | bytes 1572864 | tf_op args[6]
  66.3 0.9 fusion.15
  67.3 19.9 %psum.7 = f32[1,6144]{1,0:T(1,128)S(1)} all-reduce(bf16[1,6144]{1,0:T(2,128)(2,1)S(1)} %fusion.15), channel_id=1, replica_groups=mesh['replica'=4,'shard'=8] {'replica'}, use_global_device_ids=true, to_apply=%region_7.8 | all-reduce | flops 6144 | bytes 36864 | tf_op jit(solution)/shard_map/psum | solution.py:85
  87.2 1.5 %bitcast_subtract_fusion = (f32[1,6144]{1,0:T(1,128)}, f32[1,6144]{1,0:T(1,128)}) fusion(f32[1,6144]{1,0:T(1,128)S(1)} %psum.7, f32[16,1,6144]{2,1,0:T(1,128)} %param.19, s32[]{:T(128)S(6)} %select_n.12, f32[16,1,6144]{2,1,0:T(1,128)} %param.20), kind=kLoop, calls=%fused_computation.36 | loop fusion | flops 43008 | bytes 122884 | tf_op jit(solution)/shard_map/sub | solution.py:87
  88.7 9.5 %reduce-scatter.2.cloned.1.call-done = bf16[768,256]{0,1:T(8,128)(2,1)} async-done(((bf16[6144,256]{0,1:T(8,128)(2,1)}), bf16[768,256]{0,1:T(8,128)(2,1)}) %reduce-scatter.2.cloned.1.call-update) | async-done | bytes 393232 | tf_op jit(solution)/shard_map/reduce_scatter | solution.py:62
  98.1 3.5 %multiply_subtract_fusion = (f32[768,256]{0,1:T(8,128)}, f32[768,256]{0,1:T(8,128)}, f32[768,256]{0,1:T(8,128)}) fusion(f32[768,256]{0,1:T(8,128)} %copy.19, bf16[768,256]{0,1:T(8,128)(2,1)} %reduce-scatter.2.cloned.1.call-done, f32[768,256]{0,1:T(8,128)} %copy.16, f32[768,256]{0,1:T(8,128)} %copy.17), kind=kLoop, calls=%fused_computation.10 | loop fusion | flops 3145728 | bytes 5111808 | tf_op jit(solution)/shard_map/sub | solution.py:69
  101.7 2.3 %copy.20 = f32[768,256]{1,0:T(8,128)} copy(f32[768,256]{0,1:T(8,128)} %get-tuple-element.16) | data formatting | bytes 1572864
  103.9 2.3 %copy.21 = f32[768,256]{1,0:T(8,128)} copy(f32[768,256]{0,1:T(8,128)} %get-tuple-element.17) | data formatting | bytes 1572864
  106.2 2.3 %copy.22 = f32[768,256]{1,0:T(8,128)} copy(f32[768,256]{0,1:T(8,128)} %get-tuple-element.18) | data formatting | bytes 1572864
  (12 shorter events, 0.1 us)
Async XLA Ops:
  7.2 44.1 %copy-start = (bf16[256,6144]{1,0:T(8,128)(2,1)S(1)}, bf16[256,6144]{1,0:T(8,128)(2,1)}, u32[]{:S(2)}) copy-start(bf16[256,6144]{1,0:T(8,128)(2,1)} %param.11) | copy-start | bytes 9437188
  7.2 44.1 %all-gather.2.cloned.1.call-start = ((), (), s32[]{:S(2)}) async-start(), calls=%async_computation.1 | async-start | bytes 3538944 | tf_op jit(solution)/shard_map/all_gather | solution.py:56
  9.3 45.2 %copy-start.3 = (s32[1,256]{1,0:T(1,128)S(1)}, s32[1,256]{1,0:T(1,128)}, u32[]{:S(2)}) copy-start(s32[1,256]{1,0:T(1,128)} %param.12) | copy-start | bytes 3076
  9.3 45.7 %copy-start.1 = (bf16[256,128]{1,0:T(8,128)(2,1)S(1)}, bf16[256,128]{1,0:T(8,128)(2,1)}, u32[]{:S(2)}) copy-start(bf16[256,128]{1,0:T(8,128)(2,1)} %param.14) | copy-start | bytes 196612
  9.3 45.7 %copy-start.2 = (bf16[256,128]{1,0:T(8,128)(2,1)S(1)}, bf16[256,128]{1,0:T(8,128)(2,1)}, u32[]{:S(2)}) copy-start(bf16[256,128]{1,0:T(8,128)(2,1)} %param.13) | copy-start | bytes 196612
  9.4 88.8 %reduce-scatter.2.cloned.1.call-start = ((), (), s32[]{:S(2)}) async-start(), calls=%async_computation.2 | async-start | bytes 3538944 | tf_op jit(solution)/shard_map/reduce_scatter | solution.py:62
Sparse Core Ops, SparseCore 0:
  10.2 40.9 all-gather.1
  58.9 39.1 reduce-scatter.1
where the time goes:
time: 116 us; the launch traced here: 115 us
  waiting for transfers between devices  51.3 us (44%)
  blocking collectives  19.9 us (17%)
  between operations  14.8 us (13%)
  local copies, waits for them, and re-layouts  13.8 us (12%)
  other arithmetic  8.1 us (7%)
  matrix products  7.33 us (6%)
    all_gather x1, waiting for transfers between devices, inner_step(): gathered = lax.all_gather(lowered, 'shard', axis=0, tiled=True)  41.8 us
    psum x1, blocking collectives, outer_step(): drift_mean = lax.psum(drift, 'replica') / replicas  19.9 us
    unnamed x14, local copies, waits for them, and re-layouts  13.8 us
    reduce_scatter x1, waiting for transfers between devices, inner_step(): lax.psum_scatter(grad_term.astype(jnp.bfloat16), 'shard', scatter_dimensi...  9.45 us
    sub x1, other arithmetic, inner_step(): weights - learn_rate * (first_hat / (jnp.sqrt(second_hat) + 1e-08) + deca...  3.52 us
    dot_general x1, matrix products, inner_step(): projected = jnp.dot(inputs, gathered, preferred_element_type=jnp.float32)  3.22 us
    dot_general x1, matrix products, inner_step(): lax.dot_general(inputs, grad_projected, (((0,), (0,)), ((), ())), preferr...  2.66 us
  transfers between devices with their start and end apart: 2, of which 2 were waited for; matrix products, arithmetic and copies ran while one was open for 8% of the time, Pallas kernels for 0%

commit v1 on v0

--- a/solution.py
+++ b/solution.py
@@ -6,6 +6,7 @@
 from jax.sharding import PartitionSpec as P
 
 ADAM_STEP = 100
+CHUNKS = 2
 
 
 epsilon = 1e-06
@@ -52,16 +53,61 @@
 
 
 def inner_step(inputs, doc_ids, values, cotangent, weights, moment1, moment2):
-    lowered = weights.astype(jnp.bfloat16)
-    gathered = lax.all_gather(lowered, "shard", axis=0, tiled=True)
-    projected = jnp.dot(inputs, gathered, preferred_element_type=jnp.float32)
-    grad_projected = head_grads(inputs, doc_ids[0], values, cotangent, projected)
-    grad_term = lax.dot_general(
-        inputs, grad_projected, (((0,), (0,)), ((), ())), preferred_element_type=jnp.float32
-    )
-    gradient = lax.psum_scatter(
-        grad_term.astype(jnp.bfloat16), "shard", scatter_dimension=0, tiled=True
-    ).astype(jnp.float32)
+    devices = lax.axis_size("shard")
+    chips = devices // 2
+    here = lax.axis_index("shard")
+    core = here % 2
+    rows = weights.shape[0]
+    part = rows // CHUNKS
+    ring = [(i, (i + 2) % devices) for i in range(devices)]
+    swap = [(i, i ^ 1) for i in range(devices)]
+
+    def ordered(which):
+        return [
+            lax.dynamic_slice_in_dim(
+                inputs, ((here - core - 2 * k) % devices + which) * rows, rows, axis=1
+            )
+            for k in range(chips)
+        ]
+
+    blocks = [weights[j * part : (j + 1) * part].astype(jnp.bfloat16) for j in range(CHUNKS)]
+    flying = [lax.ppermute(block, "shard", ring) for block in blocks]
+    mine = ordered(core)
+    theirs = lax.ppermute(jnp.stack(ordered(1 - core)), "shard", swap)
+    both = [jnp.concatenate([mine[k], theirs[k]], axis=0) for k in range(chips)]
+    total = jnp.float32(0.0)
+    for k in range(chips):
+        for j in range(CHUNKS):
+            total = total + jnp.dot(
+                both[k][:, j * part : (j + 1) * part],
+                blocks[j],
+                preferred_element_type=jnp.float32,
+            )
+        if k < chips - 1:
+            blocks = flying
+            if k < chips - 2:
+                flying = [lax.ppermute(block, "shard", ring) for block in blocks]
+    tokens = inputs.shape[0]
+    projected = total[:tokens] + lax.ppermute(total[tokens:], "shard", swap)
+    grad_own = head_grads(inputs, doc_ids[0], values, cotangent, projected)
+    grad_both = jnp.concatenate([grad_own, lax.ppermute(grad_own, "shard", swap)], axis=0)
+
+    def term(k, j):
+        return lax.dot_general(
+            both[k][:, j * part : (j + 1) * part],
+            grad_both,
+            (((0,), (0,)), ((), ())),
+            preferred_element_type=jnp.float32,
+        )
+
+    sums = [term(1, j).astype(jnp.bfloat16) for j in range(CHUNKS)]
+    for k in range(chips - 1):
+        later = 0 if k == chips - 2 else k + 2
+        for j in range(CHUNKS):
+            sums[j] = lax.ppermute(sums[j], "shard", ring).astype(jnp.float32) + term(later, j)
+            if later:
+                sums[j] = sums[j].astype(jnp.bfloat16)
+    gradient = jnp.concatenate(sums, axis=0)
     first_new = beta_one * moment1 + (1.0 - beta_one) * gradient
     second_new = beta_two * moment2 + (1.0 - beta_two) * gradient * gradient
     first_hat = first_new / (1.0 - beta_one**ADAM_STEP)
@@ -82,7 +128,12 @@
     )
     drift = lowered_drift.astype(jnp.float32)
     replicas = lax.axis_size("replica")
-    drift_mean = lax.psum(drift, "replica") / replicas
+    total = drift
+    step = 1
+    while step < replicas:
+        total = total + lax.ppermute(total, "replica", [(i, i ^ step) for i in range(replicas)])
+        step = 2 * step
+    drift_mean = total / replicas
     new_moment = outer_momentum * moment_now + drift_mean
     new_global = current - outer_rate * (drift_mean + outer_momentum * new_moment)
     return (new_global, new_moment)

time: 116 us -> 76.8 us (0.66)
  blocking collectives: 19.9 us -> 0 us
  between operations: 14.8 us -> 1.78 us
  local copies, waits for them, and re-layouts: 13.8 us -> 3.61 us
  starting transfers between devices: 0.08 us -> 8.37 us
  other arithmetic: 8.1 us -> 5.85 us
  waiting for transfers between devices: 51.3 us -> 49.3 us
    ppermute x0 -> x17, waiting for transfers between devices: none -> 49.3 us  [the longest x6 25.2 us: inner_step(): lax.ppermute(sums[j], 'shard', ring).astype(jnp.float32) + term(later, j)]
    all_gather x1 -> x0, waiting for transfers between devices: 41.8 us -> none  [inner_step(): gathered = lax.all_gather(lowered, 'shard', axis=0, tiled=True)]
    psum x1 -> x0, blocking collectives: 19.9 us -> none  [outer_step(): drift_mean = lax.psum(drift, 'replica') / replicas]
    unnamed x14 -> x12, local copies, waits for them, and re-layouts: 13.8 us -> 0.04 us
    reduce_scatter x1 -> x0, waiting for transfers between devices: 9.45 us -> none  [inner_step(): lax.psum_scatter(grad_term.astype(jnp.bfloat16), 'shard', scatter_dimensi...]
    ppermute x0 -> x17, starting transfers between devices: none -> 8.37 us  [the longest x6 4.31 us: inner_step(): flying = [lax.ppermute(block, 'shard', ring) for block in blocks]]
    dynamic_slice x0 -> x1, local copies, waits for them, and re-layouts: none -> 2.06 us  [ordered(): lax.dynamic_slice_in_dim(inputs, ((here - core - 2 * k) % devices + which...]
    convert_element_type x1 -> x2, other arithmetic: 2.07 us -> 0.05 us  [the longest x1 0.03 us: outer_step(): drift = lowered_drift.astype(jnp.float32)]
  transfers between devices with their start and end apart: 2 -> 17, of which waited for: 2 -> 13; matrix products, arithmetic and copies ran while one was open for 8% -> 15% of each run, Pallas kernels for 0% -> 0%
where the time goes in v1:
time: 76.8 us; the launch traced here: 76.5 us
  waiting for transfers between devices  49.3 us (64%)
  starting transfers between devices  8.37 us (11%)
  matrix products  7.61 us (10%)
  other arithmetic  5.85 us (8%)
  local copies, waits for them, and re-layouts  3.61 us (5%)
  between operations  1.78 us (2%)
    ppermute x6, waiting for transfers between devices, inner_step(): lax.ppermute(sums[j], 'shard', ring).astype(jnp.float32) + term(later, j)  25.2 us
    ppermute x6, waiting for transfers between devices, inner_step(): flying = [lax.ppermute(block, 'shard', ring) for block in blocks]  21.6 us
    ppermute x6, starting transfers between devices, inner_step(): flying = [lax.ppermute(block, 'shard', ring) for block in blocks]  4.31 us
    dot_general x8, matrix products, inner_step(): jnp.dot(both[k][:, j * part:(j + 1) * part], blocks[j], preferred_element...  3.66 us
    ppermute x2, starting transfers between devices, outer_step(): lax.ppermute(total, 'replica', [(i, i ^ step) for i in range(replicas)])  2.93 us
    ppermute x2, waiting for transfers between devices, outer_step(): lax.ppermute(total, 'replica', [(i, i ^ step) for i in range(replicas)])  2.5 us
    dot_general x8, matrix products, term(): lax.dot_general(both[k][:, j * part:(j + 1) * part], grad_both, (((0,), (...  2.49 us
    dynamic_slice x1, local copies, waits for them, and re-layouts, ordered(): lax.dynamic_slice_in_dim(inputs, ((here - core - 2 * k) % devices + which...  2.06 us
  transfers between devices with their start and end apart: 17, of which 13 were waited for; matrix products, arithmetic and copies ran while one was open for 15% of the time, Pallas kernels for 0%

profile of v1, /device:TPU:0, one launch (start us, length us, event | category | flops | bytes accessed | tf_op | source)
XLA Modules:
  0.0 76.5 jit_solution(1422412789987458209)
XLA Ops:
  0.8 2.1 %constant_dynamic-slice_fusion.2 = (bf16[256,768]{1,0:T(8,128)(2,1)S(1)}, bf16[1,256,768]{2,1,0:T(8,128)(2,1)S(1)}, bf16[1,256,768]{2,1,0:T(8,128)(2,1)S(1)}, bf...) fusion(bf16[256,6144]{1,0:T(8,128)(2,1)} %param.11, ...), kind=kLoop, calls=%fused_computation.85 | loop fusion | bytes 6291488 | tf_op jit(solution)/shard_map/dynamic_slice | solution.py:67
  2.8 1.4 %pad_maximum_fusion = bf16[4,256,768]{2,1,0:T(8,128)(2,1)} fusion(bf16[1,256,768]{2,1,0:T(8,128)(2,1)S(1)} %get-tuple-element.15, bf16[1,256,768]{2,1,0:T(8,128)(2,1)S(1)} %get-tuple-element.16, bf16[1,256,768]{2,1,0:T(8,128)(2,1)S(1)} %get-tuple-element.17, bf16[1,256,768]{2,1,0:T(8,128)(2,1)S(1)} %get-tuple-element.18), kind=kLoop, calls=%fused_computation | loop fusion | flops 2359296 | bytes 3145728 | tf_op jit(solution)/shard_map/stack | solution.py:76
  4.8 2.6 %collective-permute-start.2 = (bf16[384,256]{1,0:T(8,128)(2,1)S(1)}, bf16[384,256]{1,0:T(8,128)(2,1)S(1)}, u32[]{:S(2)}, u32[]{:S(2)}) collective-permute-start(bf16[384,256]{1,0:T(8,128)(2,1)S(1)} %get-tuple-element.27), channel_id=1, source_target_pairs={{0,2},{1,3},{2,4},{3,5},{4,6},{5,7},{6,0},{7,1},{8,10},{9,11},{10,... | collective-permute-start | bytes 589832 | tf_op jit(solution)/shard_map/ppermute | solution.py:74
  7.4 1.6 %collective-permute-start.1 = (bf16[384,256]{1,0:T(8,128)(2,1)S(1)}, bf16[384,256]{1,0:T(8,128)(2,1)S(1)}, u32[]{:S(2)}, u32[]{:S(2)}) collective-permute-start(bf16[384,256]{1,0:T(8,128)(2,1)S(1)} %get-tuple-element.26), channel_id=1, source_target_pairs={{0,2},{1,3},{2,4},{3,5},{4,6},{5,7},{6,0},{7,1},{8,10},{9,11},{10,... | collective-permute-start | bytes 589832 | tf_op jit(solution)/shard_map/ppermute | solution.py:74
  9.0 6.2 %collective-permute-done.2 = bf16[384,256]{1,0:T(8,128)(2,1)S(1)} collective-permute-done((bf16[384,256]{1,0:T(8,128)(2,1)S(1)}, bf16[384,256]{1,0:T(8,128)(2,1)S(1)}, u32[]{:S(2)}, u32[]{:S(2)}) %collective-permute-start.2) | collective-permute-done | bytes 196640 | tf_op jit(solution)/shard_map/ppermute | solution.py:74
  15.2 4.0 %collective-permute-done.1 = bf16[384,256]{1,0:T(8,128)(2,1)S(1)} collective-permute-done((bf16[384,256]{1,0:T(8,128)(2,1)S(1)}, bf16[384,256]{1,0:T(8,128)(2,1)S(1)}, u32[]{:S(2)}, u32[]{:S(2)}) %collective-permute-start.1) | collective-permute-done | bytes 196640 | tf_op jit(solution)/shard_map/ppermute | solution.py:74
  20.0 3.7 %collective-permute-done.4 = bf16[384,256]{1,0:T(8,128)(2,1)} collective-permute-done((bf16[384,256]{1,0:T(8,128)(2,1)S(1)}, bf16[384,256]{1,0:T(8,128)(2,1)}, u32[]{:S(2)}, u32[]{:S(2)}) %collective-permute-start.4) | collective-permute-done | bytes 196640 | tf_op jit(solution)/shard_map/ppermute | solution.py:89
  23.6 4.7 %collective-permute-done.3 = bf16[384,256]{1,0:T(8,128)(2,1)S(1)} collective-permute-done((bf16[384,256]{1,0:T(8,128)(2,1)S(1)}, bf16[384,256]{1,0:T(8,128)(2,1)S(1)}, u32[]{:S(2)}, u32[]{:S(2)}) %collective-permute-start.3) | collective-permute-done | bytes 196640 | tf_op jit(solution)/shard_map/ppermute | solution.py:89
  28.3 1.5 %slice_bitcast_fusion.2 = (bf16[256,768]{1,0:T(8,128)(2,1)S(1)}, bf16[256,768]{1,0:T(8,128)(2,1)S(1)}, bf16[256,768]{1,0:T(8,128)(2,1)S(1)}, bf16[256,768]{1,0:T(8,128)(2,1)S(1)}) fusion(bf16[4,256,768]{2,1,0:T(8,128)(2,1)} %collective-permute-done), kind=kLoop, calls=%fused_computation.36 | loop fusion | bytes 3145728 | tf_op jit(solution)/shard_map/squeeze | solution.py:77
  31.2 1.3 %fusion.21 = f32[512,256]{0,1:T(8,128)S(1)} fusion(bf16[384,256]{1,0:T(8,128)(2,1)} %collective-permute-done.4, bf16[256,768]{1,0:T(8,128)(2,1)S(1)} %get-tuple-element.24, bf16[256,768]{1,0:T(8,128)(2,1)S(1)} %get-tuple-element.21), kind=kOutput, calls=%fused_computation.74 | convolution fusion | flops 101449728 | bytes 1507328 | tf_op jit(solution)/shard_map/dot_general | solution.py:81
  33.2 3.0 %collective-permute-done.5 = bf16[384,256]{1,0:T(8,128)(2,1)S(1)} collective-permute-done((bf16[384,256]{1,0:T(8,128)(2,1)S(1)}, bf16[384,256]{1,0:T(8,128)(2,1)S(1)}, u32[]{:S(2)}, u32[]{:S(2)}) %collective-permute-start.5) | collective-permute-done | bytes 196640 | tf_op jit(solution)/shard_map/ppermute | solution.py:89
  36.6 0.9 %fusion.25 = bf16[1,6144]{1,0:T(2,128)(2,1)S(1)} fusion(bf16[1,16,1,6144]{3,1,2,0:T(8,128)(2,1)} %param.18, s32[]{:T(128)S(6)} %select_n.80, f32[16,1,6144]{2,1,0:T(1,128)} %param.19), kind=kLoop, calls=%fused_computation.79 | loop fusion | flops 18432 | bytes 49156 | tf_op jit(solution)/shard_map/convert_element_type | solution.py:127
  37.6 1.4 %collective-permute-start.15 = (f32[1,6144]{1,0:T(1,128)S(1)}, f32[1,6144]{1,0:T(1,128)S(1)}, u32[]{:S(2)}, u32[]{:S(2)}) collective-permute-start(f32[1,6144]{1,0:T(1,128)S(1)} %convert_element_type.85), channel_id=1, source_target_pairs={{0,8},{8,0},{16,24},{24,16},{1,9},{9,1},{17,25},{25,17},{2,10},{10... | collective-permute-start | bytes 73736 | tf_op jit(solution)/shard_map/ppermute | solution.py:134
  41.0 0.5 collective-permute-done.15
  41.5 1.5 %collective-permute-start.16 = (f32[1,6144]{1,0:T(1,128)S(1)}, f32[1,6144]{1,0:T(1,128)S(1)}, u32[]{:S(2)}, u32[]{:S(2)}) collective-permute-start(f32[1,6144]{1,0:T(1,128)S(1)} %convert_add_fusion.2), channel_id=1, source_target_pairs={{0,16},{8,24},{16,0},{24,8},{1,17},{9,25},{17,1},{25,9},{2,18},{10... | collective-permute-start | bytes 73736 | tf_op jit(solution)/shard_map/ppermute | solution.py:134
  43.4 2.0 %collective-permute-done.16 = f32[1,6144]{1,0:T(1,128)S(1)} collective-permute-done((f32[1,6144]{1,0:T(1,128)S(1)}, f32[1,6144]{1,0:T(1,128)S(1)}, u32[]{:S(2)}, u32[]{:S(2)}) %collective-permute-start.16) | collective-permute-done | bytes 24608 | tf_op jit(solution)/shard_map/ppermute | solution.py:134
  45.4 1.5 %bitcast_subtract_fusion = (f32[1,6144]{1,0:T(1,128)}, f32[1,6144]{1,0:T(1,128)}) fusion(f32[16,1,6144]{2,1,0:T(1,128)} %param.19, s32[]{:T(128)S(6)} %select_n.80, f32[1,6144]{1,0:T(1,128)S(1)} %convert_add_fusion.2, f32[1,6144]{1,0:T(1,128)S(1)} %collective-permute-done.16, f32[16,1,6144]{2,1,0:T(1,128)} %param.20), kind=kLoop, calls=%fused_computation.81 | loop fusion | flops 49152 | bytes 147460 | tf_op jit(solution)/shard_map/sub | solution.py:138
  47.3 5.6 %collective-permute-done.9 = bf16[384,256]{1,0:T(8,128)(2,1)S(1)} collective-permute-done((bf16[384,256]{1,0:T(8,128)(2,1)S(1)}, bf16[384,256]{1,0:T(8,128)(2,1)S(1)}, u32[]{:S(2)}, u32[]{:S(2)}) %collective-permute-start.9) | collective-permute-done | bytes 196640 | tf_op jit(solution)/shard_map/ppermute | solution.py:107
  53.3 3.2 %collective-permute-done.12 = bf16[384,256]{1,0:T(8,128)(2,1)S(1)} collective-permute-done((bf16[384,256]{1,0:T(8,128)(2,1)S(1)}, bf16[384,256]{1,0:T(8,128)(2,1)S(1)}, u32[]{:S(2)}, u32[]{:S(2)}) %collective-permute-start.12) | collective-permute-done | bytes 196640 | tf_op jit(solution)/shard_map/ppermute | solution.py:107
  56.9 5.1 %collective-permute-done.10 = bf16[384,256]{1,0:T(8,128)(2,1)S(1)} collective-permute-done((bf16[384,256]{1,0:T(8,128)(2,1)S(1)}, bf16[384,256]{1,0:T(8,128)(2,1)S(1)}, u32[]{:S(2)}, u32[]{:S(2)}) %collective-permute-start.10) | collective-permute-done | bytes 196640 | tf_op jit(solution)/shard_map/ppermute | solution.py:107
  62.3 4.1 %collective-permute-done.13 = bf16[384,256]{1,0:T(8,128)(2,1)S(1)} collective-permute-done((bf16[384,256]{1,0:T(8,128)(2,1)S(1)}, bf16[384,256]{1,0:T(8,128)(2,1)S(1)}, u32[]{:S(2)}, u32[]{:S(2)}) %collective-permute-start.13) | collective-permute-done | bytes 196640 | tf_op jit(solution)/shard_map/ppermute | solution.py:107
  66.9 4.5 %collective-permute-done.11 = bf16[384,256]{1,0:T(8,128)(2,1)S(1)} collective-permute-done((bf16[384,256]{1,0:T(8,128)(2,1)S(1)}, bf16[384,256]{1,0:T(8,128)(2,1)S(1)}, u32[]{:S(2)}, u32[]{:S(2)}) %collective-permute-start.11) | collective-permute-done | bytes 196640 | tf_op jit(solution)/shard_map/ppermute | solution.py:107
  71.7 2.7 %collective-permute-done.14 = bf16[384,256]{1,0:T(8,128)(2,1)S(1)} collective-permute-done((bf16[384,256]{1,0:T(8,128)(2,1)S(1)}, bf16[384,256]{1,0:T(8,128)(2,1)S(1)}, u32[]{:S(2)}, u32[]{:S(2)}) %collective-permute-start.14) | collective-permute-done | bytes 196640 | tf_op jit(solution)/shard_map/ppermute | solution.py:107
  74.7 1.8 %multiply_subtract_fusion = (f32[768,256]{1,0:T(8,128)}, f32[768,256]{1,0:T(8,128)}, f32[768,256]{1,0:T(8,128)}) fusion(f32[768,256]{1,0:T(8,128)S(1)} %copy-done.1, f32[384,256]{1,0:T(8,128)S(1)} %convert_add_fusion, f32[384,256]{1,0:T(8,128)S(1)} %convert_add_fusion.1, f32[768,256]{1,0:T(8,128)S(1)} %copy-done.2, f32[768,256]{1,0:T(8,128)S(1)} %copy-done.3), kind=kLoop, calls=%fused_computation.24 | loop fusion | flops 3145728 | bytes 5505024 | tf_op jit(solution)/shard_map/sub | solution.py:115
  (60 shorter events, 8.0 us)
Async XLA Ops:
  0.6 39.0 %copy-start = (bf16[256,128]{1,0:T(8,128)(2,1)S(1)}, bf16[256,128]{1,0:T(8,128)(2,1)}, u32[]{:S(2)}) copy-start(bf16[256,128]{1,0:T(8,128)(2,1)} %param.14) | copy-start | bytes 196612
  2.8 1.8 %copy-start.1 = (f32[768,256]{1,0:T(8,128)S(1)}, f32[768,256]{1,0:T(8,128)}, u32[]{:S(2)}) copy-start(f32[768,256]{1,0:T(8,128)} %param.15) | copy-start | bytes 2359300
  4.2 24.1 %collective-permute-start = (bf16[4,256,768]{2,1,0:T(8,128)(2,1)}, bf16[4,256,768]{2,1,0:T(8,128)(2,1)}, u32[]{:S(2)}, u32[]{:S(2)}) collective-permute-start(bf16[4,256,768]{2,1,0:T(8,128)(2,1)} %pad_maximum_fusion), channel_id=1, source_target_pairs={{0,1},{1,0},{2,3},{3,2},{4,5},{5,4},{6,7},{7,6},{8,9},{9,8},{10,11... | collective-permute-start | bytes 4718600 | tf_op jit(solution)/shard_map/ppermute | solution.py:76
  4.8 10.4 %collective-permute-start.2 = (bf16[384,256]{1,0:T(8,128)(2,1)S(1)}, bf16[384,256]{1,0:T(8,128)(2,1)S(1)}, u32[]{:S(2)}, u32[]{:S(2)}) collective-permute-start(bf16[384,256]{1,0:T(8,128)(2,1)S(1)} %get-tuple-element.27), channel_id=1, source_target_pairs={{0,2},{1,3},{2,4},{3,5},{4,6},{5,7},{6,0},{7,1},{8,10},{9,11},{10,... | collective-permute-start | bytes 589832 | tf_op jit(solution)/shard_map/ppermute | solution.py:74
  7.4 11.8 %collective-permute-start.1 = (bf16[384,256]{1,0:T(8,128)(2,1)S(1)}, bf16[384,256]{1,0:T(8,128)(2,1)S(1)}, u32[]{:S(2)}, u32[]{:S(2)}) collective-permute-start(bf16[384,256]{1,0:T(8,128)(2,1)S(1)} %get-tuple-element.26), channel_id=1, source_target_pairs={{0,2},{1,3},{2,4},{3,5},{4,6},{5,7},{6,0},{7,1},{8,10},{9,11},{10,... | collective-permute-start | bytes 589832 | tf_op jit(solution)/shard_map/ppermute | solution.py:74
  15.2 8.5 %collective-permute-start.4 = (bf16[384,256]{1,0:T(8,128)(2,1)S(1)}, bf16[384,256]{1,0:T(8,128)(2,1)}, u32[]{:S(2)}, u32[]{:S(2)}) collective-permute-start(bf16[384,256]{1,0:T(8,128)(2,1)S(1)} %collective-permute-done.2), channel_id=1, source_target_pairs={{0,2},{1,3},{2,4},{3,5},{4,6},{5,7},{6,0},{7,1},{8,10},{9,11},{10,... | collective-permute-start | bytes 589832 | tf_op jit(solution)/shard_map/ppermute | solution.py:89
  19.2 9.1 %collective-permute-start.3 = (bf16[384,256]{1,0:T(8,128)(2,1)S(1)}, bf16[384,256]{1,0:T(8,128)(2,1)S(1)}, u32[]{:S(2)}, u32[]{:S(2)}) collective-permute-start(bf16[384,256]{1,0:T(8,128)(2,1)S(1)} %collective-permute-done.1), channel_id=1, source_target_pairs={{0,2},{1,3},{2,4},{3,5},{4,6},{5,7},{6,0},{7,1},{8,10},{9,11},{10,... | collective-permute-start | bytes 589832 | tf_op jit(solution)/shard_map/ppermute | solution.py:89
  23.6 9.2 %collective-permute-start.6 = (bf16[384,256]{1,0:T(8,128)(2,1)}, bf16[384,256]{1,0:T(8,128)(2,1)S(1)}, u32[]{:S(2)}, u32[]{:S(2)}) collective-permute-start(bf16[384,256]{1,0:T(8,128)(2,1)} %collective-permute-done.4), channel_id=1, source_target_pairs={{0,2},{1,3},{2,4},{3,5},{4,6},{5,7},{6,0},{7,1},{8,10},{9,11},{10,... | collective-permute-start | bytes 589832 | tf_op jit(solution)/shard_map/ppermute | solution.py:89
  28.3 7.9 %collective-permute-start.5 = (bf16[384,256]{1,0:T(8,128)(2,1)S(1)}, bf16[384,256]{1,0:T(8,128)(2,1)S(1)}, u32[]{:S(2)}, u32[]{:S(2)}) collective-permute-start(bf16[384,256]{1,0:T(8,128)(2,1)S(1)} %collective-permute-done.3), channel_id=1, source_target_pairs={{0,2},{1,3},{2,4},{3,5},{4,6},{5,7},{6,0},{7,1},{8,10},{9,11},{10,... | collective-permute-start | bytes 589832 | tf_op jit(solution)/shard_map/ppermute | solution.py:89
  33.2 6.0 %copy-start.5 = (s32[1,256]{1,0:T(1,128)S(1)}, s32[1,256]{1,0:T(1,128)}, u32[]{:S(2)}) copy-start(s32[1,256]{1,0:T(1,128)} %param.12) | copy-start | bytes 3076
  36.5 3.1 %copy-start.4 = (bf16[256,128]{1,0:T(8,128)(2,1)S(1)}, bf16[256,128]{1,0:T(8,128)(2,1)}, u32[]{:S(2)}) copy-start(bf16[256,128]{1,0:T(8,128)(2,1)} %param.13) | copy-start | bytes 196612
  36.5 2.5 %collective-permute-start.7 = (f32[256,256]{0,1:T(8,128)S(1)}, f32[256,256]{0,1:T(8,128)S(1)}, u32[]{:S(2)}, u32[]{:S(2)}) collective-permute-start(f32[256,256]{0,1:T(8,128)S(1)} %slice.97), channel_id=1, source_target_pairs={{0,1},{1,0},{2,3},{3,2},{4,5},{5,4},{6,7},{7,6},{8,9},{9,8},{10,11... | collective-permute-start | bytes 786440 | tf_op jit(solution)/shard_map/ppermute | solution.py:91
  37.6 3.9 %collective-permute-start.15 = (f32[1,6144]{1,0:T(1,128)S(1)}, f32[1,6144]{1,0:T(1,128)S(1)}, u32[]{:S(2)}, u32[]{:S(2)}) collective-permute-start(f32[1,6144]{1,0:T(1,128)S(1)} %convert_element_type.85), channel_id=1, source_target_pairs={{0,8},{8,0},{16,24},{24,16},{1,9},{9,1},{17,25},{25,17},{2,10},{10... | collective-permute-start | bytes 73736 | tf_op jit(solution)/shard_map/ppermute | solution.py:134
  40.8 2.3 %collective-permute-start.8 = (bf16[256,256]{0,1:T(8,128)(2,1)S(1)}, bf16[256,256]{0,1:T(8,128)(2,1)S(1)}, u32[]{:S(2)}, u32[]{:S(2)}) collective-permute-start(bf16[256,256]{0,1:T(8,128)(2,1)S(1)} %fusion.11), channel_id=1, source_target_pairs={{0,1},{1,0},{2,3},{3,2},{4,5},{5,4},{6,7},{7,6},{8,9},{9,8},{10,11... | collective-permute-start | bytes 393224 | tf_op jit(solution)/shard_map/ppermute | solution.py:93
  41.5 3.9 %collective-permute-start.16 = (f32[1,6144]{1,0:T(1,128)S(1)}, f32[1,6144]{1,0:T(1,128)S(1)}, u32[]{:S(2)}, u32[]{:S(2)}) collective-permute-start(f32[1,6144]{1,0:T(1,128)S(1)} %convert_add_fusion.2), channel_id=1, source_target_pairs={{0,16},{8,24},{16,0},{24,8},{1,17},{9,25},{17,1},{25,9},{2,18},{10... | collective-permute-start | bytes 73736 | tf_op jit(solution)/shard_map/ppermute | solution.py:134
  43.3 9.6 %collective-permute-start.9 = (bf16[384,256]{1,0:T(8,128)(2,1)S(1)}, bf16[384,256]{1,0:T(8,128)(2,1)S(1)}, u32[]{:S(2)}, u32[]{:S(2)}) collective-permute-start(bf16[384,256]{1,0:T(8,128)(2,1)S(1)} %convolution_convert_fusion.1), channel_id=1, source_target_pairs={{0,2},{1,3},{2,4},{3,5},{4,6},{5,7},{6,0},{7,1},{8,10},{9,11},{10,... | collective-permute-start | bytes 589832 | tf_op jit(solution)/shard_map/ppermute | solution.py:107
  47.2 9.3 %collective-permute-start.12 = (bf16[384,256]{1,0:T(8,128)(2,1)S(1)}, bf16[384,256]{1,0:T(8,128)(2,1)S(1)}, u32[]{:S(2)}, u32[]{:S(2)}) collective-permute-start(bf16[384,256]{1,0:T(8,128)(2,1)S(1)} %convolution_convert_fusion), channel_id=1, source_target_pairs={{0,2},{1,3},{2,4},{3,5},{4,6},{5,7},{6,0},{7,1},{8,10},{9,11},{10,... | collective-permute-start | bytes 589832 | tf_op jit(solution)/shard_map/ppermute | solution.py:107
  53.2 8.8 %collective-permute-start.10 = (bf16[384,256]{1,0:T(8,128)(2,1)S(1)}, bf16[384,256]{1,0:T(8,128)(2,1)S(1)}, u32[]{:S(2)}, u32[]{:S(2)}) collective-permute-start(bf16[384,256]{1,0:T(8,128)(2,1)S(1)} %add_convert_fusion.3), channel_id=1, source_target_pairs={{0,2},{1,3},{2,4},{3,5},{4,6},{5,7},{6,0},{7,1},{8,10},{9,11},{10,... | collective-permute-start | bytes 589832 | tf_op jit(solution)/shard_map/ppermute | solution.py:107
  56.8 9.7 %collective-permute-start.13 = (bf16[384,256]{1,0:T(8,128)(2,1)S(1)}, bf16[384,256]{1,0:T(8,128)(2,1)S(1)}, u32[]{:S(2)}, u32[]{:S(2)}) collective-permute-start(bf16[384,256]{1,0:T(8,128)(2,1)S(1)} %add_convert_fusion.1), channel_id=1, source_target_pairs={{0,2},{1,3},{2,4},{3,5},{4,6},{5,7},{6,0},{7,1},{8,10},{9,11},{10,... | collective-permute-start | bytes 589832 | tf_op jit(solution)/shard_map/ppermute | solution.py:107
  62.3 9.1 %collective-permute-start.11 = (bf16[384,256]{1,0:T(8,128)(2,1)S(1)}, bf16[384,256]{1,0:T(8,128)(2,1)S(1)}, u32[]{:S(2)}, u32[]{:S(2)}) collective-permute-start(bf16[384,256]{1,0:T(8,128)(2,1)S(1)} %add_convert_fusion.2), channel_id=1, source_target_pairs={{0,2},{1,3},{2,4},{3,5},{4,6},{5,7},{6,0},{7,1},{8,10},{9,11},{10,... | collective-permute-start | bytes 589832 | tf_op jit(solution)/shard_map/ppermute | solution.py:107
  66.8 7.9 %copy-start.2 = (f32[768,256]{1,0:T(8,128)S(1)}, f32[768,256]{1,0:T(8,128)}, u32[]{:S(2)}) copy-start(f32[768,256]{1,0:T(8,128)} %param.16) | copy-start | bytes 2359300
  66.8 7.9 %copy-start.3 = (f32[768,256]{1,0:T(8,128)S(1)}, f32[768,256]{1,0:T(8,128)}, u32[]{:S(2)}) copy-start(f32[768,256]{1,0:T(8,128)} %param.17) | copy-start | bytes 2359300
  66.8 7.5 %collective-permute-start.14 = (bf16[384,256]{1,0:T(8,128)(2,1)S(1)}, bf16[384,256]{1,0:T(8,128)(2,1)S(1)}, u32[]{:S(2)}, u32[]{:S(2)}) collective-permute-start(bf16[384,256]{1,0:T(8,128)(2,1)S(1)} %add_convert_fusion), channel_id=1, source_target_pairs={{0,2},{1,3},{2,4},{3,5},{4,6},{5,7},{6,0},{7,1},{8,10},{9,11},{10,... | collective-permute-start | bytes 589832 | tf_op jit(solution)/shard_map/ppermute | solution.py:107

commit v2 on v1

--- a/solution.py
+++ b/solution.py
@@ -6,7 +6,7 @@
 from jax.sharding import PartitionSpec as P
 
 ADAM_STEP = 100
-CHUNKS = 2
+CHUNKS = 3
 
 
 epsilon = 1e-06
@@ -52,29 +52,62 @@
     return (jnp.concatenate([grad_query, grad_keys], axis=1) * input_scale).astype(jnp.bfloat16)
 
 
-def inner_step(inputs, doc_ids, values, cotangent, weights, moment1, moment2):
+def outer_start(frag_local, frag_global, frag_moment, frag_index):
+    chosen = frag_index[0]
+    current = lax.dynamic_index_in_dim(frag_global, chosen, 0, keepdims=False)
+    moment_now = lax.dynamic_index_in_dim(frag_moment, chosen, 0, keepdims=False)
+    local_copy = lax.dynamic_index_in_dim(frag_local[0], chosen, 0, keepdims=False)
+    drift = (current - local_copy.astype(jnp.float32)).astype(jnp.bfloat16)
+    return current, moment_now, lax.optimization_barrier(drift).astype(jnp.float32)
+
+
+def exchange(total, step):
+    replicas = lax.axis_size("replica")
+    return total + lax.ppermute(total, "replica", [(i, i ^ step) for i in range(replicas)])
+
+
+def outer_finish(current, moment_now, total):
+    drift_mean = total / lax.axis_size("replica")
+    new_moment = outer_momentum * moment_now + drift_mean
+    new_global = current - outer_rate * (drift_mean + outer_momentum * new_moment)
+    return (new_global, new_moment)
+
+
+def spot_of(chip, chips):
+    back = jnp.where(chip == 0, 0, chips - lax.div(chip, 2))
+    return jnp.where(lax.rem(chip, 2) == 1, lax.div(chip + 1, 2), back)
+
+
+def chip_at(spot, chips):
+    out = jnp.where(spot == 0, 0, 2 * spot - 1)
+    return jnp.where(2 * spot <= chips, out, 2 * (chips - spot))
+
+
+def inner_step(inputs, doc_ids, values, cotangent, weights, moment1, moment2, outer):
     devices = lax.axis_size("shard")
     chips = devices // 2
     here = lax.axis_index("shard")
-    core = here % 2
     rows = weights.shape[0]
     part = rows // CHUNKS
-    ring = [(i, (i + 2) % devices) for i in range(devices)]
+    line = [0] + [i for i in range(chips) if i % 2 == 1] + [i for i in range(chips - 1, 1, -1) if i % 2 == 0]
+    ring = [(2 * line[i] + c, 2 * line[(i + 1) % chips] + c) for i in range(chips) for c in range(2)]
+    core = lax.rem(here, 2)
+    spot = spot_of(lax.div(here, 2), chips)
     swap = [(i, i ^ 1) for i in range(devices)]
 
-    def ordered(which):
-        return [
-            lax.dynamic_slice_in_dim(
-                inputs, ((here - core - 2 * k) % devices + which) * rows, rows, axis=1
-            )
-            for k in range(chips)
-        ]
+    def ordered(tokens, k):
+        chip = chip_at(lax.rem(spot + (chips - k), chips), chips)
+        return lax.dynamic_slice_in_dim(tokens, (2 * chip + core) * rows, rows, axis=1)
 
     blocks = [weights[j * part : (j + 1) * part].astype(jnp.bfloat16) for j in range(CHUNKS)]
     flying = [lax.ppermute(block, "shard", ring) for block in blocks]
-    mine = ordered(core)
-    theirs = lax.ppermute(jnp.stack(ordered(1 - core)), "shard", swap)
-    both = [jnp.concatenate([mine[k], theirs[k]], axis=0) for k in range(chips)]
+    partner = lax.ppermute(inputs, "shard", swap)
+    outer, flying[0] = lax.optimization_barrier((outer, flying[0]))
+    current, moment_now, drift = outer_start(*outer)
+    drift = exchange(drift, 1)
+    both = [
+        jnp.concatenate([ordered(inputs, k), ordered(partner, k)], axis=0) for k in range(chips)
+    ]
     total = jnp.float32(0.0)
     for k in range(chips):
         for j in range(CHUNKS):
@@ -87,6 +120,12 @@
             blocks = flying
             if k < chips - 2:
                 flying = [lax.ppermute(block, "shard", ring) for block in blocks]
+            if k == 0:
+                drift, flying[0] = lax.optimization_barrier((drift, flying[0]))
+                drift = exchange(drift, 2)
+            if k == 1:
+                drift, flying[0] = lax.optimization_barrier((drift, flying[0]))
+                outer_done = outer_finish(current, moment_now, drift)
     tokens = inputs.shape[0]
     projected = total[:tokens] + lax.ppermute(total[tokens:], "shard", swap)
     grad_own = head_grads(inputs, doc_ids[0], values, cotangent, projected)
@@ -115,28 +154,7 @@
     weight_new = weights - learn_rate * (
         first_hat / (jnp.sqrt(second_hat) + 1e-08) + decay_rate * weights
     )
-    return (weight_new, first_new, second_new)
-
-
-def outer_step(frag_local, frag_global, frag_moment, frag_index):
-    chosen = frag_index[0]
-    current = lax.dynamic_index_in_dim(frag_global, chosen, 0, keepdims=False)
-    moment_now = lax.dynamic_index_in_dim(frag_moment, chosen, 0, keepdims=False)
-    local_copy = lax.dynamic_index_in_dim(frag_local[0], chosen, 0, keepdims=False)
-    lowered_drift = lax.optimization_barrier(
-        (current - local_copy.astype(jnp.float32)).astype(jnp.bfloat16)
-    )
-    drift = lowered_drift.astype(jnp.float32)
-    replicas = lax.axis_size("replica")
-    total = drift
-    step = 1
-    while step < replicas:
-        total = total + lax.ppermute(total, "replica", [(i, i ^ step) for i in range(replicas)])
-        step = 2 * step
-    drift_mean = total / replicas
-    new_moment = outer_momentum * moment_now + drift_mean
-    new_global = current - outer_rate * (drift_mean + outer_momentum * new_moment)
-    return (new_global, new_moment)
+    return (weight_new, first_new, second_new) + outer_done
 
 
 def on_device(
@@ -152,11 +170,16 @@
     frag_moment,
     frag_index,
 ):
-    new_weights, new_moment1, new_moment2 = inner_step(
-        inputs, doc_ids, values, cotangent, weights, moment1, moment2
-    )
-    new_global, new_moment = outer_step(frag_local, frag_global, frag_moment, frag_index)
-    return (new_weights, new_moment1, new_moment2, new_global, new_moment)
+    return inner_step(
+        inputs,
+        doc_ids,
+        values,
+        cotangent,
+        weights,
+        moment1,
+        moment2,
+        (frag_local, frag_global, frag_moment, frag_index),
+    )
 
 
 def solution(mesh):

time: 76.8 us -> 70.9 us (0.923)
  waiting for transfers between devices: 49.3 us -> 20.6 us
  starting transfers between devices: 8.37 us -> 31.7 us
    ppermute x6 -> x9, waiting for transfers between devices: 21.6 us -> 5.21 us  [inner_step(): flying = [lax.ppermute(block, 'shard', ring) for block in blocks]]
    ppermute x6 -> x9, starting transfers between devices: 0.35 us -> 12.5 us  [inner_step(): lax.ppermute(sums[j], 'shard', ring).astype(jnp.float32) + term(later, j)]
    ppermute x6 -> x9, waiting for transfers between devices: 25.2 us -> 13.8 us  [inner_step(): lax.ppermute(sums[j], 'shard', ring).astype(jnp.float32) + term(later, j)]
    ppermute x6 -> x9, starting transfers between devices: 4.31 us -> 14.9 us  [inner_step(): flying = [lax.ppermute(block, 'shard', ring) for block in blocks]]
    ppermute x3, waiting for transfers between devices: 2.51 us -> 0.01 us  [the longest x2 0.01 us: exchange(): lax.ppermute(total, 'replica', [(i, i ^ step) for i in range(replicas)])]
    ppermute x1, waiting for transfers between devices: 0.01 us -> 1.52 us  [inner_step(): projected = total[:tokens] + lax.ppermute(total[tokens:], 'shard', swap)]
    squeeze x1 -> x0, local copies, waits for them, and re-layouts: 1.45 us -> none  [inner_step(): both = [jnp.concatenate([mine[k], theirs[k]], axis=0) for k in range(chips)]]
    dynamic_slice x1 -> x2, local copies, waits for them, and re-layouts: 2.06 us -> 2.92 us  [ordered(): lax.dynamic_slice_in_dim(tokens, (2 * chip + core) * rows, rows, axis=1)]
  transfers between devices with their start and end apart: 17 -> 23, of which waited for: 13 -> 13; matrix products, arithmetic and copies ran while one was open for 15% -> 18% of each run, Pallas kernels for 0% -> 0%
where the time goes in v2:
time: 70.9 us; the launch traced here: 70.6 us
  starting transfers between devices  31.7 us (45%)
  waiting for transfers between devices  20.6 us (29%)
  matrix products  8.16 us (12%)
  other arithmetic  5.59 us (8%)
  local copies, waits for them, and re-layouts  3.01 us (4%)
  between operations  1.66 us (2%)
    ppermute x9, starting transfers between devices, inner_step(): flying = [lax.ppermute(block, 'shard', ring) for block in blocks]  14.9 us
    ppermute x9, waiting for transfers between devices, inner_step(): lax.ppermute(sums[j], 'shard', ring).astype(jnp.float32) + term(later, j)  13.8 us
    ppermute x9, starting transfers between devices, inner_step(): lax.ppermute(sums[j], 'shard', ring).astype(jnp.float32) + term(later, j)  12.5 us
    ppermute x9, waiting for transfers between devices, inner_step(): flying = [lax.ppermute(block, 'shard', ring) for block in blocks]  5.21 us
    dot_general x12, matrix products, inner_step(): jnp.dot(both[k][:, j * part:(j + 1) * part], blocks[j], preferred_element...  3.42 us
    ppermute x2, starting transfers between devices, exchange(): lax.ppermute(total, 'replica', [(i, i ^ step) for i in range(replicas)])  3.39 us
    dot_general x12, matrix products, term(): lax.dot_general(both[k][:, j * part:(j + 1) * part], grad_both, (((0,), (...  3.3 us
    dynamic_slice x2, local copies, waits for them, and re-layouts, ordered(): lax.dynamic_slice_in_dim(tokens, (2 * chip + core) * rows, rows, axis=1)  2.92 us
  transfers between devices with their start and end apart: 23, of which 13 were waited for; matrix products, arithmetic and copies ran while one was open for 18% of the time, Pallas kernels for 0%

profile of v2, /device:TPU:0, one launch (start us, length us, event | category | flops | bytes accessed | tf_op | source)
XLA Modules:
  0.0 70.6 jit_solution(2012186483675782689)
XLA Ops:
  2.4 2.6 %collective-permute-start.1 = (bf16[256,256]{1,0:T(8,128)(2,1)S(1)}, bf16[256,256]{1,0:T(8,128)(2,1)S(1)}, u32[]{:S(2)}, u32[]{:S(2)}) collective-permute-start(bf16[256,256]{1,0:T(8,128)(2,1)S(1)} %get-tuple-element.42), channel_id=1, source_target_pairs={{0,2},{1,3},{2,6},{3,7},{6,4},{7,5},{4,0},{5,1},{8,10},{9,11},{10,... | collective-permute-start | bytes 393224 | tf_op jit(solution)/shard_map/ppermute | solution.py:103
  5.0 2.6 %collective-permute-start.2 = (bf16[256,256]{1,0:T(8,128)(2,1)S(1)}, bf16[256,256]{1,0:T(8,128)(2,1)S(1)}, u32[]{:S(2)}, u32[]{:S(2)}) collective-permute-start(bf16[256,256]{1,0:T(8,128)(2,1)S(1)} %get-tuple-element.40), channel_id=1, source_target_pairs={{0,2},{1,3},{2,6},{3,7},{6,4},{7,5},{4,0},{5,1},{8,10},{9,11},{10,... | collective-permute-start | bytes 393224 | tf_op jit(solution)/shard_map/ppermute | solution.py:103
  8.7 1.7 %collective-permute-done.1 = bf16[256,256]{1,0:T(8,128)(2,1)S(1)} collective-permute-done((bf16[256,256]{1,0:T(8,128)(2,1)S(1)}, bf16[256,256]{1,0:T(8,128)(2,1)S(1)}, u32[]{:S(2)}, u32[]{:S(2)}) %collective-permute-start.1) | collective-permute-done | bytes 131104 | tf_op jit(solution)/shard_map/ppermute | solution.py:103
  11.4 1.8 %collective-permute-start.4 = (f32[1,6144]{1,0:T(1,128)S(1)}, f32[1,6144]{1,0:T(1,128)S(1)}, u32[]{:S(2)}, u32[]{:S(2)}) collective-permute-start(f32[1,6144]{1,0:T(1,128)S(1)} %convert_element_type.91), channel_id=1, source_target_pairs={{0,8},{8,0},{16,24},{24,16},{1,9},{9,1},{17,25},{25,17},{2,10},{10... | collective-permute-start | bytes 73736 | tf_op jit(solution)/shard_map/ppermute | solution.py:66
  13.9 1.9 %collective-permute-done.3 = bf16[256,256]{1,0:T(8,128)(2,1)S(1)} collective-permute-done((bf16[256,256]{1,0:T(8,128)(2,1)S(1)}, bf16[256,256]{1,0:T(8,128)(2,1)S(1)}, u32[]{:S(2)}, u32[]{:S(2)}) %collective-permute-start.3) | collective-permute-done | bytes 131104 | tf_op jit(solution)/shard_map/ppermute | solution.py:103
  15.9 1.5 %collective-permute-start.7 = (bf16[256,256]{1,0:T(8,128)(2,1)S(1)}, bf16[256,256]{1,0:T(8,128)(2,1)S(1)}, u32[]{:S(2)}, u32[]{:S(2)}) collective-permute-start(bf16[256,256]{1,0:T(8,128)(2,1)S(1)} %collective-permute-done.3), channel_id=1, source_target_pairs={{0,2},{1,3},{2,6},{3,7},{6,4},{7,5},{4,0},{5,1},{8,10},{9,11},{10,... | collective-permute-start | bytes 393224 | tf_op jit(solution)/shard_map/ppermute | solution.py:122
  17.3 2.8 %collective-permute-start.6 = (bf16[256,256]{1,0:T(8,128)(2,1)S(1)}, bf16[256,256]{1,0:T(8,128)(2,1)S(1)}, u32[]{:S(2)}, u32[]{:S(2)}) collective-permute-start(bf16[256,256]{1,0:T(8,128)(2,1)S(1)} %collective-permute-done.2), channel_id=1, source_target_pairs={{0,2},{1,3},{2,6},{3,7},{6,4},{7,5},{4,0},{5,1},{8,10},{9,11},{10,... | collective-permute-start | bytes 393224 | tf_op jit(solution)/shard_map/ppermute | solution.py:122
  20.2 1.6 %collective-permute-start.8 = (f32[1,6144]{1,0:T(1,128)S(1)}, f32[1,6144]{1,0:T(1,128)S(1)}, u32[]{:S(2)}, u32[]{:S(2)}) collective-permute-start(f32[1,6144]{1,0:T(1,128)S(1)} %convert_add_fusion.3), channel_id=1, source_target_pairs={{0,16},{8,24},{16,0},{24,8},{1,17},{9,25},{17,1},{25,9},{2,18},{10... | collective-permute-start | bytes 73736 | tf_op jit(solution)/shard_map/ppermute | solution.py:66
  21.8 1.5 %constant_dynamic-slice_fusion.5 = (bf16[256,768]{1,0:T(8,128)(2,1)S(1)}, bf16[256,768]{1,0:T(8,128)(2,1)S(1)}, bf16[256,768]{1,0:T(8,128)(2,1)S(1)}, bf16[256,768]{1,0:T(8,128)(2,1)S(1)}) fusion(bf16[256,6144]{1,0:T(8,128)(2,1)} %param.11, s32[]{:T(128)S(6)} %select_n.74, s32[]{:T(128)S(6)} %select_n.71, s32[]{:T(128)S(6)} %select_n.81, s32[]{:T(128)S(6)} %select_n.77), kind=kLoop, calls=%fused_computation.92 | loop fusion | bytes 3145744 | tf_op jit(solution)/shard_map/dynamic_slice | solution.py:100
  23.3 3.0 %collective-permute-start.11 = (bf16[256,256]{1,0:T(8,128)(2,1)S(1)}, bf16[256,256]{1,0:T(8,128)(2,1)S(1)}, u32[]{:S(2)}, u32[]{:S(2)}) collective-permute-start(bf16[256,256]{1,0:T(8,128)(2,1)S(1)} %collective-permute-done.7), channel_id=1, source_target_pairs={{0,2},{1,3},{2,6},{3,7},{6,4},{7,5},{4,0},{5,1},{8,10},{9,11},{10,... | collective-permute-start | bytes 393224 | tf_op jit(solution)/shard_map/ppermute | solution.py:122
  27.5 1.6 %collective-permute-done.9 = bf16[256,256]{1,0:T(8,128)(2,1)S(1)} collective-permute-done((bf16[256,256]{1,0:T(8,128)(2,1)S(1)}, bf16[256,256]{1,0:T(8,128)(2,1)S(1)}, u32[]{:S(2)}, u32[]{:S(2)}) %collective-permute-start.9) | collective-permute-done | bytes 131104 | tf_op jit(solution)/shard_map/ppermute | solution.py:122
  29.1 1.5 %constant_dynamic-slice_fusion.4 = (bf16[256,768]{1,0:T(8,128)(2,1)S(1)}, bf16[256,768]{1,0:T(8,128)(2,1)S(1)}, bf16[256,768]{1,0:T(8,128)(2,1)S(1)}, bf16[256,768]{1,0:T(8,128)(2,1)S(1)}) fusion(bf16[256,6144]{1,0:T(8,128)(2,1)} %collective-permute-done, s32[]{:T(128)S(6)} %select_n.74, s32[]{:T(128)S(6)} %select_n.81, s32[]{:T(128)S(6)} %select_n.77, ...), kind=kLoop, calls=%fused_computation.91 | loop fusion | bytes 3145744 | tf_op jit(solution)/shard_map/dynamic_slice | solution.py:100
  34.2 1.5 %collective-permute-done.12 = f32[256,256]{0,1:T(8,128)S(1)} collective-permute-done((f32[256,256]{0,1:T(8,128)S(1)}, f32[256,256]{0,1:T(8,128)S(1)}, u32[]{:S(2)}, u32[]{:S(2)}) %collective-permute-start.12) | collective-permute-done | bytes 262176 | tf_op jit(solution)/shard_map/ppermute | solution.py:130
  40.9 2.8 %collective-permute-start.17 = (bf16[256,256]{1,0:T(8,128)(2,1)S(1)}, bf16[256,256]{1,0:T(8,128)(2,1)S(1)}, u32[]{:S(2)}, u32[]{:S(2)}) collective-permute-start(bf16[256,256]{1,0:T(8,128)(2,1)S(1)} %convolution_convert_fusion.1), channel_id=1, source_target_pairs={{0,2},{1,3},{2,6},{3,7},{6,4},{7,5},{4,0},{5,1},{8,10},{9,11},{10,... | collective-permute-start | bytes 393224 | tf_op jit(solution)/shard_map/ppermute | solution.py:146
  44.0 2.6 %collective-permute-done.14 = bf16[256,256]{1,0:T(8,128)(2,1)S(1)} collective-permute-done((bf16[256,256]{1,0:T(8,128)(2,1)S(1)}, bf16[256,256]{1,0:T(8,128)(2,1)S(1)}, u32[]{:S(2)}, u32[]{:S(2)}) %collective-permute-start.14) | collective-permute-done | bytes 131104 | tf_op jit(solution)/shard_map/ppermute | solution.py:146
  47.5 1.9 %collective-permute-done.17 = bf16[256,256]{1,0:T(8,128)(2,1)S(1)} collective-permute-done((bf16[256,256]{1,0:T(8,128)(2,1)S(1)}, bf16[256,256]{1,0:T(8,128)(2,1)S(1)}, u32[]{:S(2)}, u32[]{:S(2)}) %collective-permute-start.17) | collective-permute-done | bytes 131104 | tf_op jit(solution)/shard_map/ppermute | solution.py:146
  49.7 1.5 %collective-permute-start.18 = (bf16[256,256]{1,0:T(8,128)(2,1)S(1)}, bf16[256,256]{1,0:T(8,128)(2,1)S(1)}, u32[]{:S(2)}, u32[]{:S(2)}) collective-permute-start(bf16[256,256]{1,0:T(8,128)(2,1)S(1)} %add_convert_fusion.3), channel_id=1, source_target_pairs={{0,2},{1,3},{2,6},{3,7},{6,4},{7,5},{4,0},{5,1},{8,10},{9,11},{10,... | collective-permute-start | bytes 393224 | tf_op jit(solution)/shard_map/ppermute | solution.py:146
  52.5 1.5 %collective-permute-start.21 = (bf16[256,256]{1,0:T(8,128)(2,1)S(1)}, bf16[256,256]{1,0:T(8,128)(2,1)S(1)}, u32[]{:S(2)}, u32[]{:S(2)}) collective-permute-start(bf16[256,256]{1,0:T(8,128)(2,1)S(1)} %add_convert_fusion.1), channel_id=1, source_target_pairs={{0,2},{1,3},{2,6},{3,7},{6,4},{7,5},{4,0},{5,1},{8,10},{9,11},{10,... | collective-permute-start | bytes 393224 | tf_op jit(solution)/shard_map/ppermute | solution.py:146
  55.3 1.5 %collective-permute-start.16 = (bf16[256,256]{1,0:T(8,128)(2,1)S(1)}, bf16[256,256]{1,0:T(8,128)(2,1)S(1)}, u32[]{:S(2)}, u32[]{:S(2)}) collective-permute-start(bf16[256,256]{1,0:T(8,128)(2,1)S(1)} %add_convert_fusion.4), channel_id=1, source_target_pairs={{0,2},{1,3},{2,6},{3,7},{6,4},{7,5},{4,0},{5,1},{8,10},{9,11},{10,... | collective-permute-start | bytes 393224 | tf_op jit(solution)/shard_map/ppermute | solution.py:146
  58.2 1.5 %collective-permute-start.19 = (bf16[256,256]{1,0:T(8,128)(2,1)S(1)}, bf16[256,256]{1,0:T(8,128)(2,1)S(1)}, u32[]{:S(2)}, u32[]{:S(2)}) collective-permute-start(bf16[256,256]{1,0:T(8,128)(2,1)S(1)} %add_convert_fusion.2), channel_id=1, source_target_pairs={{0,2},{1,3},{2,6},{3,7},{6,4},{7,5},{4,0},{5,1},{8,10},{9,11},{10,... | collective-permute-start | bytes 393224 | tf_op jit(solution)/shard_map/ppermute | solution.py:146
  60.9 1.6 %collective-permute-start.22 = (bf16[256,256]{1,0:T(8,128)(2,1)S(1)}, bf16[256,256]{1,0:T(8,128)(2,1)S(1)}, u32[]{:S(2)}, u32[]{:S(2)}) collective-permute-start(bf16[256,256]{1,0:T(8,128)(2,1)S(1)} %add_convert_fusion), channel_id=1, source_target_pairs={{0,2},{1,3},{2,6},{3,7},{6,4},{7,5},{4,0},{5,1},{8,10},{9,11},{10,... | collective-permute-start | bytes 393224 | tf_op jit(solution)/shard_map/ppermute | solution.py:146
  63.7 2.5 %collective-permute-done.19 = bf16[256,256]{1,0:T(8,128)(2,1)S(1)} collective-permute-done((bf16[256,256]{1,0:T(8,128)(2,1)S(1)}, bf16[256,256]{1,0:T(8,128)(2,1)S(1)}, u32[]{:S(2)}, u32[]{:S(2)}) %collective-permute-start.19) | collective-permute-done | bytes 131104 | tf_op jit(solution)/shard_map/ppermute | solution.py:146
  66.6 2.0 %collective-permute-done.22 = bf16[256,256]{1,0:T(8,128)(2,1)S(1)} collective-permute-done((bf16[256,256]{1,0:T(8,128)(2,1)S(1)}, bf16[256,256]{1,0:T(8,128)(2,1)S(1)}, u32[]{:S(2)}, u32[]{:S(2)}) %collective-permute-start.22) | collective-permute-done | bytes 131104 | tf_op jit(solution)/shard_map/ppermute | solution.py:146
  68.8 1.8 %multiply_subtract_fusion = (f32[768,256]{1,0:T(8,128)}, f32[768,256]{1,0:T(8,128)}, f32[768,256]{1,0:T(8,128)}) fusion(f32[768,256]{1,0:T(8,128)S(1)} %copy-done.1, f32[256,256]{1,0:T(8,128)S(1)} %convert_add_fusion, f32[256,256]{1,0:T(8,128)S(1)} %convert_add_fusion.1, f32[256,256]{1,0:T(8,128)S(1)} %convert_add_fusion.2, f32[768,256]{1,0:T(8,128)S(1)} %copy-done.2, ...), kind=kLoop, calls=%fused_computation.36 | loop fusion | flops 3342336 | bytes 5505024 | tf_op jit(solution)/shard_map/sub | solution.py:154
  (80 shorter events, 22.1 us)
Async XLA Ops:
  0.6 35.6 %copy-start = (bf16[256,128]{1,0:T(8,128)(2,1)S(1)}, bf16[256,128]{1,0:T(8,128)(2,1)}, u32[]{:S(2)}) copy-start(bf16[256,128]{1,0:T(8,128)(2,1)} %param.14) | copy-start | bytes 196612
  0.6 28.5 %collective-permute-start = (bf16[256,6144]{1,0:T(8,128)(2,1)}, bf16[256,6144]{1,0:T(8,128)(2,1)}, u32[]{:S(2)}, u32[]{:S(2)}) collective-permute-start(bf16[256,6144]{1,0:T(8,128)(2,1)} %param.11), channel_id=1, source_target_pairs={{0,1},{1,0},{2,3},{3,2},{4,5},{5,4},{6,7},{7,6},{8,9},{9,8},{10,11... | collective-permute-start | bytes 9437192 | tf_op jit(solution)/shard_map/ppermute | solution.py:104
  2.4 8.0 %collective-permute-start.1 = (bf16[256,256]{1,0:T(8,128)(2,1)S(1)}, bf16[256,256]{1,0:T(8,128)(2,1)S(1)}, u32[]{:S(2)}, u32[]{:S(2)}) collective-permute-start(bf16[256,256]{1,0:T(8,128)(2,1)S(1)} %get-tuple-element.42), channel_id=1, source_target_pairs={{0,2},{1,3},{2,6},{3,7},{6,4},{7,5},{4,0},{5,1},{8,10},{9,11},{10,... | collective-permute-start | bytes 393224 | tf_op jit(solution)/shard_map/ppermute | solution.py:103
  5.0 12.3 %collective-permute-start.2 = (bf16[256,256]{1,0:T(8,128)(2,1)S(1)}, bf16[256,256]{1,0:T(8,128)(2,1)S(1)}, u32[]{:S(2)}, u32[]{:S(2)}) collective-permute-start(bf16[256,256]{1,0:T(8,128)(2,1)S(1)} %get-tuple-element.40), channel_id=1, source_target_pairs={{0,2},{1,3},{2,6},{3,7},{6,4},{7,5},{4,0},{5,1},{8,10},{9,11},{10,... | collective-permute-start | bytes 393224 | tf_op jit(solution)/shard_map/ppermute | solution.py:103
  7.6 8.2 %collective-permute-start.3 = (bf16[256,256]{1,0:T(8,128)(2,1)S(1)}, bf16[256,256]{1,0:T(8,128)(2,1)S(1)}, u32[]{:S(2)}, u32[]{:S(2)}) collective-permute-start(bf16[256,256]{1,0:T(8,128)(2,1)S(1)} %get-tuple-element.41), channel_id=1, source_target_pairs={{0,2},{1,3},{2,6},{3,7},{6,4},{7,5},{4,0},{5,1},{8,10},{9,11},{10,... | collective-permute-start | bytes 393224 | tf_op jit(solution)/shard_map/ppermute | solution.py:103
  11.4 8.8 %collective-permute-start.4 = (f32[1,6144]{1,0:T(1,128)S(1)}, f32[1,6144]{1,0:T(1,128)S(1)}, u32[]{:S(2)}, u32[]{:S(2)}) collective-permute-start(f32[1,6144]{1,0:T(1,128)S(1)} %convert_element_type.91), channel_id=1, source_target_pairs={{0,8},{8,0},{16,24},{24,16},{1,9},{9,1},{17,25},{25,17},{2,10},{10... | collective-permute-start | bytes 73736 | tf_op jit(solution)/shard_map/ppermute | solution.py:66
  13.2 7.0 %collective-permute-start.5 = (bf16[256,256]{1,0:T(8,128)(2,1)S(1)}, bf16[256,256]{1,0:T(8,128)(2,1)S(1)}, u32[]{:S(2)}, u32[]{:S(2)}) collective-permute-start(bf16[256,256]{1,0:T(8,128)(2,1)S(1)} %collective-permute-done.1), channel_id=1, source_target_pairs={{0,2},{1,3},{2,6},{3,7},{6,4},{7,5},{4,0},{5,1},{8,10},{9,11},{10,... | collective-permute-start | bytes 393224 | tf_op jit(solution)/shard_map/ppermute | solution.py:122
  15.9 7.4 %collective-permute-start.7 = (bf16[256,256]{1,0:T(8,128)(2,1)S(1)}, bf16[256,256]{1,0:T(8,128)(2,1)S(1)}, u32[]{:S(2)}, u32[]{:S(2)}) collective-permute-start(bf16[256,256]{1,0:T(8,128)(2,1)S(1)} %collective-permute-done.3), channel_id=1, source_target_pairs={{0,2},{1,3},{2,6},{3,7},{6,4},{7,5},{4,0},{5,1},{8,10},{9,11},{10,... | collective-permute-start | bytes 393224 | tf_op jit(solution)/shard_map/ppermute | solution.py:122
  17.3 8.9 %collective-permute-start.6 = (bf16[256,256]{1,0:T(8,128)(2,1)S(1)}, bf16[256,256]{1,0:T(8,128)(2,1)S(1)}, u32[]{:S(2)}, u32[]{:S(2)}) collective-permute-start(bf16[256,256]{1,0:T(8,128)(2,1)S(1)} %collective-permute-done.2), channel_id=1, source_target_pairs={{0,2},{1,3},{2,6},{3,7},{6,4},{7,5},{4,0},{5,1},{8,10},{9,11},{10,... | collective-permute-start | bytes 393224 | tf_op jit(solution)/shard_map/ppermute | solution.py:122
  20.2 7.3 %collective-permute-start.8 = (f32[1,6144]{1,0:T(1,128)S(1)}, f32[1,6144]{1,0:T(1,128)S(1)}, u32[]{:S(2)}, u32[]{:S(2)}) collective-permute-start(f32[1,6144]{1,0:T(1,128)S(1)} %convert_add_fusion.3), channel_id=1, source_target_pairs={{0,16},{8,24},{16,0},{24,8},{1,17},{9,25},{17,1},{25,9},{2,18},{10... | collective-permute-start | bytes 73736 | tf_op jit(solution)/shard_map/ppermute | solution.py:66
  21.8 7.3 %collective-permute-start.9 = (bf16[256,256]{1,0:T(8,128)(2,1)S(1)}, bf16[256,256]{1,0:T(8,128)(2,1)S(1)}, u32[]{:S(2)}, u32[]{:S(2)}) collective-permute-start(bf16[256,256]{1,0:T(8,128)(2,1)S(1)} %collective-permute-done.5), channel_id=1, source_target_pairs={{0,2},{1,3},{2,6},{3,7},{6,4},{7,5},{4,0},{5,1},{8,10},{9,11},{10,... | collective-permute-start | bytes 393224 | tf_op jit(solution)/shard_map/ppermute | solution.py:122
  23.3 10.2 %collective-permute-start.11 = (bf16[256,256]{1,0:T(8,128)(2,1)S(1)}, bf16[256,256]{1,0:T(8,128)(2,1)S(1)}, u32[]{:S(2)}, u32[]{:S(2)}) collective-permute-start(bf16[256,256]{1,0:T(8,128)(2,1)S(1)} %collective-permute-done.7), channel_id=1, source_target_pairs={{0,2},{1,3},{2,6},{3,7},{6,4},{7,5},{4,0},{5,1},{8,10},{9,11},{10,... | collective-permute-start | bytes 393224 | tf_op jit(solution)/shard_map/ppermute | solution.py:122
  26.2 7.5 %collective-permute-start.10 = (bf16[256,256]{1,0:T(8,128)(2,1)S(1)}, bf16[256,256]{1,0:T(8,128)(2,1)S(1)}, u32[]{:S(2)}, u32[]{:S(2)}) collective-permute-start(bf16[256,256]{1,0:T(8,128)(2,1)S(1)} %collective-permute-done.6), channel_id=1, source_target_pairs={{0,2},{1,3},{2,6},{3,7},{6,4},{7,5},{4,0},{5,1},{8,10},{9,11},{10,... | collective-permute-start | bytes 393224 | tf_op jit(solution)/shard_map/ppermute | solution.py:122
  34.1 1.6 %collective-permute-start.12 = (f32[256,256]{0,1:T(8,128)S(1)}, f32[256,256]{0,1:T(8,128)S(1)}, u32[]{:S(2)}, u32[]{:S(2)}) collective-permute-start(f32[256,256]{0,1:T(8,128)S(1)} %slice.111), channel_id=1, source_target_pairs={{0,1},{1,0},{2,3},{3,2},{4,5},{5,4},{6,7},{7,6},{8,9},{9,8},{10,11... | collective-permute-start | bytes 786440 | tf_op jit(solution)/shard_map/ppermute | solution.py:130
  37.4 1.7 %collective-permute-start.13 = (bf16[256,256]{0,1:T(8,128)(2,1)S(1)}, bf16[256,256]{0,1:T(8,128)(2,1)S(1)}, u32[]{:S(2)}, u32[]{:S(2)}) collective-permute-start(bf16[256,256]{0,1:T(8,128)(2,1)S(1)} %fusion.19), channel_id=1, source_target_pairs={{0,1},{1,0},{2,3},{3,2},{4,5},{5,4},{6,7},{7,6},{8,9},{9,8},{10,11... | collective-permute-start | bytes 393224 | tf_op jit(solution)/shard_map/ppermute | solution.py:132
  39.3 7.3 %collective-permute-start.14 = (bf16[256,256]{1,0:T(8,128)(2,1)S(1)}, bf16[256,256]{1,0:T(8,128)(2,1)S(1)}, u32[]{:S(2)}, u32[]{:S(2)}) collective-permute-start(bf16[256,256]{1,0:T(8,128)(2,1)S(1)} %convolution_convert_fusion.2), channel_id=1, source_target_pairs={{0,2},{1,3},{2,6},{3,7},{6,4},{7,5},{4,0},{5,1},{8,10},{9,11},{10,... | collective-permute-start | bytes 393224 | tf_op jit(solution)/shard_map/ppermute | solution.py:146
  40.9 8.5 %collective-permute-start.17 = (bf16[256,256]{1,0:T(8,128)(2,1)S(1)}, bf16[256,256]{1,0:T(8,128)(2,1)S(1)}, u32[]{:S(2)}, u32[]{:S(2)}) collective-permute-start(bf16[256,256]{1,0:T(8,128)(2,1)S(1)} %convolution_convert_fusion.1), channel_id=1, source_target_pairs={{0,2},{1,3},{2,6},{3,7},{6,4},{7,5},{4,0},{5,1},{8,10},{9,11},{10,... | collective-permute-start | bytes 393224 | tf_op jit(solution)/shard_map/ppermute | solution.py:146
  44.0 8.3 %collective-permute-start.20 = (bf16[256,256]{1,0:T(8,128)(2,1)S(1)}, bf16[256,256]{1,0:T(8,128)(2,1)S(1)}, u32[]{:S(2)}, u32[]{:S(2)}) collective-permute-start(bf16[256,256]{1,0:T(8,128)(2,1)S(1)} %convolution_convert_fusion), channel_id=1, source_target_pairs={{0,2},{1,3},{2,6},{3,7},{6,4},{7,5},{4,0},{5,1},{8,10},{9,11},{10,... | collective-permute-start | bytes 393224 | tf_op jit(solution)/shard_map/ppermute | solution.py:146
  46.9 8.1 %collective-permute-start.15 = (bf16[256,256]{1,0:T(8,128)(2,1)S(1)}, bf16[256,256]{1,0:T(8,128)(2,1)S(1)}, u32[]{:S(2)}, u32[]{:S(2)}) collective-permute-start(bf16[256,256]{1,0:T(8,128)(2,1)S(1)} %add_convert_fusion.5), channel_id=1, source_target_pairs={{0,2},{1,3},{2,6},{3,7},{6,4},{7,5},{4,0},{5,1},{8,10},{9,11},{10,... | collective-permute-start | bytes 393224 | tf_op jit(solution)/shard_map/ppermute | solution.py:146
  49.7 8.1 %collective-permute-start.18 = (bf16[256,256]{1,0:T(8,128)(2,1)S(1)}, bf16[256,256]{1,0:T(8,128)(2,1)S(1)}, u32[]{:S(2)}, u32[]{:S(2)}) collective-permute-start(bf16[256,256]{1,0:T(8,128)(2,1)S(1)} %add_convert_fusion.3), channel_id=1, source_target_pairs={{0,2},{1,3},{2,6},{3,7},{6,4},{7,5},{4,0},{5,1},{8,10},{9,11},{10,... | collective-permute-start | bytes 393224 | tf_op jit(solution)/shard_map/ppermute | solution.py:146
  52.5 8.1 %collective-permute-start.21 = (bf16[256,256]{1,0:T(8,128)(2,1)S(1)}, bf16[256,256]{1,0:T(8,128)(2,1)S(1)}, u32[]{:S(2)}, u32[]{:S(2)}) collective-permute-start(bf16[256,256]{1,0:T(8,128)(2,1)S(1)} %add_convert_fusion.1), channel_id=1, source_target_pairs={{0,2},{1,3},{2,6},{3,7},{6,4},{7,5},{4,0},{5,1},{8,10},{9,11},{10,... | collective-permute-start | bytes 393224 | tf_op jit(solution)/shard_map/ppermute | solution.py:146
  55.3 8.1 %collective-permute-start.16 = (bf16[256,256]{1,0:T(8,128)(2,1)S(1)}, bf16[256,256]{1,0:T(8,128)(2,1)S(1)}, u32[]{:S(2)}, u32[]{:S(2)}) collective-permute-start(bf16[256,256]{1,0:T(8,128)(2,1)S(1)} %add_convert_fusion.4), channel_id=1, source_target_pairs={{0,2},{1,3},{2,6},{3,7},{6,4},{7,5},{4,0},{5,1},{8,10},{9,11},{10,... | collective-permute-start | bytes 393224 | tf_op jit(solution)/shard_map/ppermute | solution.py:146
  58.2 8.1 %collective-permute-start.19 = (bf16[256,256]{1,0:T(8,128)(2,1)S(1)}, bf16[256,256]{1,0:T(8,128)(2,1)S(1)}, u32[]{:S(2)}, u32[]{:S(2)}) collective-permute-start(bf16[256,256]{1,0:T(8,128)(2,1)S(1)} %add_convert_fusion.2), channel_id=1, source_target_pairs={{0,2},{1,3},{2,6},{3,7},{6,4},{7,5},{4,0},{5,1},{8,10},{9,11},{10,... | collective-permute-start | bytes 393224 | tf_op jit(solution)/shard_map/ppermute | solution.py:146
  60.9 7.6 %collective-permute-start.22 = (bf16[256,256]{1,0:T(8,128)(2,1)S(1)}, bf16[256,256]{1,0:T(8,128)(2,1)S(1)}, u32[]{:S(2)}, u32[]{:S(2)}) collective-permute-start(bf16[256,256]{1,0:T(8,128)(2,1)S(1)} %add_convert_fusion), channel_id=1, source_target_pairs={{0,2},{1,3},{2,6},{3,7},{6,4},{7,5},{4,0},{5,1},{8,10},{9,11},{10,... | collective-permute-start | bytes 393224 | tf_op jit(solution)/shard_map/ppermute | solution.py:146
  (5 other events, 37.1 us)

commit v3 on v2

--- a/solution.py
+++ b/solution.py
@@ -6,7 +6,8 @@
 from jax.sharding import PartitionSpec as P
 
 ADAM_STEP = 100
-CHUNKS = 3
+GATHER_CHUNKS = 3
+SCATTER_CHUNKS = 3
 
 
 epsilon = 1e-06
@@ -30,7 +31,7 @@
     k_rate = lax.rsqrt(jnp.mean(keys_part * keys_part, axis=1, keepdims=True) + epsilon)
     q_unit = queries * q_rate
     k_unit = keys_part * k_rate
-    scores = jnp.dot(q_unit, k_unit.T, precision=lax.Precision.HIGHEST) * score_scale
+    scores = jnp.dot(q_unit, k_unit.T, precision=lax.Precision.HIGH) * score_scale
     position = jnp.arange(doc_ids.shape[0])
     allowed = (doc_ids[:, None] == doc_ids[None, :]) & (position[None, :] <= position[:, None])
     raised = jnp.where(allowed, jnp.exp(scores), jnp.float32(0.0))
@@ -41,8 +42,8 @@
         * (grad_attention - jnp.sum(attention * grad_attention, axis=1, keepdims=True))
         * score_scale
     )
-    grad_qunit = jnp.dot(grad_scores, k_unit, precision=lax.Precision.HIGHEST)
-    grad_kunit = jnp.dot(grad_scores.T, q_unit, precision=lax.Precision.HIGHEST)
+    grad_qunit = jnp.dot(grad_scores, k_unit, precision=lax.Precision.HIGH)
+    grad_kunit = jnp.dot(grad_scores.T, q_unit, precision=lax.Precision.HIGH)
     grad_query = q_rate * (
         grad_qunit - q_unit * jnp.mean(grad_qunit * q_unit, axis=1, keepdims=True)
     )
@@ -52,25 +53,40 @@
     return (jnp.concatenate([grad_query, grad_keys], axis=1) * input_scale).astype(jnp.bfloat16)
 
 
-def outer_start(frag_local, frag_global, frag_moment, frag_index):
+def drift_of(outer):
+    frag_local, frag_global, frag_moment, frag_index = outer
+    chosen = frag_index[0]
+    current = lax.dynamic_index_in_dim(frag_global, chosen, 0, keepdims=False)
+    local_copy = lax.dynamic_index_in_dim(frag_local[0], chosen, 0, keepdims=False)
+    drift = (current - local_copy.astype(jnp.float32)).astype(jnp.bfloat16)
+    return lax.optimization_barrier(drift).astype(jnp.float32)
+
+
+def exchange(total, step):
+    replicas = lax.axis_size("replica")
+    return total + lax.ppermute(total, "replica", [(i, i ^ step) for i in range(replicas)])
+
+
+def outer_finish(outer, total):
+    frag_local, frag_global, frag_moment, frag_index = outer
     chosen = frag_index[0]
     current = lax.dynamic_index_in_dim(frag_global, chosen, 0, keepdims=False)
     moment_now = lax.dynamic_index_in_dim(frag_moment, chosen, 0, keepdims=False)
-    local_copy = lax.dynamic_index_in_dim(frag_local[0], chosen, 0, keepdims=False)
-    drift = (current - local_copy.astype(jnp.float32)).astype(jnp.bfloat16)
-    return current, moment_now, lax.optimization_barrier(drift).astype(jnp.float32)
-
-
-def exchange(total, step):
-    replicas = lax.axis_size("replica")
-    return total + lax.ppermute(total, "replica", [(i, i ^ step) for i in range(replicas)])
-
-
-def outer_finish(current, moment_now, total):
     drift_mean = total / lax.axis_size("replica")
     new_moment = outer_momentum * moment_now + drift_mean
     new_global = current - outer_rate * (drift_mean + outer_momentum * new_moment)
     return (new_global, new_moment)
+
+
+def adam(gradient, weights, moment1, moment2):
+    first_new = beta_one * moment1 + (1.0 - beta_one) * gradient
+    second_new = beta_two * moment2 + (1.0 - beta_two) * gradient * gradient
+    first_hat = first_new / (1.0 - beta_one**ADAM_STEP)
+    second_hat = second_new / (1.0 - beta_two**ADAM_STEP)
+    weight_new = weights - learn_rate * (
+        first_hat / (jnp.sqrt(second_hat) + 1e-08) + decay_rate * weights
+    )
+    return (weight_new, first_new, second_new)
 
 
 def spot_of(chip, chips):
@@ -88,7 +104,6 @@
     chips = devices // 2
     here = lax.axis_index("shard")
     rows = weights.shape[0]
-    part = rows // CHUNKS
     line = [0] + [i for i in range(chips) if i % 2 == 1] + [i for i in range(chips - 1, 1, -1) if i % 2 == 0]
     ring = [(2 * line[i] + c, 2 * line[(i + 1) % chips] + c) for i in range(chips) for c in range(2)]
     core = lax.rem(here, 2)
@@ -99,18 +114,22 @@
         chip = chip_at(lax.rem(spot + (chips - k), chips), chips)
         return lax.dynamic_slice_in_dim(tokens, (2 * chip + core) * rows, rows, axis=1)
 
-    blocks = [weights[j * part : (j + 1) * part].astype(jnp.bfloat16) for j in range(CHUNKS)]
+    part = rows // GATHER_CHUNKS
+    lowered = weights.astype(jnp.bfloat16)
+    blocks = [lowered[j * part : (j + 1) * part] for j in range(GATHER_CHUNKS)]
     flying = [lax.ppermute(block, "shard", ring) for block in blocks]
     partner = lax.ppermute(inputs, "shard", swap)
     outer, flying[0] = lax.optimization_barrier((outer, flying[0]))
-    current, moment_now, drift = outer_start(*outer)
-    drift = exchange(drift, 1)
+    drift = exchange(drift_of(outer), 1)
     both = [
         jnp.concatenate([ordered(inputs, k), ordered(partner, k)], axis=0) for k in range(chips)
     ]
     total = jnp.float32(0.0)
     for k in range(chips):
-        for j in range(CHUNKS):
+        if k in (0,):
+            block = lowered if k == 0 else jnp.concatenate(blocks, axis=0)
+            total = total + jnp.dot(both[k], block, preferred_element_type=jnp.float32)
+        for j in range(GATHER_CHUNKS if k not in (0,) else 0):
             total = total + jnp.dot(
                 both[k][:, j * part : (j + 1) * part],
                 blocks[j],
@@ -125,11 +144,12 @@
                 drift = exchange(drift, 2)
             if k == 1:
                 drift, flying[0] = lax.optimization_barrier((drift, flying[0]))
-                outer_done = outer_finish(current, moment_now, drift)
     tokens = inputs.shape[0]
     projected = total[:tokens] + lax.ppermute(total[tokens:], "shard", swap)
     grad_own = head_grads(inputs, doc_ids[0], values, cotangent, projected)
     grad_both = jnp.concatenate([grad_own, lax.ppermute(grad_own, "shard", swap)], axis=0)
+
+    part = rows // SCATTER_CHUNKS
 
     def term(k, j):
         return lax.dot_general(
@@ -139,22 +159,15 @@
             preferred_element_type=jnp.float32,
         )
 
-    sums = [term(1, j).astype(jnp.bfloat16) for j in range(CHUNKS)]
-    for k in range(chips - 1):
-        later = 0 if k == chips - 2 else k + 2
-        for j in range(CHUNKS):
-            sums[j] = lax.ppermute(sums[j], "shard", ring).astype(jnp.float32) + term(later, j)
-            if later:
-                sums[j] = sums[j].astype(jnp.bfloat16)
-    gradient = jnp.concatenate(sums, axis=0)
-    first_new = beta_one * moment1 + (1.0 - beta_one) * gradient
-    second_new = beta_two * moment2 + (1.0 - beta_two) * gradient * gradient
-    first_hat = first_new / (1.0 - beta_one**ADAM_STEP)
-    second_hat = second_new / (1.0 - beta_two**ADAM_STEP)
-    weight_new = weights - learn_rate * (
-        first_hat / (jnp.sqrt(second_hat) + 1e-08) + decay_rate * weights
-    )
-    return (weight_new, first_new, second_new) + outer_done
+    sums = [term(1, j).astype(jnp.bfloat16) for j in range(SCATTER_CHUNKS)]
+    for k in range(2, chips):
+        for j in range(SCATTER_CHUNKS):
+            came = lax.ppermute(sums[j], "shard", ring)
+            sums[j] = (came.astype(jnp.float32) + term(k, j)).astype(jnp.bfloat16)
+    for j in range(SCATTER_CHUNKS):
+        sums[j] = lax.ppermute(sums[j], "shard", ring).astype(jnp.float32) + term(0, j)
+    updated = adam(jnp.concatenate(sums, axis=0), weights, moment1, moment2)
+    return updated + outer_finish(outer, drift)
 
 
 def on_device(

time: 70.9 us -> 70.1 us (0.989)
  matrix products: 8.16 us -> 7.37 us
    convert_element_type x2 -> x3, other arithmetic: 0.96 us -> 2.13 us  [the longest x1 1.17 us: inner_step(): lowered = weights.astype(jnp.bfloat16)]
    another operation x1 -> x0, other arithmetic: 1.17 us -> none
    dot_general x12 -> x9, matrix products: 3.42 us -> 2.51 us  [inner_step(): jnp.dot(both[k][:, j * part:(j + 1) * part], blocks[j], preferred_element...]
  transfers between devices with their start and end apart: 23 -> 23, of which waited for: 13 -> 13; matrix products, arithmetic and copies ran while one was open for 18% -> 17% of each run, Pallas kernels for 0% -> 0%
where the time goes in v3:
time: 70.1 us; the launch traced here: 69.8 us
  starting transfers between devices  31.6 us (45%)
  waiting for transfers between devices  20.6 us (29%)
  matrix products  7.37 us (11%)
  other arithmetic  5.59 us (8%)
  local copies, waits for them, and re-layouts  3.01 us (4%)
  between operations  1.65 us (2%)
    ppermute x9, starting transfers between devices, inner_step(): flying = [lax.ppermute(block, 'shard', ring) for block in blocks]  14.9 us
    ppermute x6, waiting for transfers between devices, inner_step(): came = lax.ppermute(sums[j], 'shard', ring)  8.37 us
    ppermute x6, starting transfers between devices, inner_step(): came = lax.ppermute(sums[j], 'shard', ring)  7.86 us
    ppermute x3, waiting for transfers between devices, inner_step(): lax.ppermute(sums[j], 'shard', ring).astype(jnp.float32) + term(0, j)  5.44 us
    ppermute x9, waiting for transfers between devices, inner_step(): flying = [lax.ppermute(block, 'shard', ring) for block in blocks]  5.21 us
    ppermute x3, starting transfers between devices, inner_step(): lax.ppermute(sums[j], 'shard', ring).astype(jnp.float32) + term(0, j)  4.66 us
    ppermute x2, starting transfers between devices, exchange(): lax.ppermute(total, 'replica', [(i, i ^ step) for i in range(replicas)])  3.39 us
    dot_general x12, matrix products, term(): lax.dot_general(both[k][:, j * part:(j + 1) * part], grad_both, (((0,), (...  3.3 us
  transfers between devices with their start and end apart: 23, of which 13 were waited for; matrix products, arithmetic and copies ran while one was open for 17% of the time, Pallas kernels for 0%

profile of v3, /device:TPU:0, one launch (start us, length us, event | category | flops | bytes accessed | tf_op | source)
XLA Modules:
  0.0 69.8 jit_solution(16235039856517395998)
XLA Ops:
  2.4 2.6 %collective-permute-start.1 = (bf16[256,256]{1,0:T(8,128)(2,1)S(1)}, bf16[256,256]{1,0:T(8,128)(2,1)S(1)}, u32[]{:S(2)}, u32[]{:S(2)}) collective-permute-start(bf16[256,256]{1,0:T(8,128)(2,1)S(1)} %get-tuple-element.42), channel_id=1, source_target_pairs={{0,2},{1,3},{2,6},{3,7},{6,4},{7,5},{4,0},{5,1},{8,10},{9,11},{10,... | collective-permute-start | bytes 393224 | tf_op jit(solution)/shard_map/ppermute | solution.py:120
  5.0 2.6 %collective-permute-start.2 = (bf16[256,256]{1,0:T(8,128)(2,1)S(1)}, bf16[256,256]{1,0:T(8,128)(2,1)S(1)}, u32[]{:S(2)}, u32[]{:S(2)}) collective-permute-start(bf16[256,256]{1,0:T(8,128)(2,1)S(1)} %get-tuple-element.40), channel_id=1, source_target_pairs={{0,2},{1,3},{2,6},{3,7},{6,4},{7,5},{4,0},{5,1},{8,10},{9,11},{10,... | collective-permute-start | bytes 393224 | tf_op jit(solution)/shard_map/ppermute | solution.py:120
  8.7 1.7 %collective-permute-done.1 = bf16[256,256]{1,0:T(8,128)(2,1)S(1)} collective-permute-done((bf16[256,256]{1,0:T(8,128)(2,1)S(1)}, bf16[256,256]{1,0:T(8,128)(2,1)S(1)}, u32[]{:S(2)}, u32[]{:S(2)}) %collective-permute-start.1) | collective-permute-done | bytes 131104 | tf_op jit(solution)/shard_map/ppermute | solution.py:120
  11.4 1.8 %collective-permute-start.4 = (f32[1,6144]{1,0:T(1,128)S(1)}, f32[1,6144]{1,0:T(1,128)S(1)}, u32[]{:S(2)}, u32[]{:S(2)}) collective-permute-start(f32[1,6144]{1,0:T(1,128)S(1)} %convert_element_type.92), channel_id=1, source_target_pairs={{0,8},{8,0},{16,24},{24,16},{1,9},{9,1},{17,25},{25,17},{2,10},{10... | collective-permute-start | bytes 73736 | tf_op jit(solution)/shard_map/ppermute | solution.py:67
  13.9 1.9 %collective-permute-done.3 = bf16[256,256]{1,0:T(8,128)(2,1)S(1)} collective-permute-done((bf16[256,256]{1,0:T(8,128)(2,1)S(1)}, bf16[256,256]{1,0:T(8,128)(2,1)S(1)}, u32[]{:S(2)}, u32[]{:S(2)}) %collective-permute-start.3) | collective-permute-done | bytes 131104 | tf_op jit(solution)/shard_map/ppermute | solution.py:120
  15.9 1.5 %collective-permute-start.7 = (bf16[256,256]{1,0:T(8,128)(2,1)S(1)}, bf16[256,256]{1,0:T(8,128)(2,1)S(1)}, u32[]{:S(2)}, u32[]{:S(2)}) collective-permute-start(bf16[256,256]{1,0:T(8,128)(2,1)S(1)} %collective-permute-done.3), channel_id=1, source_target_pairs={{0,2},{1,3},{2,6},{3,7},{6,4},{7,5},{4,0},{5,1},{8,10},{9,11},{10,... | collective-permute-start | bytes 393224 | tf_op jit(solution)/shard_map/ppermute | solution.py:141
  17.3 2.8 %collective-permute-start.6 = (bf16[256,256]{1,0:T(8,128)(2,1)S(1)}, bf16[256,256]{1,0:T(8,128)(2,1)S(1)}, u32[]{:S(2)}, u32[]{:S(2)}) collective-permute-start(bf16[256,256]{1,0:T(8,128)(2,1)S(1)} %collective-permute-done.2), channel_id=1, source_target_pairs={{0,2},{1,3},{2,6},{3,7},{6,4},{7,5},{4,0},{5,1},{8,10},{9,11},{10,... | collective-permute-start | bytes 393224 | tf_op jit(solution)/shard_map/ppermute | solution.py:141
  20.2 1.6 %collective-permute-start.8 = (f32[1,6144]{1,0:T(1,128)S(1)}, f32[1,6144]{1,0:T(1,128)S(1)}, u32[]{:S(2)}, u32[]{:S(2)}) collective-permute-start(f32[1,6144]{1,0:T(1,128)S(1)} %convert_add_fusion.3), channel_id=1, source_target_pairs={{0,16},{8,24},{16,0},{24,8},{1,17},{9,25},{17,1},{25,9},{2,18},{10... | collective-permute-start | bytes 73736 | tf_op jit(solution)/shard_map/ppermute | solution.py:67
  21.8 1.5 %constant_dynamic-slice_fusion.5 = (bf16[256,768]{1,0:T(8,128)(2,1)S(1)}, bf16[256,768]{1,0:T(8,128)(2,1)S(1)}, bf16[256,768]{1,0:T(8,128)(2,1)S(1)}, bf16[256,768]{1,0:T(8,128)(2,1)S(1)}) fusion(bf16[256,6144]{1,0:T(8,128)(2,1)} %param.11, s32[]{:T(128)S(6)} %select_n.75, s32[]{:T(128)S(6)} %select_n.72, s32[]{:T(128)S(6)} %select_n.82, s32[]{:T(128)S(6)} %select_n.78), kind=kLoop, calls=%fused_computation.96 | loop fusion | bytes 3145744 | tf_op jit(solution)/shard_map/dynamic_slice | solution.py:115
  23.3 3.0 %collective-permute-start.11 = (bf16[256,256]{1,0:T(8,128)(2,1)S(1)}, bf16[256,256]{1,0:T(8,128)(2,1)S(1)}, u32[]{:S(2)}, u32[]{:S(2)}) collective-permute-start(bf16[256,256]{1,0:T(8,128)(2,1)S(1)} %collective-permute-done.7), channel_id=1, source_target_pairs={{0,2},{1,3},{2,6},{3,7},{6,4},{7,5},{4,0},{5,1},{8,10},{9,11},{10,... | collective-permute-start | bytes 393224 | tf_op jit(solution)/shard_map/ppermute | solution.py:141
  27.5 1.6 %collective-permute-done.9 = bf16[256,256]{1,0:T(8,128)(2,1)S(1)} collective-permute-done((bf16[256,256]{1,0:T(8,128)(2,1)S(1)}, bf16[256,256]{1,0:T(8,128)(2,1)S(1)}, u32[]{:S(2)}, u32[]{:S(2)}) %collective-permute-start.9) | collective-permute-done | bytes 131104 | tf_op jit(solution)/shard_map/ppermute | solution.py:141
  29.1 1.5 %constant_dynamic-slice_fusion.4 = (bf16[256,768]{1,0:T(8,128)(2,1)S(1)}, bf16[256,768]{1,0:T(8,128)(2,1)S(1)}, bf16[256,768]{1,0:T(8,128)(2,1)S(1)}, bf16[256,768]{1,0:T(8,128)(2,1)S(1)}) fusion(bf16[256,6144]{1,0:T(8,128)(2,1)} %collective-permute-done, s32[]{:T(128)S(6)} %select_n.75, s32[]{:T(128)S(6)} %select_n.82, s32[]{:T(128)S(6)} %select_n.78, ...), kind=kLoop, calls=%fused_computation.95 | loop fusion | bytes 3145744 | tf_op jit(solution)/shard_map/dynamic_slice | solution.py:115
  33.7 1.5 %collective-permute-done.12 = f32[256,256]{0,1:T(8,128)S(1)} collective-permute-done((f32[256,256]{0,1:T(8,128)S(1)}, f32[256,256]{0,1:T(8,128)S(1)}, u32[]{:S(2)}, u32[]{:S(2)}) %collective-permute-start.12) | collective-permute-done | bytes 262176 | tf_op jit(solution)/shard_map/ppermute | solution.py:148
  40.1 2.8 %collective-permute-start.17 = (bf16[256,256]{1,0:T(8,128)(2,1)S(1)}, bf16[256,256]{1,0:T(8,128)(2,1)S(1)}, u32[]{:S(2)}, u32[]{:S(2)}) collective-permute-start(bf16[256,256]{1,0:T(8,128)(2,1)S(1)} %convolution_convert_fusion.1), channel_id=1, source_target_pairs={{0,2},{1,3},{2,6},{3,7},{6,4},{7,5},{4,0},{5,1},{8,10},{9,11},{10,... | collective-permute-start | bytes 393224 | tf_op jit(solution)/shard_map/ppermute | solution.py:165
  43.2 2.6 %collective-permute-done.14 = bf16[256,256]{1,0:T(8,128)(2,1)S(1)} collective-permute-done((bf16[256,256]{1,0:T(8,128)(2,1)S(1)}, bf16[256,256]{1,0:T(8,128)(2,1)S(1)}, u32[]{:S(2)}, u32[]{:S(2)}) %collective-permute-start.14) | collective-permute-done | bytes 131104 | tf_op jit(solution)/shard_map/ppermute | solution.py:165
  46.7 1.9 %collective-permute-done.17 = bf16[256,256]{1,0:T(8,128)(2,1)S(1)} collective-permute-done((bf16[256,256]{1,0:T(8,128)(2,1)S(1)}, bf16[256,256]{1,0:T(8,128)(2,1)S(1)}, u32[]{:S(2)}, u32[]{:S(2)}) %collective-permute-start.17) | collective-permute-done | bytes 131104 | tf_op jit(solution)/shard_map/ppermute | solution.py:165
  48.9 1.5 %collective-permute-start.18 = (bf16[256,256]{1,0:T(8,128)(2,1)S(1)}, bf16[256,256]{1,0:T(8,128)(2,1)S(1)}, u32[]{:S(2)}, u32[]{:S(2)}) collective-permute-start(bf16[256,256]{1,0:T(8,128)(2,1)S(1)} %add_convert_fusion.3), channel_id=1, source_target_pairs={{0,2},{1,3},{2,6},{3,7},{6,4},{7,5},{4,0},{5,1},{8,10},{9,11},{10,... | collective-permute-start | bytes 393224 | tf_op jit(solution)/shard_map/ppermute | solution.py:165
  51.7 1.5 %collective-permute-start.21 = (bf16[256,256]{1,0:T(8,128)(2,1)S(1)}, bf16[256,256]{1,0:T(8,128)(2,1)S(1)}, u32[]{:S(2)}, u32[]{:S(2)}) collective-permute-start(bf16[256,256]{1,0:T(8,128)(2,1)S(1)} %add_convert_fusion.1), channel_id=1, source_target_pairs={{0,2},{1,3},{2,6},{3,7},{6,4},{7,5},{4,0},{5,1},{8,10},{9,11},{10,... | collective-permute-start | bytes 393224 | tf_op jit(solution)/shard_map/ppermute | solution.py:165
  54.5 1.5 %collective-permute-start.16 = (bf16[256,256]{1,0:T(8,128)(2,1)S(1)}, bf16[256,256]{1,0:T(8,128)(2,1)S(1)}, u32[]{:S(2)}, u32[]{:S(2)}) collective-permute-start(bf16[256,256]{1,0:T(8,128)(2,1)S(1)} %add_convert_fusion.4), channel_id=1, source_target_pairs={{0,2},{1,3},{2,6},{3,7},{6,4},{7,5},{4,0},{5,1},{8,10},{9,11},{10,... | collective-permute-start | bytes 393224 | tf_op jit(solution)/shard_map/ppermute | solution.py:168
  57.4 1.5 %collective-permute-start.19 = (bf16[256,256]{1,0:T(8,128)(2,1)S(1)}, bf16[256,256]{1,0:T(8,128)(2,1)S(1)}, u32[]{:S(2)}, u32[]{:S(2)}) collective-permute-start(bf16[256,256]{1,0:T(8,128)(2,1)S(1)} %add_convert_fusion.2), channel_id=1, source_target_pairs={{0,2},{1,3},{2,6},{3,7},{6,4},{7,5},{4,0},{5,1},{8,10},{9,11},{10,... | collective-permute-start | bytes 393224 | tf_op jit(solution)/shard_map/ppermute | solution.py:168
  60.1 1.6 %collective-permute-start.22 = (bf16[256,256]{1,0:T(8,128)(2,1)S(1)}, bf16[256,256]{1,0:T(8,128)(2,1)S(1)}, u32[]{:S(2)}, u32[]{:S(2)}) collective-permute-start(bf16[256,256]{1,0:T(8,128)(2,1)S(1)} %add_convert_fusion), channel_id=1, source_target_pairs={{0,2},{1,3},{2,6},{3,7},{6,4},{7,5},{4,0},{5,1},{8,10},{9,11},{10,... | collective-permute-start | bytes 393224 | tf_op jit(solution)/shard_map/ppermute | solution.py:168
  62.9 2.5 %collective-permute-done.19 = bf16[256,256]{1,0:T(8,128)(2,1)S(1)} collective-permute-done((bf16[256,256]{1,0:T(8,128)(2,1)S(1)}, bf16[256,256]{1,0:T(8,128)(2,1)S(1)}, u32[]{:S(2)}, u32[]{:S(2)}) %collective-permute-start.19) | collective-permute-done | bytes 131104 | tf_op jit(solution)/shard_map/ppermute | solution.py:168
  65.8 2.0 %collective-permute-done.22 = bf16[256,256]{1,0:T(8,128)(2,1)S(1)} collective-permute-done((bf16[256,256]{1,0:T(8,128)(2,1)S(1)}, bf16[256,256]{1,0:T(8,128)(2,1)S(1)}, u32[]{:S(2)}, u32[]{:S(2)}) %collective-permute-start.22) | collective-permute-done | bytes 131104 | tf_op jit(solution)/shard_map/ppermute | solution.py:168
  68.0 1.8 %multiply_subtract_fusion = (f32[768,256]{1,0:T(8,128)}, f32[768,256]{1,0:T(8,128)}, f32[768,256]{1,0:T(8,128)}) fusion(f32[768,256]{1,0:T(8,128)S(1)} %copy-done.1, f32[256,256]{1,0:T(8,128)S(1)} %convert_add_fusion, f32[256,256]{1,0:T(8,128)S(1)} %convert_add_fusion.1, f32[256,256]{1,0:T(8,128)S(1)} %convert_add_fusion.2, f32[768,256]{1,0:T(8,128)S(1)} %copy-done.2, ...), kind=kLoop, calls=%fused_computation.37 | loop fusion | flops 3342336 | bytes 5505024 | tf_op jit(solution)/shard_map/sub | solution.py:86
  (78 shorter events, 21.3 us)
Async XLA Ops:
  0.6 35.0 %copy-start = (bf16[256,128]{1,0:T(8,128)(2,1)S(1)}, bf16[256,128]{1,0:T(8,128)(2,1)}, u32[]{:S(2)}) copy-start(bf16[256,128]{1,0:T(8,128)(2,1)} %param.14) | copy-start | bytes 196612
  0.6 28.5 %collective-permute-start = (bf16[256,6144]{1,0:T(8,128)(2,1)}, bf16[256,6144]{1,0:T(8,128)(2,1)}, u32[]{:S(2)}, u32[]{:S(2)}) collective-permute-start(bf16[256,6144]{1,0:T(8,128)(2,1)} %param.11), channel_id=1, source_target_pairs={{0,1},{1,0},{2,3},{3,2},{4,5},{5,4},{6,7},{7,6},{8,9},{9,8},{10,11... | collective-permute-start | bytes 9437192 | tf_op jit(solution)/shard_map/ppermute | solution.py:121
  2.4 8.0 %collective-permute-start.1 = (bf16[256,256]{1,0:T(8,128)(2,1)S(1)}, bf16[256,256]{1,0:T(8,128)(2,1)S(1)}, u32[]{:S(2)}, u32[]{:S(2)}) collective-permute-start(bf16[256,256]{1,0:T(8,128)(2,1)S(1)} %get-tuple-element.42), channel_id=1, source_target_pairs={{0,2},{1,3},{2,6},{3,7},{6,4},{7,5},{4,0},{5,1},{8,10},{9,11},{10,... | collective-permute-start | bytes 393224 | tf_op jit(solution)/shard_map/ppermute | solution.py:120
  5.0 12.3 %collective-permute-start.2 = (bf16[256,256]{1,0:T(8,128)(2,1)S(1)}, bf16[256,256]{1,0:T(8,128)(2,1)S(1)}, u32[]{:S(2)}, u32[]{:S(2)}) collective-permute-start(bf16[256,256]{1,0:T(8,128)(2,1)S(1)} %get-tuple-element.40), channel_id=1, source_target_pairs={{0,2},{1,3},{2,6},{3,7},{6,4},{7,5},{4,0},{5,1},{8,10},{9,11},{10,... | collective-permute-start | bytes 393224 | tf_op jit(solution)/shard_map/ppermute | solution.py:120
  7.6 8.2 %collective-permute-start.3 = (bf16[256,256]{1,0:T(8,128)(2,1)S(1)}, bf16[256,256]{1,0:T(8,128)(2,1)S(1)}, u32[]{:S(2)}, u32[]{:S(2)}) collective-permute-start(bf16[256,256]{1,0:T(8,128)(2,1)S(1)} %get-tuple-element.41), channel_id=1, source_target_pairs={{0,2},{1,3},{2,6},{3,7},{6,4},{7,5},{4,0},{5,1},{8,10},{9,11},{10,... | collective-permute-start | bytes 393224 | tf_op jit(solution)/shard_map/ppermute | solution.py:120
  11.4 8.8 %collective-permute-start.4 = (f32[1,6144]{1,0:T(1,128)S(1)}, f32[1,6144]{1,0:T(1,128)S(1)}, u32[]{:S(2)}, u32[]{:S(2)}) collective-permute-start(f32[1,6144]{1,0:T(1,128)S(1)} %convert_element_type.92), channel_id=1, source_target_pairs={{0,8},{8,0},{16,24},{24,16},{1,9},{9,1},{17,25},{25,17},{2,10},{10... | collective-permute-start | bytes 73736 | tf_op jit(solution)/shard_map/ppermute | solution.py:67
  13.2 7.0 %collective-permute-start.5 = (bf16[256,256]{1,0:T(8,128)(2,1)S(1)}, bf16[256,256]{1,0:T(8,128)(2,1)S(1)}, u32[]{:S(2)}, u32[]{:S(2)}) collective-permute-start(bf16[256,256]{1,0:T(8,128)(2,1)S(1)} %collective-permute-done.1), channel_id=1, source_target_pairs={{0,2},{1,3},{2,6},{3,7},{6,4},{7,5},{4,0},{5,1},{8,10},{9,11},{10,... | collective-permute-start | bytes 393224 | tf_op jit(solution)/shard_map/ppermute | solution.py:141
  15.9 7.4 %collective-permute-start.7 = (bf16[256,256]{1,0:T(8,128)(2,1)S(1)}, bf16[256,256]{1,0:T(8,128)(2,1)S(1)}, u32[]{:S(2)}, u32[]{:S(2)}) collective-permute-start(bf16[256,256]{1,0:T(8,128)(2,1)S(1)} %collective-permute-done.3), channel_id=1, source_target_pairs={{0,2},{1,3},{2,6},{3,7},{6,4},{7,5},{4,0},{5,1},{8,10},{9,11},{10,... | collective-permute-start | bytes 393224 | tf_op jit(solution)/shard_map/ppermute | solution.py:141
  17.3 8.9 %collective-permute-start.6 = (bf16[256,256]{1,0:T(8,128)(2,1)S(1)}, bf16[256,256]{1,0:T(8,128)(2,1)S(1)}, u32[]{:S(2)}, u32[]{:S(2)}) collective-permute-start(bf16[256,256]{1,0:T(8,128)(2,1)S(1)} %collective-permute-done.2), channel_id=1, source_target_pairs={{0,2},{1,3},{2,6},{3,7},{6,4},{7,5},{4,0},{5,1},{8,10},{9,11},{10,... | collective-permute-start | bytes 393224 | tf_op jit(solution)/shard_map/ppermute | solution.py:141
  20.2 7.3 %collective-permute-start.8 = (f32[1,6144]{1,0:T(1,128)S(1)}, f32[1,6144]{1,0:T(1,128)S(1)}, u32[]{:S(2)}, u32[]{:S(2)}) collective-permute-start(f32[1,6144]{1,0:T(1,128)S(1)} %convert_add_fusion.3), channel_id=1, source_target_pairs={{0,16},{8,24},{16,0},{24,8},{1,17},{9,25},{17,1},{25,9},{2,18},{10... | collective-permute-start | bytes 73736 | tf_op jit(solution)/shard_map/ppermute | solution.py:67
  21.8 7.3 %collective-permute-start.9 = (bf16[256,256]{1,0:T(8,128)(2,1)S(1)}, bf16[256,256]{1,0:T(8,128)(2,1)S(1)}, u32[]{:S(2)}, u32[]{:S(2)}) collective-permute-start(bf16[256,256]{1,0:T(8,128)(2,1)S(1)} %collective-permute-done.5), channel_id=1, source_target_pairs={{0,2},{1,3},{2,6},{3,7},{6,4},{7,5},{4,0},{5,1},{8,10},{9,11},{10,... | collective-permute-start | bytes 393224 | tf_op jit(solution)/shard_map/ppermute | solution.py:141
  23.3 9.8 %collective-permute-start.11 = (bf16[256,256]{1,0:T(8,128)(2,1)S(1)}, bf16[256,256]{1,0:T(8,128)(2,1)S(1)}, u32[]{:S(2)}, u32[]{:S(2)}) collective-permute-start(bf16[256,256]{1,0:T(8,128)(2,1)S(1)} %collective-permute-done.7), channel_id=1, source_target_pairs={{0,2},{1,3},{2,6},{3,7},{6,4},{7,5},{4,0},{5,1},{8,10},{9,11},{10,... | collective-permute-start | bytes 393224 | tf_op jit(solution)/shard_map/ppermute | solution.py:141
  26.2 7.1 %collective-permute-start.10 = (bf16[256,256]{1,0:T(8,128)(2,1)S(1)}, bf16[256,256]{1,0:T(8,128)(2,1)S(1)}, u32[]{:S(2)}, u32[]{:S(2)}) collective-permute-start(bf16[256,256]{1,0:T(8,128)(2,1)S(1)} %collective-permute-done.6), channel_id=1, source_target_pairs={{0,2},{1,3},{2,6},{3,7},{6,4},{7,5},{4,0},{5,1},{8,10},{9,11},{10,... | collective-permute-start | bytes 393224 | tf_op jit(solution)/shard_map/ppermute | solution.py:141
  33.6 1.6 %collective-permute-start.12 = (f32[256,256]{0,1:T(8,128)S(1)}, f32[256,256]{0,1:T(8,128)S(1)}, u32[]{:S(2)}, u32[]{:S(2)}) collective-permute-start(f32[256,256]{0,1:T(8,128)S(1)} %slice.101), channel_id=1, source_target_pairs={{0,1},{1,0},{2,3},{3,2},{4,5},{5,4},{6,7},{7,6},{8,9},{9,8},{10,11... | collective-permute-start | bytes 786440 | tf_op jit(solution)/shard_map/ppermute | solution.py:148
  36.6 1.7 %collective-permute-start.13 = (bf16[256,256]{0,1:T(8,128)(2,1)S(1)}, bf16[256,256]{0,1:T(8,128)(2,1)S(1)}, u32[]{:S(2)}, u32[]{:S(2)}) collective-permute-start(bf16[256,256]{0,1:T(8,128)(2,1)S(1)} %fusion.25), channel_id=1, source_target_pairs={{0,1},{1,0},{2,3},{3,2},{4,5},{5,4},{6,7},{7,6},{8,9},{9,8},{10,11... | collective-permute-start | bytes 393224 | tf_op jit(solution)/shard_map/ppermute | solution.py:150
  38.5 7.3 %collective-permute-start.14 = (bf16[256,256]{1,0:T(8,128)(2,1)S(1)}, bf16[256,256]{1,0:T(8,128)(2,1)S(1)}, u32[]{:S(2)}, u32[]{:S(2)}) collective-permute-start(bf16[256,256]{1,0:T(8,128)(2,1)S(1)} %convolution_convert_fusion.2), channel_id=1, source_target_pairs={{0,2},{1,3},{2,6},{3,7},{6,4},{7,5},{4,0},{5,1},{8,10},{9,11},{10,... | collective-permute-start | bytes 393224 | tf_op jit(solution)/shard_map/ppermute | solution.py:165
  40.1 8.5 %collective-permute-start.17 = (bf16[256,256]{1,0:T(8,128)(2,1)S(1)}, bf16[256,256]{1,0:T(8,128)(2,1)S(1)}, u32[]{:S(2)}, u32[]{:S(2)}) collective-permute-start(bf16[256,256]{1,0:T(8,128)(2,1)S(1)} %convolution_convert_fusion.1), channel_id=1, source_target_pairs={{0,2},{1,3},{2,6},{3,7},{6,4},{7,5},{4,0},{5,1},{8,10},{9,11},{10,... | collective-permute-start | bytes 393224 | tf_op jit(solution)/shard_map/ppermute | solution.py:165
  43.2 8.3 %collective-permute-start.20 = (bf16[256,256]{1,0:T(8,128)(2,1)S(1)}, bf16[256,256]{1,0:T(8,128)(2,1)S(1)}, u32[]{:S(2)}, u32[]{:S(2)}) collective-permute-start(bf16[256,256]{1,0:T(8,128)(2,1)S(1)} %convolution_convert_fusion), channel_id=1, source_target_pairs={{0,2},{1,3},{2,6},{3,7},{6,4},{7,5},{4,0},{5,1},{8,10},{9,11},{10,... | collective-permute-start | bytes 393224 | tf_op jit(solution)/shard_map/ppermute | solution.py:165
  46.1 8.1 %collective-permute-start.15 = (bf16[256,256]{1,0:T(8,128)(2,1)S(1)}, bf16[256,256]{1,0:T(8,128)(2,1)S(1)}, u32[]{:S(2)}, u32[]{:S(2)}) collective-permute-start(bf16[256,256]{1,0:T(8,128)(2,1)S(1)} %add_convert_fusion.5), channel_id=1, source_target_pairs={{0,2},{1,3},{2,6},{3,7},{6,4},{7,5},{4,0},{5,1},{8,10},{9,11},{10,... | collective-permute-start | bytes 393224 | tf_op jit(solution)/shard_map/ppermute | solution.py:165
  48.9 8.1 %collective-permute-start.18 = (bf16[256,256]{1,0:T(8,128)(2,1)S(1)}, bf16[256,256]{1,0:T(8,128)(2,1)S(1)}, u32[]{:S(2)}, u32[]{:S(2)}) collective-permute-start(bf16[256,256]{1,0:T(8,128)(2,1)S(1)} %add_convert_fusion.3), channel_id=1, source_target_pairs={{0,2},{1,3},{2,6},{3,7},{6,4},{7,5},{4,0},{5,1},{8,10},{9,11},{10,... | collective-permute-start | bytes 393224 | tf_op jit(solution)/shard_map/ppermute | solution.py:165
  51.7 8.1 %collective-permute-start.21 = (bf16[256,256]{1,0:T(8,128)(2,1)S(1)}, bf16[256,256]{1,0:T(8,128)(2,1)S(1)}, u32[]{:S(2)}, u32[]{:S(2)}) collective-permute-start(bf16[256,256]{1,0:T(8,128)(2,1)S(1)} %add_convert_fusion.1), channel_id=1, source_target_pairs={{0,2},{1,3},{2,6},{3,7},{6,4},{7,5},{4,0},{5,1},{8,10},{9,11},{10,... | collective-permute-start | bytes 393224 | tf_op jit(solution)/shard_map/ppermute | solution.py:165
  54.5 8.1 %collective-permute-start.16 = (bf16[256,256]{1,0:T(8,128)(2,1)S(1)}, bf16[256,256]{1,0:T(8,128)(2,1)S(1)}, u32[]{:S(2)}, u32[]{:S(2)}) collective-permute-start(bf16[256,256]{1,0:T(8,128)(2,1)S(1)} %add_convert_fusion.4), channel_id=1, source_target_pairs={{0,2},{1,3},{2,6},{3,7},{6,4},{7,5},{4,0},{5,1},{8,10},{9,11},{10,... | collective-permute-start | bytes 393224 | tf_op jit(solution)/shard_map/ppermute | solution.py:168
  57.4 8.1 %collective-permute-start.19 = (bf16[256,256]{1,0:T(8,128)(2,1)S(1)}, bf16[256,256]{1,0:T(8,128)(2,1)S(1)}, u32[]{:S(2)}, u32[]{:S(2)}) collective-permute-start(bf16[256,256]{1,0:T(8,128)(2,1)S(1)} %add_convert_fusion.2), channel_id=1, source_target_pairs={{0,2},{1,3},{2,6},{3,7},{6,4},{7,5},{4,0},{5,1},{8,10},{9,11},{10,... | collective-permute-start | bytes 393224 | tf_op jit(solution)/shard_map/ppermute | solution.py:168
  60.1 7.6 %collective-permute-start.22 = (bf16[256,256]{1,0:T(8,128)(2,1)S(1)}, bf16[256,256]{1,0:T(8,128)(2,1)S(1)}, u32[]{:S(2)}, u32[]{:S(2)}) collective-permute-start(bf16[256,256]{1,0:T(8,128)(2,1)S(1)} %add_convert_fusion), channel_id=1, source_target_pairs={{0,2},{1,3},{2,6},{3,7},{6,4},{7,5},{4,0},{5,1},{8,10},{9,11},{10,... | collective-permute-start | bytes 393224 | tf_op jit(solution)/shard_map/ppermute | solution.py:168
  (5 other events, 37.0 us)

commit v4 on v3

--- a/solution.py
+++ b/solution.py
@@ -6,7 +6,7 @@
 from jax.sharding import PartitionSpec as P
 
 ADAM_STEP = 100
-GATHER_CHUNKS = 3
+GATHER_CHUNKS = 2
 SCATTER_CHUNKS = 3
 
 
@@ -53,13 +53,14 @@
     return (jnp.concatenate([grad_query, grad_keys], axis=1) * input_scale).astype(jnp.bfloat16)
 
 
-def drift_of(outer):
-    frag_local, frag_global, frag_moment, frag_index = outer
+def outer_start(frag_local, frag_global, frag_moment, frag_index):
     chosen = frag_index[0]
     current = lax.dynamic_index_in_dim(frag_global, chosen, 0, keepdims=False)
+    moment_now = lax.dynamic_index_in_dim(frag_moment, chosen, 0, keepdims=False)
     local_copy = lax.dynamic_index_in_dim(frag_local[0], chosen, 0, keepdims=False)
     drift = (current - local_copy.astype(jnp.float32)).astype(jnp.bfloat16)
-    return lax.optimization_barrier(drift).astype(jnp.float32)
+    current, moment_now, drift = lax.optimization_barrier((current, moment_now, drift))
+    return current, moment_now, drift.astype(jnp.float32)
 
 
 def exchange(total, step):
@@ -67,11 +68,7 @@
     return total + lax.ppermute(total, "replica", [(i, i ^ step) for i in range(replicas)])
 
 
-def outer_finish(outer, total):
-    frag_local, frag_global, frag_moment, frag_index = outer
-    chosen = frag_index[0]
-    current = lax.dynamic_index_in_dim(frag_global, chosen, 0, keepdims=False)
-    moment_now = lax.dynamic_index_in_dim(frag_moment, chosen, 0, keepdims=False)
+def outer_finish(current, moment_now, total):
     drift_mean = total / lax.axis_size("replica")
     new_moment = outer_momentum * moment_now + drift_mean
     new_global = current - outer_rate * (drift_mean + outer_momentum * new_moment)
@@ -119,8 +116,9 @@
     blocks = [lowered[j * part : (j + 1) * part] for j in range(GATHER_CHUNKS)]
     flying = [lax.ppermute(block, "shard", ring) for block in blocks]
     partner = lax.ppermute(inputs, "shard", swap)
-    outer, flying[0] = lax.optimization_barrier((outer, flying[0]))
-    drift = exchange(drift_of(outer), 1)
+    current, moment_now, drift = outer_start(*outer)
+    drift, flying[0] = lax.optimization_barrier((drift, flying[0]))
+    drift = exchange(drift, 1)
     both = [
         jnp.concatenate([ordered(inputs, k), ordered(partner, k)], axis=0) for k in range(chips)
     ]
@@ -142,8 +140,6 @@
             if k == 0:
                 drift, flying[0] = lax.optimization_barrier((drift, flying[0]))
                 drift = exchange(drift, 2)
-            if k == 1:
-                drift, flying[0] = lax.optimization_barrier((drift, flying[0]))
     tokens = inputs.shape[0]
     projected = total[:tokens] + lax.ppermute(total[tokens:], "shard", swap)
     grad_own = head_grads(inputs, doc_ids[0], values, cotangent, projected)
@@ -167,7 +163,7 @@
     for j in range(SCATTER_CHUNKS):
         sums[j] = lax.ppermute(sums[j], "shard", ring).astype(jnp.float32) + term(0, j)
     updated = adam(jnp.concatenate(sums, axis=0), weights, moment1, moment2)
-    return updated + outer_finish(outer, drift)
+    return updated + outer_finish(current, moment_now, drift)
 
 
 def on_device(

time: 70.1 us -> 69.2 us (0.987)
  starting transfers between devices: 31.6 us -> 30.1 us
  waiting for transfers between devices: 20.6 us -> 21.7 us
  other arithmetic: 5.59 us -> 4.81 us
  local copies, waits for them, and re-layouts: 3.01 us -> 3.77 us
    ppermute x9 -> x6, waiting for transfers between devices: 5.21 us -> 8.54 us  [inner_step(): flying = [lax.ppermute(block, 'shard', ring) for block in blocks]]
    ppermute x9 -> x6, starting transfers between devices: 14.9 us -> 11.8 us  [inner_step(): flying = [lax.ppermute(block, 'shard', ring) for block in blocks]]
    ppermute x6, waiting for transfers between devices: 8.37 us -> 6.84 us  [inner_step(): came = lax.ppermute(sums[j], 'shard', ring)]
    ppermute x1, waiting for transfers between devices: 1.52 us -> 0.01 us  [inner_step(): projected = total[:tokens] + lax.ppermute(total[tokens:], 'shard', swap)]
    ppermute x2, waiting for transfers between devices: 0.01 us -> 1.52 us  [exchange(): lax.ppermute(total, 'replica', [(i, i ^ step) for i in range(replicas)])]
    ppermute x6, starting transfers between devices: 7.86 us -> 8.9 us  [inner_step(): came = lax.ppermute(sums[j], 'shard', ring)]
    ppermute x3, starting transfers between devices: 4.66 us -> 5.46 us  [inner_step(): lax.ppermute(sums[j], 'shard', ring).astype(jnp.float32) + term(0, j)]
    squeeze x0 -> x1, local copies, waits for them, and re-layouts: none -> 0.76 us  [outer_start(): lax.dynamic_index_in_dim(frag_moment, chosen, 0, keepdims=False)]
  transfers between devices with their start and end apart: 23 -> 20, of which waited for: 13 -> 16; matrix products, arithmetic and copies ran while one was open for 17% -> 19% of each run, Pallas kernels for 0% -> 0%
where the time goes in v4:
time: 69.2 us; the launch traced here: 68.9 us
  starting transfers between devices  30.1 us (43%)
  waiting for transfers between devices  21.7 us (31%)
  matrix products  6.92 us (10%)
  other arithmetic  4.81 us (7%)
  local copies, waits for them, and re-layouts  3.77 us (5%)
  between operations  1.65 us (2%)
    ppermute x6, starting transfers between devices, inner_step(): flying = [lax.ppermute(block, 'shard', ring) for block in blocks]  11.8 us
    ppermute x6, starting transfers between devices, inner_step(): came = lax.ppermute(sums[j], 'shard', ring)  8.9 us
    ppermute x6, waiting for transfers between devices, inner_step(): flying = [lax.ppermute(block, 'shard', ring) for block in blocks]  8.54 us
    ppermute x6, waiting for transfers between devices, inner_step(): came = lax.ppermute(sums[j], 'shard', ring)  6.84 us
    ppermute x3, starting transfers between devices, inner_step(): lax.ppermute(sums[j], 'shard', ring).astype(jnp.float32) + term(0, j)  5.46 us
    ppermute x3, waiting for transfers between devices, inner_step(): lax.ppermute(sums[j], 'shard', ring).astype(jnp.float32) + term(0, j)  4.76 us
    dot_general x12, matrix products, term(): lax.dot_general(both[k][:, j * part:(j + 1) * part], grad_both, (((0,), (...  3.3 us
    ppermute x2, starting transfers between devices, exchange(): lax.ppermute(total, 'replica', [(i, i ^ step) for i in range(replicas)])  3.13 us
  transfers between devices with their start and end apart: 20, of which 16 were waited for; matrix products, arithmetic and copies ran while one was open for 19% of the time, Pallas kernels for 0%

profile of v4, /device:TPU:0, one launch (start us, length us, event | category | flops | bytes accessed | tf_op | source)
XLA Modules:
  0.0 68.9 jit_solution(13057027323135868976)
XLA Ops:
  1.2 1.2 %convert_element_type.88 = bf16[768,256]{1,0:T(8,128)(2,1)S(1)} convert(f32[768,256]{1,0:T(8,128)} %param.15) | non-fusion elementwise | flops 196608 | bytes 1179648 | tf_op jit(solution)/shard_map/convert_element_type | solution.py:115
  2.4 2.6 %collective-permute-start.1 = (bf16[384,256]{1,0:T(8,128)(2,1)S(1)}, bf16[384,256]{1,0:T(8,128)(2,1)S(1)}, u32[]{:S(2)}, u32[]{:S(2)}) collective-permute-start(bf16[384,256]{1,0:T(8,128)(2,1)S(1)} %get-tuple-element.37), channel_id=1, source_target_pairs={{0,2},{1,3},{2,6},{3,7},{6,4},{7,5},{4,0},{5,1},{8,10},{9,11},{10,... | collective-permute-start | bytes 589832 | tf_op jit(solution)/shard_map/ppermute | solution.py:117
  5.0 2.6 %collective-permute-start.2 = (bf16[384,256]{1,0:T(8,128)(2,1)S(1)}, bf16[384,256]{1,0:T(8,128)(2,1)S(1)}, u32[]{:S(2)}, u32[]{:S(2)}) collective-permute-start(bf16[384,256]{1,0:T(8,128)(2,1)S(1)} %get-tuple-element.36), channel_id=1, source_target_pairs={{0,2},{1,3},{2,6},{3,7},{6,4},{7,5},{4,0},{5,1},{8,10},{9,11},{10,... | collective-permute-start | bytes 589832 | tf_op jit(solution)/shard_map/ppermute | solution.py:117
  10.0 1.8 %collective-permute-done.1 = bf16[384,256]{1,0:T(8,128)(2,1)S(1)} collective-permute-done((bf16[384,256]{1,0:T(8,128)(2,1)S(1)}, bf16[384,256]{1,0:T(8,128)(2,1)S(1)}, u32[]{:S(2)}, u32[]{:S(2)}) %collective-permute-start.1) | collective-permute-done | bytes 196640 | tf_op jit(solution)/shard_map/ppermute | solution.py:117
  11.8 1.0 %collective-permute-start.4 = (bf16[384,256]{1,0:T(8,128)(2,1)S(1)}, bf16[384,256]{1,0:T(8,128)(2,1)S(1)}, u32[]{:S(2)}, u32[]{:S(2)}) collective-permute-start(bf16[384,256]{1,0:T(8,128)(2,1)S(1)} %collective-permute-done.1), channel_id=1, source_target_pairs={{0,2},{1,3},{2,6},{3,7},{6,4},{7,5},{4,0},{5,1},{8,10},{9,11},{10,... | collective-permute-start | bytes 589832 | tf_op jit(solution)/shard_map/ppermute | solution.py:139
  12.8 3.2 %collective-permute-done.2 = bf16[384,256]{1,0:T(8,128)(2,1)S(1)} collective-permute-done((bf16[384,256]{1,0:T(8,128)(2,1)S(1)}, bf16[384,256]{1,0:T(8,128)(2,1)S(1)}, u32[]{:S(2)}, u32[]{:S(2)}) %collective-permute-start.2) | collective-permute-done | bytes 196640 | tf_op jit(solution)/shard_map/ppermute | solution.py:117
  16.0 1.0 %collective-permute-start.5 = (bf16[384,256]{1,0:T(8,128)(2,1)S(1)}, bf16[384,256]{1,0:T(8,128)(2,1)S(1)}, u32[]{:S(2)}, u32[]{:S(2)}) collective-permute-start(bf16[384,256]{1,0:T(8,128)(2,1)S(1)} %collective-permute-done.2), channel_id=1, source_target_pairs={{0,2},{1,3},{2,6},{3,7},{6,4},{7,5},{4,0},{5,1},{8,10},{9,11},{10,... | collective-permute-start | bytes 589832 | tf_op jit(solution)/shard_map/ppermute | solution.py:139
  17.0 1.5 %collective-permute-start.3 = (f32[1,6144]{1,0:T(1,128)S(1)}, f32[1,6144]{1,0:T(1,128)S(1)}, u32[]{:S(2)}, u32[]{:S(2)}) collective-permute-start(f32[1,6144]{1,0:T(1,128)S(1)} %convert_element_type.92), channel_id=1, source_target_pairs={{0,8},{8,0},{16,24},{24,16},{1,9},{9,1},{17,25},{25,17},{2,10},{10... | collective-permute-start | bytes 73736 | tf_op jit(solution)/shard_map/ppermute | solution.py:68
  18.5 1.5 %constant_dynamic-slice_fusion.5 = (bf16[256,768]{1,0:T(8,128)(2,1)S(1)}, bf16[256,768]{1,0:T(8,128)(2,1)S(1)}, bf16[256,768]{1,0:T(8,128)(2,1)S(1)}, bf16[256,768]{1,0:T(8,128)(2,1)S(1)}) fusion(bf16[256,6144]{1,0:T(8,128)(2,1)} %param.11, s32[]{:T(128)S(6)} %select_n.74, s32[]{:T(128)S(6)} %select_n.71, s32[]{:T(128)S(6)} %select_n.81, s32[]{:T(128)S(6)} %select_n.78), kind=kLoop, calls=%fused_computation.127 | loop fusion | bytes 3145744 | tf_op jit(solution)/shard_map/dynamic_slice | solution.py:112
  20.9 3.4 %collective-permute-start.6 = (bf16[384,256]{1,0:T(8,128)(2,1)S(1)}, bf16[384,256]{1,0:T(8,128)(2,1)S(1)}, u32[]{:S(2)}, u32[]{:S(2)}) collective-permute-start(bf16[384,256]{1,0:T(8,128)(2,1)S(1)} %collective-permute-done.4), channel_id=1, source_target_pairs={{0,2},{1,3},{2,6},{3,7},{6,4},{7,5},{4,0},{5,1},{8,10},{9,11},{10,... | collective-permute-start | bytes 589832 | tf_op jit(solution)/shard_map/ppermute | solution.py:139
  25.8 1.5 %constant_dynamic-slice_fusion.4 = (bf16[256,768]{1,0:T(8,128)(2,1)S(1)}, bf16[256,768]{1,0:T(8,128)(2,1)S(1)}, bf16[256,768]{1,0:T(8,128)(2,1)S(1)}, bf16[256,768]{1,0:T(8,128)(2,1)S(1)}) fusion(bf16[256,6144]{1,0:T(8,128)(2,1)} %collective-permute-done, s32[]{:T(128)S(6)} %select_n.74, s32[]{:T(128)S(6)} %select_n.81, s32[]{:T(128)S(6)} %select_n.78, ...), kind=kLoop, calls=%fused_computation.126 | loop fusion | bytes 3145744 | tf_op jit(solution)/shard_map/dynamic_slice | solution.py:112
  30.2 2.4 %collective-permute-done.7 = bf16[384,256]{1,0:T(8,128)(2,1)S(1)} collective-permute-done((bf16[384,256]{1,0:T(8,128)(2,1)S(1)}, bf16[384,256]{1,0:T(8,128)(2,1)S(1)}, u32[]{:S(2)}, u32[]{:S(2)}) %collective-permute-start.7) | collective-permute-done | bytes 196640 | tf_op jit(solution)/shard_map/ppermute | solution.py:139
  33.1 1.6 %collective-permute-start.19 = (f32[1,6144]{1,0:T(1,128)S(1)}, f32[1,6144]{1,0:T(1,128)S(1)}, u32[]{:S(2)}, u32[]{:S(2)}) collective-permute-start(f32[1,6144]{1,0:T(1,128)S(1)} %add.166), channel_id=1, source_target_pairs={{0,16},{8,24},{16,0},{24,8},{1,17},{9,25},{17,1},{25,9},{2,18},{10... | collective-permute-start | bytes 73736 | tf_op jit(solution)/shard_map/ppermute | solution.py:68
  39.2 3.3 %collective-permute-start.13 = (bf16[256,256]{1,0:T(8,128)(2,1)S(1)}, bf16[256,256]{1,0:T(8,128)(2,1)S(1)}, u32[]{:S(2)}, u32[]{:S(2)}) collective-permute-start(bf16[256,256]{1,0:T(8,128)(2,1)S(1)} %convolution_convert_fusion.1), channel_id=1, source_target_pairs={{0,2},{1,3},{2,6},{3,7},{6,4},{7,5},{4,0},{5,1},{8,10},{9,11},{10,... | collective-permute-start | bytes 393224 | tf_op jit(solution)/shard_map/ppermute | solution.py:161
  42.9 2.4 %collective-permute-done.16 = bf16[256,256]{1,0:T(8,128)(2,1)S(1)} collective-permute-done((bf16[256,256]{1,0:T(8,128)(2,1)S(1)}, bf16[256,256]{1,0:T(8,128)(2,1)S(1)}, u32[]{:S(2)}, u32[]{:S(2)}) %collective-permute-start.16) | collective-permute-done | bytes 131104 | tf_op jit(solution)/shard_map/ppermute | solution.py:161
  46.5 1.6 %collective-permute-done.13 = bf16[256,256]{1,0:T(8,128)(2,1)S(1)} collective-permute-done((bf16[256,256]{1,0:T(8,128)(2,1)S(1)}, bf16[256,256]{1,0:T(8,128)(2,1)S(1)}, u32[]{:S(2)}, u32[]{:S(2)}) %collective-permute-start.13) | collective-permute-done | bytes 131104 | tf_op jit(solution)/shard_map/ppermute | solution.py:161
  48.4 1.8 %collective-permute-start.14 = (bf16[256,256]{1,0:T(8,128)(2,1)S(1)}, bf16[256,256]{1,0:T(8,128)(2,1)S(1)}, u32[]{:S(2)}, u32[]{:S(2)}) collective-permute-start(bf16[256,256]{1,0:T(8,128)(2,1)S(1)} %add_convert_fusion.3), channel_id=1, source_target_pairs={{0,2},{1,3},{2,6},{3,7},{6,4},{7,5},{4,0},{5,1},{8,10},{9,11},{10,... | collective-permute-start | bytes 393224 | tf_op jit(solution)/shard_map/ppermute | solution.py:161
  51.2 1.8 %collective-permute-start.11 = (bf16[256,256]{1,0:T(8,128)(2,1)S(1)}, bf16[256,256]{1,0:T(8,128)(2,1)S(1)}, u32[]{:S(2)}, u32[]{:S(2)}) collective-permute-start(bf16[256,256]{1,0:T(8,128)(2,1)S(1)} %add_convert_fusion.5), channel_id=1, source_target_pairs={{0,2},{1,3},{2,6},{3,7},{6,4},{7,5},{4,0},{5,1},{8,10},{9,11},{10,... | collective-permute-start | bytes 393224 | tf_op jit(solution)/shard_map/ppermute | solution.py:161
  54.0 1.8 %collective-permute-start.18 = (bf16[256,256]{1,0:T(8,128)(2,1)S(1)}, bf16[256,256]{1,0:T(8,128)(2,1)S(1)}, u32[]{:S(2)}, u32[]{:S(2)}) collective-permute-start(bf16[256,256]{1,0:T(8,128)(2,1)S(1)} %add_convert_fusion), channel_id=1, source_target_pairs={{0,2},{1,3},{2,6},{3,7},{6,4},{7,5},{4,0},{5,1},{8,10},{9,11},{10,... | collective-permute-start | bytes 393224 | tf_op jit(solution)/shard_map/ppermute | solution.py:164
  56.9 1.8 %collective-permute-start.15 = (bf16[256,256]{1,0:T(8,128)(2,1)S(1)}, bf16[256,256]{1,0:T(8,128)(2,1)S(1)}, u32[]{:S(2)}, u32[]{:S(2)}) collective-permute-start(bf16[256,256]{1,0:T(8,128)(2,1)S(1)} %add_convert_fusion.2), channel_id=1, source_target_pairs={{0,2},{1,3},{2,6},{3,7},{6,4},{7,5},{4,0},{5,1},{8,10},{9,11},{10,... | collective-permute-start | bytes 393224 | tf_op jit(solution)/shard_map/ppermute | solution.py:164
  59.6 1.8 %collective-permute-start.12 = (bf16[256,256]{1,0:T(8,128)(2,1)S(1)}, bf16[256,256]{1,0:T(8,128)(2,1)S(1)}, u32[]{:S(2)}, u32[]{:S(2)}) collective-permute-start(bf16[256,256]{1,0:T(8,128)(2,1)S(1)} %add_convert_fusion.4), channel_id=1, source_target_pairs={{0,2},{1,3},{2,6},{3,7},{6,4},{7,5},{4,0},{5,1},{8,10},{9,11},{10,... | collective-permute-start | bytes 393224 | tf_op jit(solution)/shard_map/ppermute | solution.py:164
  62.4 2.5 %collective-permute-done.15 = bf16[256,256]{1,0:T(8,128)(2,1)S(1)} collective-permute-done((bf16[256,256]{1,0:T(8,128)(2,1)S(1)}, bf16[256,256]{1,0:T(8,128)(2,1)S(1)}, u32[]{:S(2)}, u32[]{:S(2)}) %collective-permute-start.15) | collective-permute-done | bytes 131104 | tf_op jit(solution)/shard_map/ppermute | solution.py:164
  65.3 1.6 %collective-permute-done.12 = bf16[256,256]{1,0:T(8,128)(2,1)S(1)} collective-permute-done((bf16[256,256]{1,0:T(8,128)(2,1)S(1)}, bf16[256,256]{1,0:T(8,128)(2,1)S(1)}, u32[]{:S(2)}, u32[]{:S(2)}) %collective-permute-start.12) | collective-permute-done | bytes 131104 | tf_op jit(solution)/shard_map/ppermute | solution.py:164
  67.1 1.8 %multiply_subtract_fusion = (f32[768,256]{1,0:T(8,128)}, f32[768,256]{1,0:T(8,128)}, f32[768,256]{1,0:T(8,128)}) fusion(f32[768,256]{1,0:T(8,128)S(1)} %copy-done.1, f32[256,256]{1,0:T(8,128)S(1)} %convert_add_fusion, f32[256,256]{1,0:T(8,128)S(1)} %convert_add_fusion.1, f32[256,256]{1,0:T(8,128)S(1)} %convert_add_fusion.2, f32[768,256]{1,0:T(8,128)S(1)} %copy-done.2, ...), kind=kLoop, calls=%fused_computation.46 | loop fusion | flops 3342336 | bytes 5505024 | tf_op jit(solution)/shard_map/sub | solution.py:83
  (70 shorter events, 19.6 us)
Async XLA Ops:
  0.6 34.6 %copy-start = (bf16[256,128]{1,0:T(8,128)(2,1)S(1)}, bf16[256,128]{1,0:T(8,128)(2,1)}, u32[]{:S(2)}) copy-start(bf16[256,128]{1,0:T(8,128)(2,1)} %param.14) | copy-start | bytes 196612
  0.6 25.1 %collective-permute-start = (bf16[256,6144]{1,0:T(8,128)(2,1)}, bf16[256,6144]{1,0:T(8,128)(2,1)}, u32[]{:S(2)}, u32[]{:S(2)}) collective-permute-start(bf16[256,6144]{1,0:T(8,128)(2,1)} %param.11), channel_id=1, source_target_pairs={{0,1},{1,0},{2,3},{3,2},{4,5},{5,4},{6,7},{7,6},{8,9},{9,8},{10,11... | collective-permute-start | bytes 9437192 | tf_op jit(solution)/shard_map/ppermute | solution.py:118
  2.4 9.4 %collective-permute-start.1 = (bf16[384,256]{1,0:T(8,128)(2,1)S(1)}, bf16[384,256]{1,0:T(8,128)(2,1)S(1)}, u32[]{:S(2)}, u32[]{:S(2)}) collective-permute-start(bf16[384,256]{1,0:T(8,128)(2,1)S(1)} %get-tuple-element.37), channel_id=1, source_target_pairs={{0,2},{1,3},{2,6},{3,7},{6,4},{7,5},{4,0},{5,1},{8,10},{9,11},{10,... | collective-permute-start | bytes 589832 | tf_op jit(solution)/shard_map/ppermute | solution.py:117
  5.0 11.0 %collective-permute-start.2 = (bf16[384,256]{1,0:T(8,128)(2,1)S(1)}, bf16[384,256]{1,0:T(8,128)(2,1)S(1)}, u32[]{:S(2)}, u32[]{:S(2)}) collective-permute-start(bf16[384,256]{1,0:T(8,128)(2,1)S(1)} %get-tuple-element.36), channel_id=1, source_target_pairs={{0,2},{1,3},{2,6},{3,7},{6,4},{7,5},{4,0},{5,1},{8,10},{9,11},{10,... | collective-permute-start | bytes 589832 | tf_op jit(solution)/shard_map/ppermute | solution.py:117
  11.8 9.1 %collective-permute-start.4 = (bf16[384,256]{1,0:T(8,128)(2,1)S(1)}, bf16[384,256]{1,0:T(8,128)(2,1)S(1)}, u32[]{:S(2)}, u32[]{:S(2)}) collective-permute-start(bf16[384,256]{1,0:T(8,128)(2,1)S(1)} %collective-permute-done.1), channel_id=1, source_target_pairs={{0,2},{1,3},{2,6},{3,7},{6,4},{7,5},{4,0},{5,1},{8,10},{9,11},{10,... | collective-permute-start | bytes 589832 | tf_op jit(solution)/shard_map/ppermute | solution.py:139
  16.0 8.7 %collective-permute-start.5 = (bf16[384,256]{1,0:T(8,128)(2,1)S(1)}, bf16[384,256]{1,0:T(8,128)(2,1)S(1)}, u32[]{:S(2)}, u32[]{:S(2)}) collective-permute-start(bf16[384,256]{1,0:T(8,128)(2,1)S(1)} %collective-permute-done.2), channel_id=1, source_target_pairs={{0,2},{1,3},{2,6},{3,7},{6,4},{7,5},{4,0},{5,1},{8,10},{9,11},{10,... | collective-permute-start | bytes 589832 | tf_op jit(solution)/shard_map/ppermute | solution.py:139
  17.0 3.8 %collective-permute-start.3 = (f32[1,6144]{1,0:T(1,128)S(1)}, f32[1,6144]{1,0:T(1,128)S(1)}, u32[]{:S(2)}, u32[]{:S(2)}) collective-permute-start(f32[1,6144]{1,0:T(1,128)S(1)} %convert_element_type.92), channel_id=1, source_target_pairs={{0,8},{8,0},{16,24},{24,16},{1,9},{9,1},{17,25},{25,17},{2,10},{10... | collective-permute-start | bytes 73736 | tf_op jit(solution)/shard_map/ppermute | solution.py:68
  20.9 8.6 %collective-permute-start.6 = (bf16[384,256]{1,0:T(8,128)(2,1)S(1)}, bf16[384,256]{1,0:T(8,128)(2,1)S(1)}, u32[]{:S(2)}, u32[]{:S(2)}) collective-permute-start(bf16[384,256]{1,0:T(8,128)(2,1)S(1)} %collective-permute-done.4), channel_id=1, source_target_pairs={{0,2},{1,3},{2,6},{3,7},{6,4},{7,5},{4,0},{5,1},{8,10},{9,11},{10,... | collective-permute-start | bytes 589832 | tf_op jit(solution)/shard_map/ppermute | solution.py:139
  24.7 7.9 %collective-permute-start.7 = (bf16[384,256]{1,0:T(8,128)(2,1)S(1)}, bf16[384,256]{1,0:T(8,128)(2,1)S(1)}, u32[]{:S(2)}, u32[]{:S(2)}) collective-permute-start(bf16[384,256]{1,0:T(8,128)(2,1)S(1)} %collective-permute-done.5), channel_id=1, source_target_pairs={{0,2},{1,3},{2,6},{3,7},{6,4},{7,5},{4,0},{5,1},{8,10},{9,11},{10,... | collective-permute-start | bytes 589832 | tf_op jit(solution)/shard_map/ppermute | solution.py:139
  33.0 1.7 %collective-permute-start.8 = (f32[256,256]{0,1:T(8,128)S(1)}, f32[256,256]{0,1:T(8,128)S(1)}, u32[]{:S(2)}, u32[]{:S(2)}) collective-permute-start(f32[256,256]{0,1:T(8,128)S(1)} %slice.113), channel_id=1, source_target_pairs={{0,1},{1,0},{2,3},{3,2},{4,5},{5,4},{6,7},{7,6},{8,9},{9,8},{10,11... | collective-permute-start | bytes 786440 | tf_op jit(solution)/shard_map/ppermute | solution.py:144
  33.1 3.9 %collective-permute-start.19 = (f32[1,6144]{1,0:T(1,128)S(1)}, f32[1,6144]{1,0:T(1,128)S(1)}, u32[]{:S(2)}, u32[]{:S(2)}) collective-permute-start(f32[1,6144]{1,0:T(1,128)S(1)} %add.166), channel_id=1, source_target_pairs={{0,16},{8,24},{16,0},{24,8},{1,17},{9,25},{17,1},{25,9},{2,18},{10... | collective-permute-start | bytes 73736 | tf_op jit(solution)/shard_map/ppermute | solution.py:68
  36.1 1.6 %collective-permute-start.9 = (bf16[256,256]{0,1:T(8,128)(2,1)S(1)}, bf16[256,256]{0,1:T(8,128)(2,1)S(1)}, u32[]{:S(2)}, u32[]{:S(2)}) collective-permute-start(bf16[256,256]{0,1:T(8,128)(2,1)S(1)} %fusion.53), channel_id=1, source_target_pairs={{0,1},{1,0},{2,3},{3,2},{4,5},{5,4},{6,7},{7,6},{8,9},{9,8},{10,11... | collective-permute-start | bytes 393224 | tf_op jit(solution)/shard_map/ppermute | solution.py:146
  38.0 7.3 %collective-permute-start.16 = (bf16[256,256]{1,0:T(8,128)(2,1)S(1)}, bf16[256,256]{1,0:T(8,128)(2,1)S(1)}, u32[]{:S(2)}, u32[]{:S(2)}) collective-permute-start(bf16[256,256]{1,0:T(8,128)(2,1)S(1)} %convolution_convert_fusion), channel_id=1, source_target_pairs={{0,2},{1,3},{2,6},{3,7},{6,4},{7,5},{4,0},{5,1},{8,10},{9,11},{10,... | collective-permute-start | bytes 393224 | tf_op jit(solution)/shard_map/ppermute | solution.py:161
  39.2 8.9 %collective-permute-start.13 = (bf16[256,256]{1,0:T(8,128)(2,1)S(1)}, bf16[256,256]{1,0:T(8,128)(2,1)S(1)}, u32[]{:S(2)}, u32[]{:S(2)}) collective-permute-start(bf16[256,256]{1,0:T(8,128)(2,1)S(1)} %convolution_convert_fusion.1), channel_id=1, source_target_pairs={{0,2},{1,3},{2,6},{3,7},{6,4},{7,5},{4,0},{5,1},{8,10},{9,11},{10,... | collective-permute-start | bytes 393224 | tf_op jit(solution)/shard_map/ppermute | solution.py:161
  42.9 8.1 %collective-permute-start.10 = (bf16[256,256]{1,0:T(8,128)(2,1)S(1)}, bf16[256,256]{1,0:T(8,128)(2,1)S(1)}, u32[]{:S(2)}, u32[]{:S(2)}) collective-permute-start(bf16[256,256]{1,0:T(8,128)(2,1)S(1)} %convolution_convert_fusion.2), channel_id=1, source_target_pairs={{0,2},{1,3},{2,6},{3,7},{6,4},{7,5},{4,0},{5,1},{8,10},{9,11},{10,... | collective-permute-start | bytes 393224 | tf_op jit(solution)/shard_map/ppermute | solution.py:161
  45.6 8.1 %collective-permute-start.17 = (bf16[256,256]{1,0:T(8,128)(2,1)S(1)}, bf16[256,256]{1,0:T(8,128)(2,1)S(1)}, u32[]{:S(2)}, u32[]{:S(2)}) collective-permute-start(bf16[256,256]{1,0:T(8,128)(2,1)S(1)} %add_convert_fusion.1), channel_id=1, source_target_pairs={{0,2},{1,3},{2,6},{3,7},{6,4},{7,5},{4,0},{5,1},{8,10},{9,11},{10,... | collective-permute-start | bytes 393224 | tf_op jit(solution)/shard_map/ppermute | solution.py:161
  48.4 8.1 %collective-permute-start.14 = (bf16[256,256]{1,0:T(8,128)(2,1)S(1)}, bf16[256,256]{1,0:T(8,128)(2,1)S(1)}, u32[]{:S(2)}, u32[]{:S(2)}) collective-permute-start(bf16[256,256]{1,0:T(8,128)(2,1)S(1)} %add_convert_fusion.3), channel_id=1, source_target_pairs={{0,2},{1,3},{2,6},{3,7},{6,4},{7,5},{4,0},{5,1},{8,10},{9,11},{10,... | collective-permute-start | bytes 393224 | tf_op jit(solution)/shard_map/ppermute | solution.py:161
  51.2 8.1 %collective-permute-start.11 = (bf16[256,256]{1,0:T(8,128)(2,1)S(1)}, bf16[256,256]{1,0:T(8,128)(2,1)S(1)}, u32[]{:S(2)}, u32[]{:S(2)}) collective-permute-start(bf16[256,256]{1,0:T(8,128)(2,1)S(1)} %add_convert_fusion.5), channel_id=1, source_target_pairs={{0,2},{1,3},{2,6},{3,7},{6,4},{7,5},{4,0},{5,1},{8,10},{9,11},{10,... | collective-permute-start | bytes 393224 | tf_op jit(solution)/shard_map/ppermute | solution.py:161
  54.0 8.1 %collective-permute-start.18 = (bf16[256,256]{1,0:T(8,128)(2,1)S(1)}, bf16[256,256]{1,0:T(8,128)(2,1)S(1)}, u32[]{:S(2)}, u32[]{:S(2)}) collective-permute-start(bf16[256,256]{1,0:T(8,128)(2,1)S(1)} %add_convert_fusion), channel_id=1, source_target_pairs={{0,2},{1,3},{2,6},{3,7},{6,4},{7,5},{4,0},{5,1},{8,10},{9,11},{10,... | collective-permute-start | bytes 393224 | tf_op jit(solution)/shard_map/ppermute | solution.py:164
  56.8 10.3 %copy-start.1 = (f32[768,256]{1,0:T(8,128)S(1)}, f32[768,256]{1,0:T(8,128)}, u32[]{:S(2)}) copy-start(f32[768,256]{1,0:T(8,128)} %param.15) | copy-start | bytes 2359300
  56.8 10.3 %copy-start.2 = (f32[768,256]{1,0:T(8,128)S(1)}, f32[768,256]{1,0:T(8,128)}, u32[]{:S(2)}) copy-start(f32[768,256]{1,0:T(8,128)} %param.16) | copy-start | bytes 2359300
  56.8 10.3 %copy-start.3 = (f32[768,256]{1,0:T(8,128)S(1)}, f32[768,256]{1,0:T(8,128)}, u32[]{:S(2)}) copy-start(f32[768,256]{1,0:T(8,128)} %param.17) | copy-start | bytes 2359300
  56.9 8.1 %collective-permute-start.15 = (bf16[256,256]{1,0:T(8,128)(2,1)S(1)}, bf16[256,256]{1,0:T(8,128)(2,1)S(1)}, u32[]{:S(2)}, u32[]{:S(2)}) collective-permute-start(bf16[256,256]{1,0:T(8,128)(2,1)S(1)} %add_convert_fusion.2), channel_id=1, source_target_pairs={{0,2},{1,3},{2,6},{3,7},{6,4},{7,5},{4,0},{5,1},{8,10},{9,11},{10,... | collective-permute-start | bytes 393224 | tf_op jit(solution)/shard_map/ppermute | solution.py:164
  59.6 7.2 %collective-permute-start.12 = (bf16[256,256]{1,0:T(8,128)(2,1)S(1)}, bf16[256,256]{1,0:T(8,128)(2,1)S(1)}, u32[]{:S(2)}, u32[]{:S(2)}) collective-permute-start(bf16[256,256]{1,0:T(8,128)(2,1)S(1)} %add_convert_fusion.4), channel_id=1, source_target_pairs={{0,2},{1,3},{2,6},{3,7},{6,4},{7,5},{4,0},{5,1},{8,10},{9,11},{10,... | collective-permute-start | bytes 393224 | tf_op jit(solution)/shard_map/ppermute | solution.py:164
  (2 other events, 10.4 us)

commit v5 on v4

--- a/solution.py
+++ b/solution.py
@@ -6,8 +6,8 @@
 from jax.sharding import PartitionSpec as P
 
 ADAM_STEP = 100
-GATHER_CHUNKS = 2
-SCATTER_CHUNKS = 3
+GATHER_SHARES = (24, 24)
+SCATTER_SHARES = (16, 16, 16)
 
 
 epsilon = 1e-06
@@ -65,6 +65,8 @@
 
 def exchange(total, step):
     replicas = lax.axis_size("replica")
+    if step >= replicas:
+        return total
     return total + lax.ppermute(total, "replica", [(i, i ^ step) for i in range(replicas)])
 
 
@@ -84,6 +86,11 @@
         first_hat / (jnp.sqrt(second_hat) + 1e-08) + decay_rate * weights
     )
     return (weight_new, first_new, second_new)
+
+
+def spans(rows, shares):
+    ends = [rows * sum(shares[:j]) // sum(shares) for j in range(len(shares) + 1)]
+    return [slice(a, b) for a, b in zip(ends[:-1], ends[1:])]
 
 
 def spot_of(chip, chips):
@@ -111,9 +118,9 @@
         chip = chip_at(lax.rem(spot + (chips - k), chips), chips)
         return lax.dynamic_slice_in_dim(tokens, (2 * chip + core) * rows, rows, axis=1)
 
-    part = rows // GATHER_CHUNKS
+    cuts = spans(rows, GATHER_SHARES)
     lowered = weights.astype(jnp.bfloat16)
-    blocks = [lowered[j * part : (j + 1) * part] for j in range(GATHER_CHUNKS)]
+    blocks = [lowered[cut] for cut in cuts]
     flying = [lax.ppermute(block, "shard", ring) for block in blocks]
     partner = lax.ppermute(inputs, "shard", swap)
     current, moment_now, drift = outer_start(*outer)
@@ -122,46 +129,47 @@
     both = [
         jnp.concatenate([ordered(inputs, k), ordered(partner, k)], axis=0) for k in range(chips)
     ]
-    total = jnp.float32(0.0)
     for k in range(chips):
-        if k in (0,):
-            block = lowered if k == 0 else jnp.concatenate(blocks, axis=0)
-            total = total + jnp.dot(both[k], block, preferred_element_type=jnp.float32)
-        for j in range(GATHER_CHUNKS if k not in (0,) else 0):
-            total = total + jnp.dot(
-                both[k][:, j * part : (j + 1) * part],
-                blocks[j],
-                preferred_element_type=jnp.float32,
-            )
+        if k == 0:
+            total = jnp.dot(both[0], lowered, preferred_element_type=jnp.float32)
+        else:
+            for cut, block in zip(cuts, blocks):
+                total = total + jnp.dot(
+                    both[k][:, cut], block, preferred_element_type=jnp.float32
+                )
         if k < chips - 1:
             blocks = flying
             if k < chips - 2:
                 flying = [lax.ppermute(block, "shard", ring) for block in blocks]
             if k == 0:
                 drift, flying[0] = lax.optimization_barrier((drift, flying[0]))
-                drift = exchange(drift, 2)
+                step = 2
+                while step < lax.axis_size("replica"):
+                    drift = exchange(drift, step)
+                    step = 2 * step
     tokens = inputs.shape[0]
     projected = total[:tokens] + lax.ppermute(total[tokens:], "shard", swap)
     grad_own = head_grads(inputs, doc_ids[0], values, cotangent, projected)
     grad_both = jnp.concatenate([grad_own, lax.ppermute(grad_own, "shard", swap)], axis=0)
 
-    part = rows // SCATTER_CHUNKS
+    cuts = spans(rows, SCATTER_SHARES)
 
     def term(k, j):
         return lax.dot_general(
-            both[k][:, j * part : (j + 1) * part],
+            both[k][:, cuts[j]],
             grad_both,
             (((0,), (0,)), ((), ())),
             preferred_element_type=jnp.float32,
         )
 
-    sums = [term(1, j).astype(jnp.bfloat16) for j in range(SCATTER_CHUNKS)]
+    sums = [term(1, j).astype(jnp.bfloat16) for j in range(len(cuts))]
     for k in range(2, chips):
-        for j in range(SCATTER_CHUNKS):
+        for j in range(len(cuts)):
             came = lax.ppermute(sums[j], "shard", ring)
             sums[j] = (came.astype(jnp.float32) + term(k, j)).astype(jnp.bfloat16)
-    for j in range(SCATTER_CHUNKS):
-        sums[j] = lax.ppermute(sums[j], "shard", ring).astype(jnp.float32) + term(0, j)
+    for j in range(len(cuts)):
+        own = lax.optimization_barrier(term(0, j))
+        sums[j] = lax.ppermute(sums[j], "shard", ring).astype(jnp.float32) + own
     updated = adam(jnp.concatenate(sums, axis=0), weights, moment1, moment2)
     return updated + outer_finish(current, moment_now, drift)
 

time: 69.2 us -> 69 us (level)
  waiting for transfers between devices: 21.7 us -> 20.7 us
    ppermute x6, waiting for transfers between devices: 6.84 us -> 5.32 us  [inner_step(): came = lax.ppermute(sums[j], 'shard', ring)]
where the time goes in v5:
time: 69 us; the launch traced here: 68.7 us
  starting transfers between devices  30.7 us (44%)
  waiting for transfers between devices  20.7 us (30%)
  matrix products  6.93 us (10%)
  other arithmetic  4.92 us (7%)
  local copies, waits for them, and re-layouts  3.77 us (5%)
  between operations  1.66 us (2%)
    ppermute x6, starting transfers between devices, inner_step(): flying = [lax.ppermute(block, 'shard', ring) for block in blocks]  11.8 us
    ppermute x6, starting transfers between devices, inner_step(): came = lax.ppermute(sums[j], 'shard', ring)  9.25 us
    ppermute x6, waiting for transfers between devices, inner_step(): flying = [lax.ppermute(block, 'shard', ring) for block in blocks]  8.54 us
    ppermute x3, starting transfers between devices, inner_step(): sums[j] = lax.ppermute(sums[j], 'shard', ring).astype(jnp.float32) + own  5.73 us
    ppermute x6, waiting for transfers between devices, inner_step(): came = lax.ppermute(sums[j], 'shard', ring)  5.32 us
    ppermute x3, waiting for transfers between devices, inner_step(): sums[j] = lax.ppermute(sums[j], 'shard', ring).astype(jnp.float32) + own  5.3 us
    dot_general x12, matrix products, term(): lax.dot_general(both[k][:, cuts[j]], grad_both, (((0,), (0,)), ((), ())),...  3.3 us
    ppermute x2, starting transfers between devices, exchange(): lax.ppermute(total, 'replica', [(i, i ^ step) for i in range(replicas)])  3.13 us
  transfers between devices with their start and end apart: 20, of which 16 were waited for; matrix products, arithmetic and copies ran while one was open for 19% of the time, Pallas kernels for 0%

profile of v5, /device:TPU:0, one launch (start us, length us, event | category | flops | bytes accessed | tf_op | source)
XLA Modules:
  0.0 68.7 jit_solution(10913167371169956561)
XLA Ops:
  1.2 1.2 %convert_element_type.88 = bf16[768,256]{1,0:T(8,128)(2,1)S(1)} convert(f32[768,256]{1,0:T(8,128)} %param.15) | non-fusion elementwise | flops 196608 | bytes 1179648 | tf_op jit(solution)/shard_map/convert_element_type | solution.py:122
  2.4 2.6 %collective-permute-start.1 = (bf16[384,256]{1,0:T(8,128)(2,1)S(1)}, bf16[384,256]{1,0:T(8,128)(2,1)S(1)}, u32[]{:S(2)}, u32[]{:S(2)}) collective-permute-start(bf16[384,256]{1,0:T(8,128)(2,1)S(1)} %get-tuple-element.37), channel_id=1, source_target_pairs={{0,2},{1,3},{2,6},{3,7},{6,4},{7,5},{4,0},{5,1},{8,10},{9,11},{10,... | collective-permute-start | bytes 589832 | tf_op jit(solution)/shard_map/ppermute | solution.py:124
  5.0 2.6 %collective-permute-start.2 = (bf16[384,256]{1,0:T(8,128)(2,1)S(1)}, bf16[384,256]{1,0:T(8,128)(2,1)S(1)}, u32[]{:S(2)}, u32[]{:S(2)}) collective-permute-start(bf16[384,256]{1,0:T(8,128)(2,1)S(1)} %get-tuple-element.36), channel_id=1, source_target_pairs={{0,2},{1,3},{2,6},{3,7},{6,4},{7,5},{4,0},{5,1},{8,10},{9,11},{10,... | collective-permute-start | bytes 589832 | tf_op jit(solution)/shard_map/ppermute | solution.py:124
  10.0 1.8 %collective-permute-done.1 = bf16[384,256]{1,0:T(8,128)(2,1)S(1)} collective-permute-done((bf16[384,256]{1,0:T(8,128)(2,1)S(1)}, bf16[384,256]{1,0:T(8,128)(2,1)S(1)}, u32[]{:S(2)}, u32[]{:S(2)}) %collective-permute-start.1) | collective-permute-done | bytes 196640 | tf_op jit(solution)/shard_map/ppermute | solution.py:124
  11.8 1.0 %collective-permute-start.4 = (bf16[384,256]{1,0:T(8,128)(2,1)S(1)}, bf16[384,256]{1,0:T(8,128)(2,1)S(1)}, u32[]{:S(2)}, u32[]{:S(2)}) collective-permute-start(bf16[384,256]{1,0:T(8,128)(2,1)S(1)} %collective-permute-done.1), channel_id=1, source_target_pairs={{0,2},{1,3},{2,6},{3,7},{6,4},{7,5},{4,0},{5,1},{8,10},{9,11},{10,... | collective-permute-start | bytes 589832 | tf_op jit(solution)/shard_map/ppermute | solution.py:143
  12.8 3.2 %collective-permute-done.2 = bf16[384,256]{1,0:T(8,128)(2,1)S(1)} collective-permute-done((bf16[384,256]{1,0:T(8,128)(2,1)S(1)}, bf16[384,256]{1,0:T(8,128)(2,1)S(1)}, u32[]{:S(2)}, u32[]{:S(2)}) %collective-permute-start.2) | collective-permute-done | bytes 196640 | tf_op jit(solution)/shard_map/ppermute | solution.py:124
  16.0 1.0 %collective-permute-start.5 = (bf16[384,256]{1,0:T(8,128)(2,1)S(1)}, bf16[384,256]{1,0:T(8,128)(2,1)S(1)}, u32[]{:S(2)}, u32[]{:S(2)}) collective-permute-start(bf16[384,256]{1,0:T(8,128)(2,1)S(1)} %collective-permute-done.2), channel_id=1, source_target_pairs={{0,2},{1,3},{2,6},{3,7},{6,4},{7,5},{4,0},{5,1},{8,10},{9,11},{10,... | collective-permute-start | bytes 589832 | tf_op jit(solution)/shard_map/ppermute | solution.py:143
  17.0 1.5 %collective-permute-start.3 = (f32[1,6144]{1,0:T(1,128)S(1)}, f32[1,6144]{1,0:T(1,128)S(1)}, u32[]{:S(2)}, u32[]{:S(2)}) collective-permute-start(f32[1,6144]{1,0:T(1,128)S(1)} %convert_element_type.92), channel_id=1, source_target_pairs={{0,8},{8,0},{16,24},{24,16},{1,9},{9,1},{17,25},{25,17},{2,10},{10... | collective-permute-start | bytes 73736 | tf_op jit(solution)/shard_map/ppermute | solution.py:70
  18.5 1.5 %constant_dynamic-slice_fusion.7 = (bf16[256,768]{1,0:T(8,128)(2,1)S(1)}, bf16[256,768]{1,0:T(8,128)(2,1)S(1)}, bf16[256,768]{1,0:T(8,128)(2,1)S(1)}, bf16[256,768]{1,0:T(8,128)(2,1)S(1)}) fusion(bf16[256,6144]{1,0:T(8,128)(2,1)} %param.11, s32[]{:T(128)S(6)} %select_n.71, s32[]{:T(128)S(6)} %select_n.74, s32[]{:T(128)S(6)} %select_n.81, s32[]{:T(128)S(6)} %select_n.78), kind=kLoop, calls=%fused_computation.129 | loop fusion | bytes 3145744 | tf_op jit(solution)/shard_map/dynamic_slice | solution.py:119
  20.9 3.4 %collective-permute-start.6 = (bf16[384,256]{1,0:T(8,128)(2,1)S(1)}, bf16[384,256]{1,0:T(8,128)(2,1)S(1)}, u32[]{:S(2)}, u32[]{:S(2)}) collective-permute-start(bf16[384,256]{1,0:T(8,128)(2,1)S(1)} %collective-permute-done.4), channel_id=1, source_target_pairs={{0,2},{1,3},{2,6},{3,7},{6,4},{7,5},{4,0},{5,1},{8,10},{9,11},{10,... | collective-permute-start | bytes 589832 | tf_op jit(solution)/shard_map/ppermute | solution.py:143
  25.8 1.5 %constant_dynamic-slice_fusion.6 = (bf16[256,768]{1,0:T(8,128)(2,1)S(1)}, bf16[256,768]{1,0:T(8,128)(2,1)S(1)}, bf16[256,768]{1,0:T(8,128)(2,1)S(1)}, bf16[256,768]{1,0:T(8,128)(2,1)S(1)}) fusion(bf16[256,6144]{1,0:T(8,128)(2,1)} %collective-permute-done, s32[]{:T(128)S(6)} %select_n.71, s32[]{:T(128)S(6)} %select_n.81, s32[]{:T(128)S(6)} %select_n.78, ...), kind=kLoop, calls=%fused_computation.128 | loop fusion | bytes 3145744 | tf_op jit(solution)/shard_map/dynamic_slice | solution.py:119
  30.2 2.4 %collective-permute-done.7 = bf16[384,256]{1,0:T(8,128)(2,1)S(1)} collective-permute-done((bf16[384,256]{1,0:T(8,128)(2,1)S(1)}, bf16[384,256]{1,0:T(8,128)(2,1)S(1)}, u32[]{:S(2)}, u32[]{:S(2)}) %collective-permute-start.7) | collective-permute-done | bytes 196640 | tf_op jit(solution)/shard_map/ppermute | solution.py:143
  33.1 1.6 %collective-permute-start.19 = (f32[1,6144]{1,0:T(1,128)S(1)}, f32[1,6144]{1,0:T(1,128)S(1)}, u32[]{:S(2)}, u32[]{:S(2)}) collective-permute-start(f32[1,6144]{1,0:T(1,128)S(1)} %add.166), channel_id=1, source_target_pairs={{0,16},{8,24},{16,0},{24,8},{1,17},{9,25},{17,1},{25,9},{2,18},{10... | collective-permute-start | bytes 73736 | tf_op jit(solution)/shard_map/ppermute | solution.py:70
  39.5 3.3 %collective-permute-start.13 = (bf16[256,256]{1,0:T(8,128)(2,1)S(1)}, bf16[256,256]{1,0:T(8,128)(2,1)S(1)}, u32[]{:S(2)}, u32[]{:S(2)}) collective-permute-start(bf16[256,256]{1,0:T(8,128)(2,1)S(1)} %convolution_convert_fusion.1), channel_id=1, source_target_pairs={{0,2},{1,3},{2,6},{3,7},{6,4},{7,5},{4,0},{5,1},{8,10},{9,11},{10,... | collective-permute-start | bytes 393224 | tf_op jit(solution)/shard_map/ppermute | solution.py:168
  43.8 1.5 %collective-permute-done.10 = bf16[256,256]{1,0:T(8,128)(2,1)S(1)} collective-permute-done((bf16[256,256]{1,0:T(8,128)(2,1)S(1)}, bf16[256,256]{1,0:T(8,128)(2,1)S(1)}, u32[]{:S(2)}, u32[]{:S(2)}) %collective-permute-start.10) | collective-permute-done | bytes 131104 | tf_op jit(solution)/shard_map/ppermute | solution.py:168
  46.5 1.4 %collective-permute-done.13 = bf16[256,256]{1,0:T(8,128)(2,1)S(1)} collective-permute-done((bf16[256,256]{1,0:T(8,128)(2,1)S(1)}, bf16[256,256]{1,0:T(8,128)(2,1)S(1)}, u32[]{:S(2)}, u32[]{:S(2)}) %collective-permute-start.13) | collective-permute-done | bytes 131104 | tf_op jit(solution)/shard_map/ppermute | solution.py:168
  48.1 2.1 %collective-permute-start.14 = (bf16[256,256]{1,0:T(8,128)(2,1)S(1)}, bf16[256,256]{1,0:T(8,128)(2,1)S(1)}, u32[]{:S(2)}, u32[]{:S(2)}) collective-permute-start(bf16[256,256]{1,0:T(8,128)(2,1)S(1)} %add_convert_fusion.3), channel_id=1, source_target_pairs={{0,2},{1,3},{2,6},{3,7},{6,4},{7,5},{4,0},{5,1},{8,10},{9,11},{10,... | collective-permute-start | bytes 393224 | tf_op jit(solution)/shard_map/ppermute | solution.py:168
  51.1 1.9 %collective-permute-start.17 = (bf16[256,256]{1,0:T(8,128)(2,1)S(1)}, bf16[256,256]{1,0:T(8,128)(2,1)S(1)}, u32[]{:S(2)}, u32[]{:S(2)}) collective-permute-start(bf16[256,256]{1,0:T(8,128)(2,1)S(1)} %add_convert_fusion.1), channel_id=1, source_target_pairs={{0,2},{1,3},{2,6},{3,7},{6,4},{7,5},{4,0},{5,1},{8,10},{9,11},{10,... | collective-permute-start | bytes 393224 | tf_op jit(solution)/shard_map/ppermute | solution.py:168
  53.9 1.9 %collective-permute-start.12 = (bf16[256,256]{1,0:T(8,128)(2,1)S(1)}, bf16[256,256]{1,0:T(8,128)(2,1)S(1)}, u32[]{:S(2)}, u32[]{:S(2)}) collective-permute-start(bf16[256,256]{1,0:T(8,128)(2,1)S(1)} %add_convert_fusion.4), channel_id=1, source_target_pairs={{0,2},{1,3},{2,6},{3,7},{6,4},{7,5},{4,0},{5,1},{8,10},{9,11},{10,... | collective-permute-start | bytes 393224 | tf_op jit(solution)/shard_map/ppermute | solution.py:172
  56.7 1.9 %collective-permute-start.15 = (bf16[256,256]{1,0:T(8,128)(2,1)S(1)}, bf16[256,256]{1,0:T(8,128)(2,1)S(1)}, u32[]{:S(2)}, u32[]{:S(2)}) collective-permute-start(bf16[256,256]{1,0:T(8,128)(2,1)S(1)} %add_convert_fusion.2), channel_id=1, source_target_pairs={{0,2},{1,3},{2,6},{3,7},{6,4},{7,5},{4,0},{5,1},{8,10},{9,11},{10,... | collective-permute-start | bytes 393224 | tf_op jit(solution)/shard_map/ppermute | solution.py:172
  59.5 1.9 %collective-permute-start.18 = (bf16[256,256]{1,0:T(8,128)(2,1)S(1)}, bf16[256,256]{1,0:T(8,128)(2,1)S(1)}, u32[]{:S(2)}, u32[]{:S(2)}) collective-permute-start(bf16[256,256]{1,0:T(8,128)(2,1)S(1)} %add_convert_fusion), channel_id=1, source_target_pairs={{0,2},{1,3},{2,6},{3,7},{6,4},{7,5},{4,0},{5,1},{8,10},{9,11},{10,... | collective-permute-start | bytes 393224 | tf_op jit(solution)/shard_map/ppermute | solution.py:172
  62.1 2.8 %collective-permute-done.15 = bf16[256,256]{1,0:T(8,128)(2,1)S(1)} collective-permute-done((bf16[256,256]{1,0:T(8,128)(2,1)S(1)}, bf16[256,256]{1,0:T(8,128)(2,1)S(1)}, u32[]{:S(2)}, u32[]{:S(2)}) %collective-permute-start.15) | collective-permute-done | bytes 131104 | tf_op jit(solution)/shard_map/ppermute | solution.py:172
  64.9 1.9 %collective-permute-done.18 = bf16[256,256]{1,0:T(8,128)(2,1)S(1)} collective-permute-done((bf16[256,256]{1,0:T(8,128)(2,1)S(1)}, bf16[256,256]{1,0:T(8,128)(2,1)S(1)}, u32[]{:S(2)}, u32[]{:S(2)}) %collective-permute-start.18) | collective-permute-done | bytes 131104 | tf_op jit(solution)/shard_map/ppermute | solution.py:172
  66.9 1.8 %multiply_subtract_fusion = (f32[768,256]{1,0:T(8,128)}, f32[768,256]{1,0:T(8,128)}, f32[768,256]{1,0:T(8,128)}) fusion(f32[768,256]{1,0:T(8,128)S(1)} %copy-done.1, f32[256,256]{1,0:T(8,128)S(1)} %convert_add_fusion, f32[256,256]{1,0:T(8,128)S(1)} %convert_add_fusion.1, f32[256,256]{1,0:T(8,128)S(1)} %convert_add_fusion.2, f32[768,256]{1,0:T(8,128)S(1)} %copy-done.2, ...), kind=kLoop, calls=%fused_computation.46 | loop fusion | flops 3342336 | bytes 5505024 | tf_op jit(solution)/shard_map/sub | solution.py:85
  (73 shorter events, 19.3 us)
Async XLA Ops:
  0.6 34.6 %copy-start = (bf16[256,128]{1,0:T(8,128)(2,1)S(1)}, bf16[256,128]{1,0:T(8,128)(2,1)}, u32[]{:S(2)}) copy-start(bf16[256,128]{1,0:T(8,128)(2,1)} %param.14) | copy-start | bytes 196612
  0.6 25.1 %collective-permute-start = (bf16[256,6144]{1,0:T(8,128)(2,1)}, bf16[256,6144]{1,0:T(8,128)(2,1)}, u32[]{:S(2)}, u32[]{:S(2)}) collective-permute-start(bf16[256,6144]{1,0:T(8,128)(2,1)} %param.11), channel_id=1, source_target_pairs={{0,1},{1,0},{2,3},{3,2},{4,5},{5,4},{6,7},{7,6},{8,9},{9,8},{10,11... | collective-permute-start | bytes 9437192 | tf_op jit(solution)/shard_map/ppermute | solution.py:125
  2.4 9.4 %collective-permute-start.1 = (bf16[384,256]{1,0:T(8,128)(2,1)S(1)}, bf16[384,256]{1,0:T(8,128)(2,1)S(1)}, u32[]{:S(2)}, u32[]{:S(2)}) collective-permute-start(bf16[384,256]{1,0:T(8,128)(2,1)S(1)} %get-tuple-element.37), channel_id=1, source_target_pairs={{0,2},{1,3},{2,6},{3,7},{6,4},{7,5},{4,0},{5,1},{8,10},{9,11},{10,... | collective-permute-start | bytes 589832 | tf_op jit(solution)/shard_map/ppermute | solution.py:124
  5.0 11.0 %collective-permute-start.2 = (bf16[384,256]{1,0:T(8,128)(2,1)S(1)}, bf16[384,256]{1,0:T(8,128)(2,1)S(1)}, u32[]{:S(2)}, u32[]{:S(2)}) collective-permute-start(bf16[384,256]{1,0:T(8,128)(2,1)S(1)} %get-tuple-element.36), channel_id=1, source_target_pairs={{0,2},{1,3},{2,6},{3,7},{6,4},{7,5},{4,0},{5,1},{8,10},{9,11},{10,... | collective-permute-start | bytes 589832 | tf_op jit(solution)/shard_map/ppermute | solution.py:124
  11.8 9.1 %collective-permute-start.4 = (bf16[384,256]{1,0:T(8,128)(2,1)S(1)}, bf16[384,256]{1,0:T(8,128)(2,1)S(1)}, u32[]{:S(2)}, u32[]{:S(2)}) collective-permute-start(bf16[384,256]{1,0:T(8,128)(2,1)S(1)} %collective-permute-done.1), channel_id=1, source_target_pairs={{0,2},{1,3},{2,6},{3,7},{6,4},{7,5},{4,0},{5,1},{8,10},{9,11},{10,... | collective-permute-start | bytes 589832 | tf_op jit(solution)/shard_map/ppermute | solution.py:143
  16.0 8.7 %collective-permute-start.5 = (bf16[384,256]{1,0:T(8,128)(2,1)S(1)}, bf16[384,256]{1,0:T(8,128)(2,1)S(1)}, u32[]{:S(2)}, u32[]{:S(2)}) collective-permute-start(bf16[384,256]{1,0:T(8,128)(2,1)S(1)} %collective-permute-done.2), channel_id=1, source_target_pairs={{0,2},{1,3},{2,6},{3,7},{6,4},{7,5},{4,0},{5,1},{8,10},{9,11},{10,... | collective-permute-start | bytes 589832 | tf_op jit(solution)/shard_map/ppermute | solution.py:143
  17.0 3.8 %collective-permute-start.3 = (f32[1,6144]{1,0:T(1,128)S(1)}, f32[1,6144]{1,0:T(1,128)S(1)}, u32[]{:S(2)}, u32[]{:S(2)}) collective-permute-start(f32[1,6144]{1,0:T(1,128)S(1)} %convert_element_type.92), channel_id=1, source_target_pairs={{0,8},{8,0},{16,24},{24,16},{1,9},{9,1},{17,25},{25,17},{2,10},{10... | collective-permute-start | bytes 73736 | tf_op jit(solution)/shard_map/ppermute | solution.py:70
  20.9 8.6 %collective-permute-start.6 = (bf16[384,256]{1,0:T(8,128)(2,1)S(1)}, bf16[384,256]{1,0:T(8,128)(2,1)S(1)}, u32[]{:S(2)}, u32[]{:S(2)}) collective-permute-start(bf16[384,256]{1,0:T(8,128)(2,1)S(1)} %collective-permute-done.4), channel_id=1, source_target_pairs={{0,2},{1,3},{2,6},{3,7},{6,4},{7,5},{4,0},{5,1},{8,10},{9,11},{10,... | collective-permute-start | bytes 589832 | tf_op jit(solution)/shard_map/ppermute | solution.py:143
  24.7 7.9 %collective-permute-start.7 = (bf16[384,256]{1,0:T(8,128)(2,1)S(1)}, bf16[384,256]{1,0:T(8,128)(2,1)S(1)}, u32[]{:S(2)}, u32[]{:S(2)}) collective-permute-start(bf16[384,256]{1,0:T(8,128)(2,1)S(1)} %collective-permute-done.5), channel_id=1, source_target_pairs={{0,2},{1,3},{2,6},{3,7},{6,4},{7,5},{4,0},{5,1},{8,10},{9,11},{10,... | collective-permute-start | bytes 589832 | tf_op jit(solution)/shard_map/ppermute | solution.py:143
  33.0 1.7 %collective-permute-start.8 = (f32[256,256]{0,1:T(8,128)S(1)}, f32[256,256]{0,1:T(8,128)S(1)}, u32[]{:S(2)}, u32[]{:S(2)}) collective-permute-start(f32[256,256]{0,1:T(8,128)S(1)} %slice.113), channel_id=1, source_target_pairs={{0,1},{1,0},{2,3},{3,2},{4,5},{5,4},{6,7},{7,6},{8,9},{9,8},{10,11... | collective-permute-start | bytes 786440 | tf_op jit(solution)/shard_map/ppermute | solution.py:151
  33.1 3.9 %collective-permute-start.19 = (f32[1,6144]{1,0:T(1,128)S(1)}, f32[1,6144]{1,0:T(1,128)S(1)}, u32[]{:S(2)}, u32[]{:S(2)}) collective-permute-start(f32[1,6144]{1,0:T(1,128)S(1)} %add.166), channel_id=1, source_target_pairs={{0,16},{8,24},{16,0},{24,8},{1,17},{9,25},{17,1},{25,9},{2,18},{10... | collective-permute-start | bytes 73736 | tf_op jit(solution)/shard_map/ppermute | solution.py:70
  36.1 1.6 %collective-permute-start.9 = (bf16[256,256]{0,1:T(8,128)(2,1)S(1)}, bf16[256,256]{0,1:T(8,128)(2,1)S(1)}, u32[]{:S(2)}, u32[]{:S(2)}) collective-permute-start(bf16[256,256]{0,1:T(8,128)(2,1)S(1)} %fusion.53), channel_id=1, source_target_pairs={{0,1},{1,0},{2,3},{3,2},{4,5},{5,4},{6,7},{7,6},{8,9},{9,8},{10,11... | collective-permute-start | bytes 393224 | tf_op jit(solution)/shard_map/ppermute | solution.py:153
  38.0 7.3 %collective-permute-start.10 = (bf16[256,256]{1,0:T(8,128)(2,1)S(1)}, bf16[256,256]{1,0:T(8,128)(2,1)S(1)}, u32[]{:S(2)}, u32[]{:S(2)}) collective-permute-start(bf16[256,256]{1,0:T(8,128)(2,1)S(1)} %convolution_convert_fusion.2), channel_id=1, source_target_pairs={{0,2},{1,3},{2,6},{3,7},{6,4},{7,5},{4,0},{5,1},{8,10},{9,11},{10,... | collective-permute-start | bytes 393224 | tf_op jit(solution)/shard_map/ppermute | solution.py:168
  39.5 8.3 %collective-permute-start.13 = (bf16[256,256]{1,0:T(8,128)(2,1)S(1)}, bf16[256,256]{1,0:T(8,128)(2,1)S(1)}, u32[]{:S(2)}, u32[]{:S(2)}) collective-permute-start(bf16[256,256]{1,0:T(8,128)(2,1)S(1)} %convolution_convert_fusion.1), channel_id=1, source_target_pairs={{0,2},{1,3},{2,6},{3,7},{6,4},{7,5},{4,0},{5,1},{8,10},{9,11},{10,... | collective-permute-start | bytes 393224 | tf_op jit(solution)/shard_map/ppermute | solution.py:168
  43.4 7.4 %collective-permute-start.16 = (bf16[256,256]{1,0:T(8,128)(2,1)S(1)}, bf16[256,256]{1,0:T(8,128)(2,1)S(1)}, u32[]{:S(2)}, u32[]{:S(2)}) collective-permute-start(bf16[256,256]{1,0:T(8,128)(2,1)S(1)} %convolution_convert_fusion), channel_id=1, source_target_pairs={{0,2},{1,3},{2,6},{3,7},{6,4},{7,5},{4,0},{5,1},{8,10},{9,11},{10,... | collective-permute-start | bytes 393224 | tf_op jit(solution)/shard_map/ppermute | solution.py:168
  45.6 8.1 %collective-permute-start.11 = (bf16[256,256]{1,0:T(8,128)(2,1)S(1)}, bf16[256,256]{1,0:T(8,128)(2,1)S(1)}, u32[]{:S(2)}, u32[]{:S(2)}) collective-permute-start(bf16[256,256]{1,0:T(8,128)(2,1)S(1)} %add_convert_fusion.5), channel_id=1, source_target_pairs={{0,2},{1,3},{2,6},{3,7},{6,4},{7,5},{4,0},{5,1},{8,10},{9,11},{10,... | collective-permute-start | bytes 393224 | tf_op jit(solution)/shard_map/ppermute | solution.py:168
  48.1 8.3 %collective-permute-start.14 = (bf16[256,256]{1,0:T(8,128)(2,1)S(1)}, bf16[256,256]{1,0:T(8,128)(2,1)S(1)}, u32[]{:S(2)}, u32[]{:S(2)}) collective-permute-start(bf16[256,256]{1,0:T(8,128)(2,1)S(1)} %add_convert_fusion.3), channel_id=1, source_target_pairs={{0,2},{1,3},{2,6},{3,7},{6,4},{7,5},{4,0},{5,1},{8,10},{9,11},{10,... | collective-permute-start | bytes 393224 | tf_op jit(solution)/shard_map/ppermute | solution.py:168
  51.1 15.7 %copy-start.1 = (f32[768,256]{1,0:T(8,128)S(1)}, f32[768,256]{1,0:T(8,128)}, u32[]{:S(2)}) copy-start(f32[768,256]{1,0:T(8,128)} %param.15) | copy-start | bytes 2359300
  51.1 15.7 %copy-start.2 = (f32[768,256]{1,0:T(8,128)S(1)}, f32[768,256]{1,0:T(8,128)}, u32[]{:S(2)}) copy-start(f32[768,256]{1,0:T(8,128)} %param.16) | copy-start | bytes 2359300
  51.1 15.7 %copy-start.3 = (f32[768,256]{1,0:T(8,128)S(1)}, f32[768,256]{1,0:T(8,128)}, u32[]{:S(2)}) copy-start(f32[768,256]{1,0:T(8,128)} %param.17) | copy-start | bytes 2359300
  51.1 8.1 %collective-permute-start.17 = (bf16[256,256]{1,0:T(8,128)(2,1)S(1)}, bf16[256,256]{1,0:T(8,128)(2,1)S(1)}, u32[]{:S(2)}, u32[]{:S(2)}) collective-permute-start(bf16[256,256]{1,0:T(8,128)(2,1)S(1)} %add_convert_fusion.1), channel_id=1, source_target_pairs={{0,2},{1,3},{2,6},{3,7},{6,4},{7,5},{4,0},{5,1},{8,10},{9,11},{10,... | collective-permute-start | bytes 393224 | tf_op jit(solution)/shard_map/ppermute | solution.py:168
  53.9 8.1 %collective-permute-start.12 = (bf16[256,256]{1,0:T(8,128)(2,1)S(1)}, bf16[256,256]{1,0:T(8,128)(2,1)S(1)}, u32[]{:S(2)}, u32[]{:S(2)}) collective-permute-start(bf16[256,256]{1,0:T(8,128)(2,1)S(1)} %add_convert_fusion.4), channel_id=1, source_target_pairs={{0,2},{1,3},{2,6},{3,7},{6,4},{7,5},{4,0},{5,1},{8,10},{9,11},{10,... | collective-permute-start | bytes 393224 | tf_op jit(solution)/shard_map/ppermute | solution.py:172
  56.7 8.1 %collective-permute-start.15 = (bf16[256,256]{1,0:T(8,128)(2,1)S(1)}, bf16[256,256]{1,0:T(8,128)(2,1)S(1)}, u32[]{:S(2)}, u32[]{:S(2)}) collective-permute-start(bf16[256,256]{1,0:T(8,128)(2,1)S(1)} %add_convert_fusion.2), channel_id=1, source_target_pairs={{0,2},{1,3},{2,6},{3,7},{6,4},{7,5},{4,0},{5,1},{8,10},{9,11},{10,... | collective-permute-start | bytes 393224 | tf_op jit(solution)/shard_map/ppermute | solution.py:172
  59.5 7.3 %collective-permute-start.18 = (bf16[256,256]{1,0:T(8,128)(2,1)S(1)}, bf16[256,256]{1,0:T(8,128)(2,1)S(1)}, u32[]{:S(2)}, u32[]{:S(2)}) collective-permute-start(bf16[256,256]{1,0:T(8,128)(2,1)S(1)} %add_convert_fusion), channel_id=1, source_target_pairs={{0,2},{1,3},{2,6},{3,7},{6,4},{7,5},{4,0},{5,1},{8,10},{9,11},{10,... | collective-permute-start | bytes 393224 | tf_op jit(solution)/shard_map/ppermute | solution.py:172
  (2 other events, 10.4 us)

commit v6 on v5

--- a/solution.py
+++ b/solution.py
@@ -94,13 +94,12 @@
 
 
 def spot_of(chip, chips):
-    back = jnp.where(chip == 0, 0, chips - lax.div(chip, 2))
-    return jnp.where(lax.rem(chip, 2) == 1, lax.div(chip + 1, 2), back)
+    back = chips - lax.div(chip + 1, 2)
+    return jnp.where(lax.rem(chip, 2) == 0, lax.div(chip, 2), back)
 
 
 def chip_at(spot, chips):
-    out = jnp.where(spot == 0, 0, 2 * spot - 1)
-    return jnp.where(2 * spot <= chips, out, 2 * (chips - spot))
+    return jnp.where(2 * spot < chips, 2 * spot, 2 * (chips - spot) - 1)
 
 
 def inner_step(inputs, doc_ids, values, cotangent, weights, moment1, moment2, outer):
@@ -108,7 +107,7 @@
     chips = devices // 2
     here = lax.axis_index("shard")
     rows = weights.shape[0]
-    line = [0] + [i for i in range(chips) if i % 2 == 1] + [i for i in range(chips - 1, 1, -1) if i % 2 == 0]
+    line = list(range(0, chips, 2)) + list(range(chips - 1 - chips % 2, 0, -2))
     ring = [(2 * line[i] + c, 2 * line[(i + 1) % chips] + c) for i in range(chips) for c in range(2)]
     core = lax.rem(here, 2)
     spot = spot_of(lax.div(here, 2), chips)

time: 69 us -> 68.2 us (0.988)
  waiting for transfers between devices: 20.7 us -> 9.71 us
  starting transfers between devices: 30.7 us -> 40.9 us
    ppermute x6, waiting for transfers between devices: 5.32 us -> 0.46 us  [inner_step(): came = lax.ppermute(sums[j], 'shard', ring)]
    ppermute x6, waiting for transfers between devices: 8.54 us -> 4.01 us  [inner_step(): flying = [lax.ppermute(block, 'shard', ring) for block in blocks]]
    ppermute x6, starting transfers between devices: 11.8 us -> 16.1 us  [inner_step(): flying = [lax.ppermute(block, 'shard', ring) for block in blocks]]
    ppermute x6, starting transfers between devices: 9.25 us -> 13.4 us  [inner_step(): came = lax.ppermute(sums[j], 'shard', ring)]
    ppermute x3, starting transfers between devices: 5.73 us -> 7.53 us  [inner_step(): sums[j] = lax.ppermute(sums[j], 'shard', ring).astype(jnp.float32) + own]
    ppermute x3, waiting for transfers between devices: 5.3 us -> 3.64 us  [inner_step(): sums[j] = lax.ppermute(sums[j], 'shard', ring).astype(jnp.float32) + own]
  transfers between devices with their start and end apart: 20 -> 20, of which waited for: 16 -> 9; matrix products, arithmetic and copies ran while one was open for 19% -> 19% of each run, Pallas kernels for 0% -> 0%
where the time goes in v6:
time: 68.2 us; the launch traced here: 67.9 us
  starting transfers between devices  40.9 us (60%)
  waiting for transfers between devices  9.71 us (14%)
  matrix products  6.92 us (10%)
  other arithmetic  4.92 us (7%)
  local copies, waits for them, and re-layouts  3.77 us (6%)
  between operations  1.67 us (2%)
    ppermute x6, starting transfers between devices, inner_step(): flying = [lax.ppermute(block, 'shard', ring) for block in blocks]  16.1 us
    ppermute x6, starting transfers between devices, inner_step(): came = lax.ppermute(sums[j], 'shard', ring)  13.4 us
    ppermute x3, starting transfers between devices, inner_step(): sums[j] = lax.ppermute(sums[j], 'shard', ring).astype(jnp.float32) + own  7.53 us
    ppermute x6, waiting for transfers between devices, inner_step(): flying = [lax.ppermute(block, 'shard', ring) for block in blocks]  4.01 us
    ppermute x3, waiting for transfers between devices, inner_step(): sums[j] = lax.ppermute(sums[j], 'shard', ring).astype(jnp.float32) + own  3.64 us
    dot_general x12, matrix products, term(): lax.dot_general(both[k][:, cuts[j]], grad_both, (((0,), (0,)), ((), ())),...  3.29 us
    ppermute x2, starting transfers between devices, exchange(): lax.ppermute(total, 'replica', [(i, i ^ step) for i in range(replicas)])  3.05 us
    dynamic_slice x2, local copies, waits for them, and re-layouts, ordered(): lax.dynamic_slice_in_dim(tokens, (2 * chip + core) * rows, rows, axis=1)  2.92 us
  transfers between devices with their start and end apart: 20, of which 9 were waited for; matrix products, arithmetic and copies ran while one was open for 19% of the time, Pallas kernels for 0%

profile of v6, /device:TPU:0, one launch (start us, length us, event | category | flops | bytes accessed | tf_op | source)
XLA Modules:
  0.0 67.9 jit_solution(14564893225801579218)
XLA Ops:
  1.2 1.2 %convert_element_type.88 = bf16[768,256]{1,0:T(8,128)(2,1)S(1)} convert(f32[768,256]{1,0:T(8,128)} %param.15) | non-fusion elementwise | flops 196608 | bytes 1179648 | tf_op jit(solution)/shard_map/convert_element_type | solution.py:121
  2.4 3.7 %collective-permute-start.1 = (bf16[384,256]{1,0:T(8,128)(2,1)S(1)}, bf16[384,256]{1,0:T(8,128)(2,1)S(1)}, u32[]{:S(2)}, u32[]{:S(2)}) collective-permute-start(bf16[384,256]{1,0:T(8,128)(2,1)S(1)} %get-tuple-element.37), channel_id=1, source_target_pairs={{0,4},{1,5},{4,6},{5,7},{6,2},{7,3},{2,0},{3,1},{8,12},{9,13},{12,... | collective-permute-start | bytes 589832 | tf_op jit(solution)/shard_map/ppermute | solution.py:123
  6.0 1.6 %collective-permute-start.2 = (bf16[384,256]{1,0:T(8,128)(2,1)S(1)}, bf16[384,256]{1,0:T(8,128)(2,1)S(1)}, u32[]{:S(2)}, u32[]{:S(2)}) collective-permute-start(bf16[384,256]{1,0:T(8,128)(2,1)S(1)} %get-tuple-element.36), channel_id=1, source_target_pairs={{0,4},{1,5},{4,6},{5,7},{6,2},{7,3},{2,0},{3,1},{8,12},{9,13},{12,... | collective-permute-start | bytes 589832 | tf_op jit(solution)/shard_map/ppermute | solution.py:123
  9.0 0.9 %fusion.61 = bf16[1,6144]{1,0:T(2,128)(2,1)S(1)} fusion(bf16[1,16,1,6144]{3,1,2,0:T(8,128)(2,1)} %param.18, s32[]{:T(128)S(6)} %select_n.52, f32[16,1,6144]{2,1,0:T(1,128)} %param.19), kind=kLoop, calls=%fused_computation.116 | loop fusion | flops 18432 | bytes 49156 | tf_op jit(solution)/shard_map/convert_element_type | solution.py:61
  10.0 1.3 %collective-permute-done.1 = bf16[384,256]{1,0:T(8,128)(2,1)S(1)} collective-permute-done((bf16[384,256]{1,0:T(8,128)(2,1)S(1)}, bf16[384,256]{1,0:T(8,128)(2,1)S(1)}, u32[]{:S(2)}, u32[]{:S(2)}) %collective-permute-start.1) | collective-permute-done | bytes 196640 | tf_op jit(solution)/shard_map/ppermute | solution.py:123
  11.2 3.4 %collective-permute-start.4 = (bf16[384,256]{1,0:T(8,128)(2,1)S(1)}, bf16[384,256]{1,0:T(8,128)(2,1)S(1)}, u32[]{:S(2)}, u32[]{:S(2)}) collective-permute-start(bf16[384,256]{1,0:T(8,128)(2,1)S(1)} %collective-permute-done.1), channel_id=1, source_target_pairs={{0,4},{1,5},{4,6},{5,7},{6,2},{7,3},{2,0},{3,1},{8,12},{9,13},{12,... | collective-permute-start | bytes 589832 | tf_op jit(solution)/shard_map/ppermute | solution.py:142
  15.5 3.4 %collective-permute-start.5 = (bf16[384,256]{1,0:T(8,128)(2,1)S(1)}, bf16[384,256]{1,0:T(8,128)(2,1)S(1)}, u32[]{:S(2)}, u32[]{:S(2)}) collective-permute-start(bf16[384,256]{1,0:T(8,128)(2,1)S(1)} %collective-permute-done.2), channel_id=1, source_target_pairs={{0,4},{1,5},{4,6},{5,7},{6,2},{7,3},{2,0},{3,1},{8,12},{9,13},{12,... | collective-permute-start | bytes 589832 | tf_op jit(solution)/shard_map/ppermute | solution.py:142
  18.8 1.5 %collective-permute-start.3 = (f32[1,6144]{1,0:T(1,128)S(1)}, f32[1,6144]{1,0:T(1,128)S(1)}, u32[]{:S(2)}, u32[]{:S(2)}) collective-permute-start(f32[1,6144]{1,0:T(1,128)S(1)} %convert_element_type.92), channel_id=1, source_target_pairs={{0,8},{8,0},{16,24},{24,16},{1,9},{9,1},{17,25},{25,17},{2,10},{10... | collective-permute-start | bytes 73736 | tf_op jit(solution)/shard_map/ppermute | solution.py:70
  20.3 1.5 %constant_dynamic-slice_fusion.7 = (bf16[256,768]{1,0:T(8,128)(2,1)S(1)}, bf16[256,768]{1,0:T(8,128)(2,1)S(1)}, bf16[256,768]{1,0:T(8,128)(2,1)S(1)}, bf16[256,768]{1,0:T(8,128)(2,1)S(1)}) fusion(bf16[256,6144]{1,0:T(8,128)(2,1)} %param.11, s32[]{:T(128)S(6)} %select_n.49, s32[]{:T(128)S(6)} %select_n.51, s32[]{:T(128)S(6)} %select_n.56, s32[]{:T(128)S(6)} %select_n.54), kind=kLoop, calls=%fused_computation.129 | loop fusion | bytes 3145744 | tf_op jit(solution)/shard_map/dynamic_slice | solution.py:118
  24.2 3.4 %collective-permute-start.7 = (bf16[384,256]{1,0:T(8,128)(2,1)S(1)}, bf16[384,256]{1,0:T(8,128)(2,1)S(1)}, u32[]{:S(2)}, u32[]{:S(2)}) collective-permute-start(bf16[384,256]{1,0:T(8,128)(2,1)S(1)} %collective-permute-done.5), channel_id=1, source_target_pairs={{0,4},{1,5},{4,6},{5,7},{6,2},{7,3},{2,0},{3,1},{8,12},{9,13},{12,... | collective-permute-start | bytes 589832 | tf_op jit(solution)/shard_map/ppermute | solution.py:142
  27.6 1.5 %constant_dynamic-slice_fusion.6 = (bf16[256,768]{1,0:T(8,128)(2,1)S(1)}, bf16[256,768]{1,0:T(8,128)(2,1)S(1)}, bf16[256,768]{1,0:T(8,128)(2,1)S(1)}, bf16[256,768]{1,0:T(8,128)(2,1)S(1)}) fusion(bf16[256,6144]{1,0:T(8,128)(2,1)} %collective-permute-done, s32[]{:T(128)S(6)} %select_n.49, s32[]{:T(128)S(6)} %select_n.56, s32[]{:T(128)S(6)} %select_n.54, ...), kind=kLoop, calls=%fused_computation.128 | loop fusion | bytes 3145744 | tf_op jit(solution)/shard_map/dynamic_slice | solution.py:118
  31.3 1.2 %collective-permute-done.7 = bf16[384,256]{1,0:T(8,128)(2,1)S(1)} collective-permute-done((bf16[384,256]{1,0:T(8,128)(2,1)S(1)}, bf16[384,256]{1,0:T(8,128)(2,1)S(1)}, u32[]{:S(2)}, u32[]{:S(2)}) %collective-permute-start.7) | collective-permute-done | bytes 196640 | tf_op jit(solution)/shard_map/ppermute | solution.py:142
  32.9 1.6 %collective-permute-start.19 = (f32[1,6144]{1,0:T(1,128)S(1)}, f32[1,6144]{1,0:T(1,128)S(1)}, u32[]{:S(2)}, u32[]{:S(2)}) collective-permute-start(f32[1,6144]{1,0:T(1,128)S(1)} %add.166), channel_id=1, source_target_pairs={{0,16},{8,24},{16,0},{24,8},{1,17},{9,25},{17,1},{25,9},{2,18},{10... | collective-permute-start | bytes 73736 | tf_op jit(solution)/shard_map/ppermute | solution.py:70
  37.8 2.9 %collective-permute-start.10 = (bf16[256,256]{1,0:T(8,128)(2,1)S(1)}, bf16[256,256]{1,0:T(8,128)(2,1)S(1)}, u32[]{:S(2)}, u32[]{:S(2)}) collective-permute-start(bf16[256,256]{1,0:T(8,128)(2,1)S(1)} %convolution_convert_fusion.2), channel_id=1, source_target_pairs={{0,4},{1,5},{4,6},{5,7},{6,2},{7,3},{2,0},{3,1},{8,12},{9,13},{12,... | collective-permute-start | bytes 393224 | tf_op jit(solution)/shard_map/ppermute | solution.py:167
  42.5 1.3 %collective-permute-start.16 = (bf16[256,256]{1,0:T(8,128)(2,1)S(1)}, bf16[256,256]{1,0:T(8,128)(2,1)S(1)}, u32[]{:S(2)}, u32[]{:S(2)}) collective-permute-start(bf16[256,256]{1,0:T(8,128)(2,1)S(1)} %convolution_convert_fusion), channel_id=1, source_target_pairs={{0,4},{1,5},{4,6},{5,7},{6,2},{7,3},{2,0},{3,1},{8,12},{9,13},{12,... | collective-permute-start | bytes 393224 | tf_op jit(solution)/shard_map/ppermute | solution.py:167
  44.8 3.4 %collective-permute-start.11 = (bf16[256,256]{1,0:T(8,128)(2,1)S(1)}, bf16[256,256]{1,0:T(8,128)(2,1)S(1)}, u32[]{:S(2)}, u32[]{:S(2)}) collective-permute-start(bf16[256,256]{1,0:T(8,128)(2,1)S(1)} %add_convert_fusion.5), channel_id=1, source_target_pairs={{0,4},{1,5},{4,6},{5,7},{6,2},{7,3},{2,0},{3,1},{8,12},{9,13},{12,... | collective-permute-start | bytes 393224 | tf_op jit(solution)/shard_map/ppermute | solution.py:167
  48.6 2.5 %collective-permute-start.14 = (bf16[256,256]{1,0:T(8,128)(2,1)S(1)}, bf16[256,256]{1,0:T(8,128)(2,1)S(1)}, u32[]{:S(2)}, u32[]{:S(2)}) collective-permute-start(bf16[256,256]{1,0:T(8,128)(2,1)S(1)} %add_convert_fusion.3), channel_id=1, source_target_pairs={{0,4},{1,5},{4,6},{5,7},{6,2},{7,3},{2,0},{3,1},{8,12},{9,13},{12,... | collective-permute-start | bytes 393224 | tf_op jit(solution)/shard_map/ppermute | solution.py:167
  51.4 2.5 %collective-permute-start.17 = (bf16[256,256]{1,0:T(8,128)(2,1)S(1)}, bf16[256,256]{1,0:T(8,128)(2,1)S(1)}, u32[]{:S(2)}, u32[]{:S(2)}) collective-permute-start(bf16[256,256]{1,0:T(8,128)(2,1)S(1)} %add_convert_fusion.1), channel_id=1, source_target_pairs={{0,4},{1,5},{4,6},{5,7},{6,2},{7,3},{2,0},{3,1},{8,12},{9,13},{12,... | collective-permute-start | bytes 393224 | tf_op jit(solution)/shard_map/ppermute | solution.py:167
  54.2 2.5 %collective-permute-start.12 = (bf16[256,256]{1,0:T(8,128)(2,1)S(1)}, bf16[256,256]{1,0:T(8,128)(2,1)S(1)}, u32[]{:S(2)}, u32[]{:S(2)}) collective-permute-start(bf16[256,256]{1,0:T(8,128)(2,1)S(1)} %add_convert_fusion.4), channel_id=1, source_target_pairs={{0,4},{1,5},{4,6},{5,7},{6,2},{7,3},{2,0},{3,1},{8,12},{9,13},{12,... | collective-permute-start | bytes 393224 | tf_op jit(solution)/shard_map/ppermute | solution.py:171
  57.0 2.5 %collective-permute-start.15 = (bf16[256,256]{1,0:T(8,128)(2,1)S(1)}, bf16[256,256]{1,0:T(8,128)(2,1)S(1)}, u32[]{:S(2)}, u32[]{:S(2)}) collective-permute-start(bf16[256,256]{1,0:T(8,128)(2,1)S(1)} %add_convert_fusion.2), channel_id=1, source_target_pairs={{0,4},{1,5},{4,6},{5,7},{6,2},{7,3},{2,0},{3,1},{8,12},{9,13},{12,... | collective-permute-start | bytes 393224 | tf_op jit(solution)/shard_map/ppermute | solution.py:171
  59.8 2.5 %collective-permute-start.18 = (bf16[256,256]{1,0:T(8,128)(2,1)S(1)}, bf16[256,256]{1,0:T(8,128)(2,1)S(1)}, u32[]{:S(2)}, u32[]{:S(2)}) collective-permute-start(bf16[256,256]{1,0:T(8,128)(2,1)S(1)} %add_convert_fusion), channel_id=1, source_target_pairs={{0,4},{1,5},{4,6},{5,7},{6,2},{7,3},{2,0},{3,1},{8,12},{9,13},{12,... | collective-permute-start | bytes 393224 | tf_op jit(solution)/shard_map/ppermute | solution.py:171
  62.4 2.2 %collective-permute-done.15 = bf16[256,256]{1,0:T(8,128)(2,1)S(1)} collective-permute-done((bf16[256,256]{1,0:T(8,128)(2,1)S(1)}, bf16[256,256]{1,0:T(8,128)(2,1)S(1)}, u32[]{:S(2)}, u32[]{:S(2)}) %collective-permute-start.15) | collective-permute-done | bytes 131104 | tf_op jit(solution)/shard_map/ppermute | solution.py:171
  64.6 1.4 %collective-permute-done.18 = bf16[256,256]{1,0:T(8,128)(2,1)S(1)} collective-permute-done((bf16[256,256]{1,0:T(8,128)(2,1)S(1)}, bf16[256,256]{1,0:T(8,128)(2,1)S(1)}, u32[]{:S(2)}, u32[]{:S(2)}) %collective-permute-start.18) | collective-permute-done | bytes 131104 | tf_op jit(solution)/shard_map/ppermute | solution.py:171
  66.1 1.8 %multiply_subtract_fusion = (f32[768,256]{1,0:T(8,128)}, f32[768,256]{1,0:T(8,128)}, f32[768,256]{1,0:T(8,128)}) fusion(f32[768,256]{1,0:T(8,128)S(1)} %copy-done.1, f32[256,256]{1,0:T(8,128)S(1)} %convert_add_fusion, f32[256,256]{1,0:T(8,128)S(1)} %convert_add_fusion.1, f32[256,256]{1,0:T(8,128)S(1)} %convert_add_fusion.2, f32[768,256]{1,0:T(8,128)S(1)} %copy-done.2, ...), kind=kLoop, calls=%fused_computation.46 | loop fusion | flops 3342336 | bytes 5505024 | tf_op jit(solution)/shard_map/sub | solution.py:85
  (73 shorter events, 14.7 us)
Async XLA Ops:
  0.6 34.3 %copy-start = (bf16[256,128]{1,0:T(8,128)(2,1)S(1)}, bf16[256,128]{1,0:T(8,128)(2,1)}, u32[]{:S(2)}) copy-start(bf16[256,128]{1,0:T(8,128)(2,1)} %param.14) | copy-start | bytes 196612
  0.6 26.9 %collective-permute-start = (bf16[256,6144]{1,0:T(8,128)(2,1)}, bf16[256,6144]{1,0:T(8,128)(2,1)}, u32[]{:S(2)}, u32[]{:S(2)}) collective-permute-start(bf16[256,6144]{1,0:T(8,128)(2,1)} %param.11), channel_id=1, source_target_pairs={{0,1},{1,0},{2,3},{3,2},{4,5},{5,4},{6,7},{7,6},{8,9},{9,8},{10,11... | collective-permute-start | bytes 9437192 | tf_op jit(solution)/shard_map/ppermute | solution.py:124
  2.4 8.9 %collective-permute-start.1 = (bf16[384,256]{1,0:T(8,128)(2,1)S(1)}, bf16[384,256]{1,0:T(8,128)(2,1)S(1)}, u32[]{:S(2)}, u32[]{:S(2)}) collective-permute-start(bf16[384,256]{1,0:T(8,128)(2,1)S(1)} %get-tuple-element.37), channel_id=1, source_target_pairs={{0,4},{1,5},{4,6},{5,7},{6,2},{7,3},{2,0},{3,1},{8,12},{9,13},{12,... | collective-permute-start | bytes 589832 | tf_op jit(solution)/shard_map/ppermute | solution.py:123
  6.0 9.4 %collective-permute-start.2 = (bf16[384,256]{1,0:T(8,128)(2,1)S(1)}, bf16[384,256]{1,0:T(8,128)(2,1)S(1)}, u32[]{:S(2)}, u32[]{:S(2)}) collective-permute-start(bf16[384,256]{1,0:T(8,128)(2,1)S(1)} %get-tuple-element.36), channel_id=1, source_target_pairs={{0,4},{1,5},{4,6},{5,7},{6,2},{7,3},{2,0},{3,1},{8,12},{9,13},{12,... | collective-permute-start | bytes 589832 | tf_op jit(solution)/shard_map/ppermute | solution.py:123
  11.2 11.5 %collective-permute-start.4 = (bf16[384,256]{1,0:T(8,128)(2,1)S(1)}, bf16[384,256]{1,0:T(8,128)(2,1)S(1)}, u32[]{:S(2)}, u32[]{:S(2)}) collective-permute-start(bf16[384,256]{1,0:T(8,128)(2,1)S(1)} %collective-permute-done.1), channel_id=1, source_target_pairs={{0,4},{1,5},{4,6},{5,7},{6,2},{7,3},{2,0},{3,1},{8,12},{9,13},{12,... | collective-permute-start | bytes 589832 | tf_op jit(solution)/shard_map/ppermute | solution.py:142
  15.5 8.7 %collective-permute-start.5 = (bf16[384,256]{1,0:T(8,128)(2,1)S(1)}, bf16[384,256]{1,0:T(8,128)(2,1)S(1)}, u32[]{:S(2)}, u32[]{:S(2)}) collective-permute-start(bf16[384,256]{1,0:T(8,128)(2,1)S(1)} %collective-permute-done.2), channel_id=1, source_target_pairs={{0,4},{1,5},{4,6},{5,7},{6,2},{7,3},{2,0},{3,1},{8,12},{9,13},{12,... | collective-permute-start | bytes 589832 | tf_op jit(solution)/shard_map/ppermute | solution.py:142
  18.8 3.8 %collective-permute-start.3 = (f32[1,6144]{1,0:T(1,128)S(1)}, f32[1,6144]{1,0:T(1,128)S(1)}, u32[]{:S(2)}, u32[]{:S(2)}) collective-permute-start(f32[1,6144]{1,0:T(1,128)S(1)} %convert_element_type.92), channel_id=1, source_target_pairs={{0,8},{8,0},{16,24},{24,16},{1,9},{9,1},{17,25},{25,17},{2,10},{10... | collective-permute-start | bytes 73736 | tf_op jit(solution)/shard_map/ppermute | solution.py:70
  22.7 7.8 %collective-permute-start.6 = (bf16[384,256]{1,0:T(8,128)(2,1)S(1)}, bf16[384,256]{1,0:T(8,128)(2,1)S(1)}, u32[]{:S(2)}, u32[]{:S(2)}) collective-permute-start(bf16[384,256]{1,0:T(8,128)(2,1)S(1)} %collective-permute-done.4), channel_id=1, source_target_pairs={{0,4},{1,5},{4,6},{5,7},{6,2},{7,3},{2,0},{3,1},{8,12},{9,13},{12,... | collective-permute-start | bytes 589832 | tf_op jit(solution)/shard_map/ppermute | solution.py:142
  24.2 8.3 %collective-permute-start.7 = (bf16[384,256]{1,0:T(8,128)(2,1)S(1)}, bf16[384,256]{1,0:T(8,128)(2,1)S(1)}, u32[]{:S(2)}, u32[]{:S(2)}) collective-permute-start(bf16[384,256]{1,0:T(8,128)(2,1)S(1)} %collective-permute-done.5), channel_id=1, source_target_pairs={{0,4},{1,5},{4,6},{5,7},{6,2},{7,3},{2,0},{3,1},{8,12},{9,13},{12,... | collective-permute-start | bytes 589832 | tf_op jit(solution)/shard_map/ppermute | solution.py:142
  32.8 1.6 %collective-permute-start.8 = (f32[256,256]{0,1:T(8,128)S(1)}, f32[256,256]{0,1:T(8,128)S(1)}, u32[]{:S(2)}, u32[]{:S(2)}) collective-permute-start(f32[256,256]{0,1:T(8,128)S(1)} %slice.113), channel_id=1, source_target_pairs={{0,1},{1,0},{2,3},{3,2},{4,5},{5,4},{6,7},{7,6},{8,9},{9,8},{10,11... | collective-permute-start | bytes 786440 | tf_op jit(solution)/shard_map/ppermute | solution.py:150
  32.9 3.9 %collective-permute-start.19 = (f32[1,6144]{1,0:T(1,128)S(1)}, f32[1,6144]{1,0:T(1,128)S(1)}, u32[]{:S(2)}, u32[]{:S(2)}) collective-permute-start(f32[1,6144]{1,0:T(1,128)S(1)} %add.166), channel_id=1, source_target_pairs={{0,16},{8,24},{16,0},{24,8},{1,17},{9,25},{17,1},{25,9},{2,18},{10... | collective-permute-start | bytes 73736 | tf_op jit(solution)/shard_map/ppermute | solution.py:70
  35.9 1.7 %collective-permute-start.9 = (bf16[256,256]{0,1:T(8,128)(2,1)S(1)}, bf16[256,256]{0,1:T(8,128)(2,1)S(1)}, u32[]{:S(2)}, u32[]{:S(2)}) collective-permute-start(bf16[256,256]{0,1:T(8,128)(2,1)S(1)} %fusion.53), channel_id=1, source_target_pairs={{0,1},{1,0},{2,3},{3,2},{4,5},{5,4},{6,7},{7,6},{8,9},{9,8},{10,11... | collective-permute-start | bytes 393224 | tf_op jit(solution)/shard_map/ppermute | solution.py:152
  37.8 6.8 %collective-permute-start.10 = (bf16[256,256]{1,0:T(8,128)(2,1)S(1)}, bf16[256,256]{1,0:T(8,128)(2,1)S(1)}, u32[]{:S(2)}, u32[]{:S(2)}) collective-permute-start(bf16[256,256]{1,0:T(8,128)(2,1)S(1)} %convolution_convert_fusion.2), channel_id=1, source_target_pairs={{0,4},{1,5},{4,6},{5,7},{6,2},{7,3},{2,0},{3,1},{8,12},{9,13},{12,... | collective-permute-start | bytes 393224 | tf_op jit(solution)/shard_map/ppermute | solution.py:167
  41.2 7.0 %collective-permute-start.13 = (bf16[256,256]{1,0:T(8,128)(2,1)S(1)}, bf16[256,256]{1,0:T(8,128)(2,1)S(1)}, u32[]{:S(2)}, u32[]{:S(2)}) collective-permute-start(bf16[256,256]{1,0:T(8,128)(2,1)S(1)} %convolution_convert_fusion.1), channel_id=1, source_target_pairs={{0,4},{1,5},{4,6},{5,7},{6,2},{7,3},{2,0},{3,1},{8,12},{9,13},{12,... | collective-permute-start | bytes 393224 | tf_op jit(solution)/shard_map/ppermute | solution.py:167
  42.5 8.6 %collective-permute-start.16 = (bf16[256,256]{1,0:T(8,128)(2,1)S(1)}, bf16[256,256]{1,0:T(8,128)(2,1)S(1)}, u32[]{:S(2)}, u32[]{:S(2)}) collective-permute-start(bf16[256,256]{1,0:T(8,128)(2,1)S(1)} %convolution_convert_fusion), channel_id=1, source_target_pairs={{0,4},{1,5},{4,6},{5,7},{6,2},{7,3},{2,0},{3,1},{8,12},{9,13},{12,... | collective-permute-start | bytes 393224 | tf_op jit(solution)/shard_map/ppermute | solution.py:167
  44.8 9.1 %collective-permute-start.11 = (bf16[256,256]{1,0:T(8,128)(2,1)S(1)}, bf16[256,256]{1,0:T(8,128)(2,1)S(1)}, u32[]{:S(2)}, u32[]{:S(2)}) collective-permute-start(bf16[256,256]{1,0:T(8,128)(2,1)S(1)} %add_convert_fusion.5), channel_id=1, source_target_pairs={{0,4},{1,5},{4,6},{5,7},{6,2},{7,3},{2,0},{3,1},{8,12},{9,13},{12,... | collective-permute-start | bytes 393224 | tf_op jit(solution)/shard_map/ppermute | solution.py:167
  48.6 8.1 %collective-permute-start.14 = (bf16[256,256]{1,0:T(8,128)(2,1)S(1)}, bf16[256,256]{1,0:T(8,128)(2,1)S(1)}, u32[]{:S(2)}, u32[]{:S(2)}) collective-permute-start(bf16[256,256]{1,0:T(8,128)(2,1)S(1)} %add_convert_fusion.3), channel_id=1, source_target_pairs={{0,4},{1,5},{4,6},{5,7},{6,2},{7,3},{2,0},{3,1},{8,12},{9,13},{12,... | collective-permute-start | bytes 393224 | tf_op jit(solution)/shard_map/ppermute | solution.py:167
  51.4 14.7 %copy-start.1 = (f32[768,256]{1,0:T(8,128)S(1)}, f32[768,256]{1,0:T(8,128)}, u32[]{:S(2)}) copy-start(f32[768,256]{1,0:T(8,128)} %param.15) | copy-start | bytes 2359300
  51.4 14.7 %copy-start.2 = (f32[768,256]{1,0:T(8,128)S(1)}, f32[768,256]{1,0:T(8,128)}, u32[]{:S(2)}) copy-start(f32[768,256]{1,0:T(8,128)} %param.16) | copy-start | bytes 2359300
  51.4 14.7 %copy-start.3 = (f32[768,256]{1,0:T(8,128)S(1)}, f32[768,256]{1,0:T(8,128)}, u32[]{:S(2)}) copy-start(f32[768,256]{1,0:T(8,128)} %param.17) | copy-start | bytes 2359300
  51.4 8.1 %collective-permute-start.17 = (bf16[256,256]{1,0:T(8,128)(2,1)S(1)}, bf16[256,256]{1,0:T(8,128)(2,1)S(1)}, u32[]{:S(2)}, u32[]{:S(2)}) collective-permute-start(bf16[256,256]{1,0:T(8,128)(2,1)S(1)} %add_convert_fusion.1), channel_id=1, source_target_pairs={{0,4},{1,5},{4,6},{5,7},{6,2},{7,3},{2,0},{3,1},{8,12},{9,13},{12,... | collective-permute-start | bytes 393224 | tf_op jit(solution)/shard_map/ppermute | solution.py:167
  54.2 8.1 %collective-permute-start.12 = (bf16[256,256]{1,0:T(8,128)(2,1)S(1)}, bf16[256,256]{1,0:T(8,128)(2,1)S(1)}, u32[]{:S(2)}, u32[]{:S(2)}) collective-permute-start(bf16[256,256]{1,0:T(8,128)(2,1)S(1)} %add_convert_fusion.4), channel_id=1, source_target_pairs={{0,4},{1,5},{4,6},{5,7},{6,2},{7,3},{2,0},{3,1},{8,12},{9,13},{12,... | collective-permute-start | bytes 393224 | tf_op jit(solution)/shard_map/ppermute | solution.py:171
  57.0 7.6 %collective-permute-start.15 = (bf16[256,256]{1,0:T(8,128)(2,1)S(1)}, bf16[256,256]{1,0:T(8,128)(2,1)S(1)}, u32[]{:S(2)}, u32[]{:S(2)}) collective-permute-start(bf16[256,256]{1,0:T(8,128)(2,1)S(1)} %add_convert_fusion.2), channel_id=1, source_target_pairs={{0,4},{1,5},{4,6},{5,7},{6,2},{7,3},{2,0},{3,1},{8,12},{9,13},{12,... | collective-permute-start | bytes 393224 | tf_op jit(solution)/shard_map/ppermute | solution.py:171
  59.8 6.2 %collective-permute-start.18 = (bf16[256,256]{1,0:T(8,128)(2,1)S(1)}, bf16[256,256]{1,0:T(8,128)(2,1)S(1)}, u32[]{:S(2)}, u32[]{:S(2)}) collective-permute-start(bf16[256,256]{1,0:T(8,128)(2,1)S(1)} %add_convert_fusion), channel_id=1, source_target_pairs={{0,4},{1,5},{4,6},{5,7},{6,2},{7,3},{2,0},{3,1},{8,12},{9,13},{12,... | collective-permute-start | bytes 393224 | tf_op jit(solution)/shard_map/ppermute | solution.py:171
  (2 other events, 7.7 us)

commit v7 on v6

--- a/solution.py
+++ b/solution.py
@@ -123,7 +123,7 @@
     flying = [lax.ppermute(block, "shard", ring) for block in blocks]
     partner = lax.ppermute(inputs, "shard", swap)
     current, moment_now, drift = outer_start(*outer)
-    drift, flying[0] = lax.optimization_barrier((drift, flying[0]))
+    drift, flying[-1] = lax.optimization_barrier((drift, flying[-1]))
     drift = exchange(drift, 1)
     both = [
         jnp.concatenate([ordered(inputs, k), ordered(partner, k)], axis=0) for k in range(chips)
@@ -141,7 +141,7 @@
             if k < chips - 2:
                 flying = [lax.ppermute(block, "shard", ring) for block in blocks]
             if k == 0:
-                drift, flying[0] = lax.optimization_barrier((drift, flying[0]))
+                drift, flying[-1] = lax.optimization_barrier((drift, flying[-1]))
                 step = 2
                 while step < lax.axis_size("replica"):
                     drift = exchange(drift, step)

time: 68.2 us -> 68.2 us (level)
  no operation moved by 1% of the time
where the time goes in v7:
time: 68.2 us; the launch traced here: 67.9 us
  starting transfers between devices  40.9 us (60%)
  waiting for transfers between devices  9.71 us (14%)
  matrix products  6.91 us (10%)
  other arithmetic  4.92 us (7%)
  local copies, waits for them, and re-layouts  3.77 us (6%)
  between operations  1.67 us (2%)
    ppermute x6, starting transfers between devices, inner_step(): flying = [lax.ppermute(block, 'shard', ring) for block in blocks]  16.1 us
    ppermute x6, starting transfers between devices, inner_step(): came = lax.ppermute(sums[j], 'shard', ring)  13.4 us
    ppermute x3, starting transfers between devices, inner_step(): sums[j] = lax.ppermute(sums[j], 'shard', ring).astype(jnp.float32) + own  7.53 us
    ppermute x6, waiting for transfers between devices, inner_step(): flying = [lax.ppermute(block, 'shard', ring) for block in blocks]  4.02 us
    ppermute x3, waiting for transfers between devices, inner_step(): sums[j] = lax.ppermute(sums[j], 'shard', ring).astype(jnp.float32) + own  3.64 us
    dot_general x12, matrix products, term(): lax.dot_general(both[k][:, cuts[j]], grad_both, (((0,), (0,)), ((), ())),...  3.29 us
    ppermute x2, starting transfers between devices, exchange(): lax.ppermute(total, 'replica', [(i, i ^ step) for i in range(replicas)])  3.05 us
    dynamic_slice x2, local copies, waits for them, and re-layouts, ordered(): lax.dynamic_slice_in_dim(tokens, (2 * chip + core) * rows, rows, axis=1)  2.92 us
  transfers between devices with their start and end apart: 20, of which 9 were waited for; matrix products, arithmetic and copies ran while one was open for 19% of the time, Pallas kernels for 0%

profile of v7, /device:TPU:0, one launch (start us, length us, event | category | flops | bytes accessed | tf_op | source)
XLA Modules:
  0.0 67.9 jit_solution(11340159818575759261)
XLA Ops:
  1.2 1.2 %convert_element_type.88 = bf16[768,256]{1,0:T(8,128)(2,1)S(1)} convert(f32[768,256]{1,0:T(8,128)} %param.15) | non-fusion elementwise | flops 196608 | bytes 1179648 | tf_op jit(solution)/shard_map/convert_element_type | solution.py:121
  2.4 3.7 %collective-permute-start.2 = (bf16[384,256]{1,0:T(8,128)(2,1)S(1)}, bf16[384,256]{1,0:T(8,128)(2,1)S(1)}, u32[]{:S(2)}, u32[]{:S(2)}) collective-permute-start(bf16[384,256]{1,0:T(8,128)(2,1)S(1)} %get-tuple-element.37), channel_id=1, source_target_pairs={{0,4},{1,5},{4,6},{5,7},{6,2},{7,3},{2,0},{3,1},{8,12},{9,13},{12,... | collective-permute-start | bytes 589832 | tf_op jit(solution)/shard_map/ppermute | solution.py:123
  6.0 1.6 %collective-permute-start.1 = (bf16[384,256]{1,0:T(8,128)(2,1)S(1)}, bf16[384,256]{1,0:T(8,128)(2,1)S(1)}, u32[]{:S(2)}, u32[]{:S(2)}) collective-permute-start(bf16[384,256]{1,0:T(8,128)(2,1)S(1)} %get-tuple-element.36), channel_id=1, source_target_pairs={{0,4},{1,5},{4,6},{5,7},{6,2},{7,3},{2,0},{3,1},{8,12},{9,13},{12,... | collective-permute-start | bytes 589832 | tf_op jit(solution)/shard_map/ppermute | solution.py:123
  9.0 0.9 %fusion.61 = bf16[1,6144]{1,0:T(2,128)(2,1)S(1)} fusion(bf16[1,16,1,6144]{3,1,2,0:T(8,128)(2,1)} %param.18, s32[]{:T(128)S(6)} %select_n.52, f32[16,1,6144]{2,1,0:T(1,128)} %param.19), kind=kLoop, calls=%fused_computation.116 | loop fusion | flops 18432 | bytes 49156 | tf_op jit(solution)/shard_map/convert_element_type | solution.py:61
  10.0 1.3 %collective-permute-done.2 = bf16[384,256]{1,0:T(8,128)(2,1)S(1)} collective-permute-done((bf16[384,256]{1,0:T(8,128)(2,1)S(1)}, bf16[384,256]{1,0:T(8,128)(2,1)S(1)}, u32[]{:S(2)}, u32[]{:S(2)}) %collective-permute-start.2) | collective-permute-done | bytes 196640 | tf_op jit(solution)/shard_map/ppermute | solution.py:123
  11.2 3.4 %collective-permute-start.5 = (bf16[384,256]{1,0:T(8,128)(2,1)S(1)}, bf16[384,256]{1,0:T(8,128)(2,1)S(1)}, u32[]{:S(2)}, u32[]{:S(2)}) collective-permute-start(bf16[384,256]{1,0:T(8,128)(2,1)S(1)} %collective-permute-done.2), channel_id=1, source_target_pairs={{0,4},{1,5},{4,6},{5,7},{6,2},{7,3},{2,0},{3,1},{8,12},{9,13},{12,... | collective-permute-start | bytes 589832 | tf_op jit(solution)/shard_map/ppermute | solution.py:142
  15.5 3.4 %collective-permute-start.3 = (bf16[384,256]{1,0:T(8,128)(2,1)S(1)}, bf16[384,256]{1,0:T(8,128)(2,1)S(1)}, u32[]{:S(2)}, u32[]{:S(2)}) collective-permute-start(bf16[384,256]{1,0:T(8,128)(2,1)S(1)} %collective-permute-done.1), channel_id=1, source_target_pairs={{0,4},{1,5},{4,6},{5,7},{6,2},{7,3},{2,0},{3,1},{8,12},{9,13},{12,... | collective-permute-start | bytes 589832 | tf_op jit(solution)/shard_map/ppermute | solution.py:142
  18.8 1.5 %collective-permute-start.4 = (f32[1,6144]{1,0:T(1,128)S(1)}, f32[1,6144]{1,0:T(1,128)S(1)}, u32[]{:S(2)}, u32[]{:S(2)}) collective-permute-start(f32[1,6144]{1,0:T(1,128)S(1)} %convert_element_type.92), channel_id=1, source_target_pairs={{0,8},{8,0},{16,24},{24,16},{1,9},{9,1},{17,25},{25,17},{2,10},{10... | collective-permute-start | bytes 73736 | tf_op jit(solution)/shard_map/ppermute | solution.py:70
  20.3 1.5 %constant_dynamic-slice_fusion.7 = (bf16[256,768]{1,0:T(8,128)(2,1)S(1)}, bf16[256,768]{1,0:T(8,128)(2,1)S(1)}, bf16[256,768]{1,0:T(8,128)(2,1)S(1)}, bf16[256,768]{1,0:T(8,128)(2,1)S(1)}) fusion(bf16[256,6144]{1,0:T(8,128)(2,1)} %param.11, s32[]{:T(128)S(6)} %select_n.49, s32[]{:T(128)S(6)} %select_n.51, s32[]{:T(128)S(6)} %select_n.56, s32[]{:T(128)S(6)} %select_n.54), kind=kLoop, calls=%fused_computation.129 | loop fusion | bytes 3145744 | tf_op jit(solution)/shard_map/dynamic_slice | solution.py:118
  24.2 3.4 %collective-permute-start.6 = (bf16[384,256]{1,0:T(8,128)(2,1)S(1)}, bf16[384,256]{1,0:T(8,128)(2,1)S(1)}, u32[]{:S(2)}, u32[]{:S(2)}) collective-permute-start(bf16[384,256]{1,0:T(8,128)(2,1)S(1)} %collective-permute-done.3), channel_id=1, source_target_pairs={{0,4},{1,5},{4,6},{5,7},{6,2},{7,3},{2,0},{3,1},{8,12},{9,13},{12,... | collective-permute-start | bytes 589832 | tf_op jit(solution)/shard_map/ppermute | solution.py:142
  27.6 1.5 %constant_dynamic-slice_fusion.6 = (bf16[256,768]{1,0:T(8,128)(2,1)S(1)}, bf16[256,768]{1,0:T(8,128)(2,1)S(1)}, bf16[256,768]{1,0:T(8,128)(2,1)S(1)}, bf16[256,768]{1,0:T(8,128)(2,1)S(1)}) fusion(bf16[256,6144]{1,0:T(8,128)(2,1)} %collective-permute-done, s32[]{:T(128)S(6)} %select_n.49, s32[]{:T(128)S(6)} %select_n.56, s32[]{:T(128)S(6)} %select_n.54, ...), kind=kLoop, calls=%fused_computation.128 | loop fusion | bytes 3145744 | tf_op jit(solution)/shard_map/dynamic_slice | solution.py:118
  31.3 1.2 %collective-permute-done.6 = bf16[384,256]{1,0:T(8,128)(2,1)S(1)} collective-permute-done((bf16[384,256]{1,0:T(8,128)(2,1)S(1)}, bf16[384,256]{1,0:T(8,128)(2,1)S(1)}, u32[]{:S(2)}, u32[]{:S(2)}) %collective-permute-start.6) | collective-permute-done | bytes 196640 | tf_op jit(solution)/shard_map/ppermute | solution.py:142
  32.9 1.6 %collective-permute-start.19 = (f32[1,6144]{1,0:T(1,128)S(1)}, f32[1,6144]{1,0:T(1,128)S(1)}, u32[]{:S(2)}, u32[]{:S(2)}) collective-permute-start(f32[1,6144]{1,0:T(1,128)S(1)} %add.167), channel_id=1, source_target_pairs={{0,16},{8,24},{16,0},{24,8},{1,17},{9,25},{17,1},{25,9},{2,18},{10... | collective-permute-start | bytes 73736 | tf_op jit(solution)/shard_map/ppermute | solution.py:70
  37.8 2.9 %collective-permute-start.10 = (bf16[256,256]{1,0:T(8,128)(2,1)S(1)}, bf16[256,256]{1,0:T(8,128)(2,1)S(1)}, u32[]{:S(2)}, u32[]{:S(2)}) collective-permute-start(bf16[256,256]{1,0:T(8,128)(2,1)S(1)} %convolution_convert_fusion.2), channel_id=1, source_target_pairs={{0,4},{1,5},{4,6},{5,7},{6,2},{7,3},{2,0},{3,1},{8,12},{9,13},{12,... | collective-permute-start | bytes 393224 | tf_op jit(solution)/shard_map/ppermute | solution.py:167
  42.5 1.3 %collective-permute-start.16 = (bf16[256,256]{1,0:T(8,128)(2,1)S(1)}, bf16[256,256]{1,0:T(8,128)(2,1)S(1)}, u32[]{:S(2)}, u32[]{:S(2)}) collective-permute-start(bf16[256,256]{1,0:T(8,128)(2,1)S(1)} %convolution_convert_fusion), channel_id=1, source_target_pairs={{0,4},{1,5},{4,6},{5,7},{6,2},{7,3},{2,0},{3,1},{8,12},{9,13},{12,... | collective-permute-start | bytes 393224 | tf_op jit(solution)/shard_map/ppermute | solution.py:167
  44.8 3.4 %collective-permute-start.11 = (bf16[256,256]{1,0:T(8,128)(2,1)S(1)}, bf16[256,256]{1,0:T(8,128)(2,1)S(1)}, u32[]{:S(2)}, u32[]{:S(2)}) collective-permute-start(bf16[256,256]{1,0:T(8,128)(2,1)S(1)} %add_convert_fusion.5), channel_id=1, source_target_pairs={{0,4},{1,5},{4,6},{5,7},{6,2},{7,3},{2,0},{3,1},{8,12},{9,13},{12,... | collective-permute-start | bytes 393224 | tf_op jit(solution)/shard_map/ppermute | solution.py:167
  48.6 2.5 %collective-permute-start.14 = (bf16[256,256]{1,0:T(8,128)(2,1)S(1)}, bf16[256,256]{1,0:T(8,128)(2,1)S(1)}, u32[]{:S(2)}, u32[]{:S(2)}) collective-permute-start(bf16[256,256]{1,0:T(8,128)(2,1)S(1)} %add_convert_fusion.3), channel_id=1, source_target_pairs={{0,4},{1,5},{4,6},{5,7},{6,2},{7,3},{2,0},{3,1},{8,12},{9,13},{12,... | collective-permute-start | bytes 393224 | tf_op jit(solution)/shard_map/ppermute | solution.py:167
  51.4 2.5 %collective-permute-start.17 = (bf16[256,256]{1,0:T(8,128)(2,1)S(1)}, bf16[256,256]{1,0:T(8,128)(2,1)S(1)}, u32[]{:S(2)}, u32[]{:S(2)}) collective-permute-start(bf16[256,256]{1,0:T(8,128)(2,1)S(1)} %add_convert_fusion.1), channel_id=1, source_target_pairs={{0,4},{1,5},{4,6},{5,7},{6,2},{7,3},{2,0},{3,1},{8,12},{9,13},{12,... | collective-permute-start | bytes 393224 | tf_op jit(solution)/shard_map/ppermute | solution.py:167
  54.2 2.5 %collective-permute-start.12 = (bf16[256,256]{1,0:T(8,128)(2,1)S(1)}, bf16[256,256]{1,0:T(8,128)(2,1)S(1)}, u32[]{:S(2)}, u32[]{:S(2)}) collective-permute-start(bf16[256,256]{1,0:T(8,128)(2,1)S(1)} %add_convert_fusion.4), channel_id=1, source_target_pairs={{0,4},{1,5},{4,6},{5,7},{6,2},{7,3},{2,0},{3,1},{8,12},{9,13},{12,... | collective-permute-start | bytes 393224 | tf_op jit(solution)/shard_map/ppermute | solution.py:171
  57.0 2.5 %collective-permute-start.15 = (bf16[256,256]{1,0:T(8,128)(2,1)S(1)}, bf16[256,256]{1,0:T(8,128)(2,1)S(1)}, u32[]{:S(2)}, u32[]{:S(2)}) collective-permute-start(bf16[256,256]{1,0:T(8,128)(2,1)S(1)} %add_convert_fusion.2), channel_id=1, source_target_pairs={{0,4},{1,5},{4,6},{5,7},{6,2},{7,3},{2,0},{3,1},{8,12},{9,13},{12,... | collective-permute-start | bytes 393224 | tf_op jit(solution)/shard_map/ppermute | solution.py:171
  59.8 2.5 %collective-permute-start.18 = (bf16[256,256]{1,0:T(8,128)(2,1)S(1)}, bf16[256,256]{1,0:T(8,128)(2,1)S(1)}, u32[]{:S(2)}, u32[]{:S(2)}) collective-permute-start(bf16[256,256]{1,0:T(8,128)(2,1)S(1)} %add_convert_fusion), channel_id=1, source_target_pairs={{0,4},{1,5},{4,6},{5,7},{6,2},{7,3},{2,0},{3,1},{8,12},{9,13},{12,... | collective-permute-start | bytes 393224 | tf_op jit(solution)/shard_map/ppermute | solution.py:171
  62.3 2.2 %collective-permute-done.15 = bf16[256,256]{1,0:T(8,128)(2,1)S(1)} collective-permute-done((bf16[256,256]{1,0:T(8,128)(2,1)S(1)}, bf16[256,256]{1,0:T(8,128)(2,1)S(1)}, u32[]{:S(2)}, u32[]{:S(2)}) %collective-permute-start.15) | collective-permute-done | bytes 131104 | tf_op jit(solution)/shard_map/ppermute | solution.py:171
  64.6 1.4 %collective-permute-done.18 = bf16[256,256]{1,0:T(8,128)(2,1)S(1)} collective-permute-done((bf16[256,256]{1,0:T(8,128)(2,1)S(1)}, bf16[256,256]{1,0:T(8,128)(2,1)S(1)}, u32[]{:S(2)}, u32[]{:S(2)}) %collective-permute-start.18) | collective-permute-done | bytes 131104 | tf_op jit(solution)/shard_map/ppermute | solution.py:171
  66.1 1.8 %multiply_subtract_fusion = (f32[768,256]{1,0:T(8,128)}, f32[768,256]{1,0:T(8,128)}, f32[768,256]{1,0:T(8,128)}) fusion(f32[768,256]{1,0:T(8,128)S(1)} %copy-done.1, f32[256,256]{1,0:T(8,128)S(1)} %convert_add_fusion, f32[256,256]{1,0:T(8,128)S(1)} %convert_add_fusion.1, f32[256,256]{1,0:T(8,128)S(1)} %convert_add_fusion.2, f32[768,256]{1,0:T(8,128)S(1)} %copy-done.2, ...), kind=kLoop, calls=%fused_computation.46 | loop fusion | flops 3342336 | bytes 5505024 | tf_op jit(solution)/shard_map/sub | solution.py:85
  (73 shorter events, 14.7 us)
Async XLA Ops:
  0.6 34.3 %copy-start = (bf16[256,128]{1,0:T(8,128)(2,1)S(1)}, bf16[256,128]{1,0:T(8,128)(2,1)}, u32[]{:S(2)}) copy-start(bf16[256,128]{1,0:T(8,128)(2,1)} %param.14) | copy-start | bytes 196612
  0.6 26.9 %collective-permute-start = (bf16[256,6144]{1,0:T(8,128)(2,1)}, bf16[256,6144]{1,0:T(8,128)(2,1)}, u32[]{:S(2)}, u32[]{:S(2)}) collective-permute-start(bf16[256,6144]{1,0:T(8,128)(2,1)} %param.11), channel_id=1, source_target_pairs={{0,1},{1,0},{2,3},{3,2},{4,5},{5,4},{6,7},{7,6},{8,9},{9,8},{10,11... | collective-permute-start | bytes 9437192 | tf_op jit(solution)/shard_map/ppermute | solution.py:124
  2.4 8.9 %collective-permute-start.2 = (bf16[384,256]{1,0:T(8,128)(2,1)S(1)}, bf16[384,256]{1,0:T(8,128)(2,1)S(1)}, u32[]{:S(2)}, u32[]{:S(2)}) collective-permute-start(bf16[384,256]{1,0:T(8,128)(2,1)S(1)} %get-tuple-element.37), channel_id=1, source_target_pairs={{0,4},{1,5},{4,6},{5,7},{6,2},{7,3},{2,0},{3,1},{8,12},{9,13},{12,... | collective-permute-start | bytes 589832 | tf_op jit(solution)/shard_map/ppermute | solution.py:123
  6.0 9.4 %collective-permute-start.1 = (bf16[384,256]{1,0:T(8,128)(2,1)S(1)}, bf16[384,256]{1,0:T(8,128)(2,1)S(1)}, u32[]{:S(2)}, u32[]{:S(2)}) collective-permute-start(bf16[384,256]{1,0:T(8,128)(2,1)S(1)} %get-tuple-element.36), channel_id=1, source_target_pairs={{0,4},{1,5},{4,6},{5,7},{6,2},{7,3},{2,0},{3,1},{8,12},{9,13},{12,... | collective-permute-start | bytes 589832 | tf_op jit(solution)/shard_map/ppermute | solution.py:123
  11.2 11.5 %collective-permute-start.5 = (bf16[384,256]{1,0:T(8,128)(2,1)S(1)}, bf16[384,256]{1,0:T(8,128)(2,1)S(1)}, u32[]{:S(2)}, u32[]{:S(2)}) collective-permute-start(bf16[384,256]{1,0:T(8,128)(2,1)S(1)} %collective-permute-done.2), channel_id=1, source_target_pairs={{0,4},{1,5},{4,6},{5,7},{6,2},{7,3},{2,0},{3,1},{8,12},{9,13},{12,... | collective-permute-start | bytes 589832 | tf_op jit(solution)/shard_map/ppermute | solution.py:142
  15.5 8.7 %collective-permute-start.3 = (bf16[384,256]{1,0:T(8,128)(2,1)S(1)}, bf16[384,256]{1,0:T(8,128)(2,1)S(1)}, u32[]{:S(2)}, u32[]{:S(2)}) collective-permute-start(bf16[384,256]{1,0:T(8,128)(2,1)S(1)} %collective-permute-done.1), channel_id=1, source_target_pairs={{0,4},{1,5},{4,6},{5,7},{6,2},{7,3},{2,0},{3,1},{8,12},{9,13},{12,... | collective-permute-start | bytes 589832 | tf_op jit(solution)/shard_map/ppermute | solution.py:142
  18.8 3.8 %collective-permute-start.4 = (f32[1,6144]{1,0:T(1,128)S(1)}, f32[1,6144]{1,0:T(1,128)S(1)}, u32[]{:S(2)}, u32[]{:S(2)}) collective-permute-start(f32[1,6144]{1,0:T(1,128)S(1)} %convert_element_type.92), channel_id=1, source_target_pairs={{0,8},{8,0},{16,24},{24,16},{1,9},{9,1},{17,25},{25,17},{2,10},{10... | collective-permute-start | bytes 73736 | tf_op jit(solution)/shard_map/ppermute | solution.py:70
  22.7 8.2 %collective-permute-start.7 = (bf16[384,256]{1,0:T(8,128)(2,1)S(1)}, bf16[384,256]{1,0:T(8,128)(2,1)S(1)}, u32[]{:S(2)}, u32[]{:S(2)}) collective-permute-start(bf16[384,256]{1,0:T(8,128)(2,1)S(1)} %collective-permute-done.5), channel_id=1, source_target_pairs={{0,4},{1,5},{4,6},{5,7},{6,2},{7,3},{2,0},{3,1},{8,12},{9,13},{12,... | collective-permute-start | bytes 589832 | tf_op jit(solution)/shard_map/ppermute | solution.py:142
  24.2 8.3 %collective-permute-start.6 = (bf16[384,256]{1,0:T(8,128)(2,1)S(1)}, bf16[384,256]{1,0:T(8,128)(2,1)S(1)}, u32[]{:S(2)}, u32[]{:S(2)}) collective-permute-start(bf16[384,256]{1,0:T(8,128)(2,1)S(1)} %collective-permute-done.3), channel_id=1, source_target_pairs={{0,4},{1,5},{4,6},{5,7},{6,2},{7,3},{2,0},{3,1},{8,12},{9,13},{12,... | collective-permute-start | bytes 589832 | tf_op jit(solution)/shard_map/ppermute | solution.py:142
  32.8 1.6 %collective-permute-start.8 = (f32[256,256]{0,1:T(8,128)S(1)}, f32[256,256]{0,1:T(8,128)S(1)}, u32[]{:S(2)}, u32[]{:S(2)}) collective-permute-start(f32[256,256]{0,1:T(8,128)S(1)} %slice.113), channel_id=1, source_target_pairs={{0,1},{1,0},{2,3},{3,2},{4,5},{5,4},{6,7},{7,6},{8,9},{9,8},{10,11... | collective-permute-start | bytes 786440 | tf_op jit(solution)/shard_map/ppermute | solution.py:150
  32.9 3.9 %collective-permute-start.19 = (f32[1,6144]{1,0:T(1,128)S(1)}, f32[1,6144]{1,0:T(1,128)S(1)}, u32[]{:S(2)}, u32[]{:S(2)}) collective-permute-start(f32[1,6144]{1,0:T(1,128)S(1)} %add.167), channel_id=1, source_target_pairs={{0,16},{8,24},{16,0},{24,8},{1,17},{9,25},{17,1},{25,9},{2,18},{10... | collective-permute-start | bytes 73736 | tf_op jit(solution)/shard_map/ppermute | solution.py:70
  35.8 1.7 %collective-permute-start.9 = (bf16[256,256]{0,1:T(8,128)(2,1)S(1)}, bf16[256,256]{0,1:T(8,128)(2,1)S(1)}, u32[]{:S(2)}, u32[]{:S(2)}) collective-permute-start(bf16[256,256]{0,1:T(8,128)(2,1)S(1)} %fusion.53), channel_id=1, source_target_pairs={{0,1},{1,0},{2,3},{3,2},{4,5},{5,4},{6,7},{7,6},{8,9},{9,8},{10,11... | collective-permute-start | bytes 393224 | tf_op jit(solution)/shard_map/ppermute | solution.py:152
  37.8 6.8 %collective-permute-start.10 = (bf16[256,256]{1,0:T(8,128)(2,1)S(1)}, bf16[256,256]{1,0:T(8,128)(2,1)S(1)}, u32[]{:S(2)}, u32[]{:S(2)}) collective-permute-start(bf16[256,256]{1,0:T(8,128)(2,1)S(1)} %convolution_convert_fusion.2), channel_id=1, source_target_pairs={{0,4},{1,5},{4,6},{5,7},{6,2},{7,3},{2,0},{3,1},{8,12},{9,13},{12,... | collective-permute-start | bytes 393224 | tf_op jit(solution)/shard_map/ppermute | solution.py:167
  41.2 7.0 %collective-permute-start.13 = (bf16[256,256]{1,0:T(8,128)(2,1)S(1)}, bf16[256,256]{1,0:T(8,128)(2,1)S(1)}, u32[]{:S(2)}, u32[]{:S(2)}) collective-permute-start(bf16[256,256]{1,0:T(8,128)(2,1)S(1)} %convolution_convert_fusion.1), channel_id=1, source_target_pairs={{0,4},{1,5},{4,6},{5,7},{6,2},{7,3},{2,0},{3,1},{8,12},{9,13},{12,... | collective-permute-start | bytes 393224 | tf_op jit(solution)/shard_map/ppermute | solution.py:167
  42.5 8.6 %collective-permute-start.16 = (bf16[256,256]{1,0:T(8,128)(2,1)S(1)}, bf16[256,256]{1,0:T(8,128)(2,1)S(1)}, u32[]{:S(2)}, u32[]{:S(2)}) collective-permute-start(bf16[256,256]{1,0:T(8,128)(2,1)S(1)} %convolution_convert_fusion), channel_id=1, source_target_pairs={{0,4},{1,5},{4,6},{5,7},{6,2},{7,3},{2,0},{3,1},{8,12},{9,13},{12,... | collective-permute-start | bytes 393224 | tf_op jit(solution)/shard_map/ppermute | solution.py:167
  44.8 9.1 %collective-permute-start.11 = (bf16[256,256]{1,0:T(8,128)(2,1)S(1)}, bf16[256,256]{1,0:T(8,128)(2,1)S(1)}, u32[]{:S(2)}, u32[]{:S(2)}) collective-permute-start(bf16[256,256]{1,0:T(8,128)(2,1)S(1)} %add_convert_fusion.5), channel_id=1, source_target_pairs={{0,4},{1,5},{4,6},{5,7},{6,2},{7,3},{2,0},{3,1},{8,12},{9,13},{12,... | collective-permute-start | bytes 393224 | tf_op jit(solution)/shard_map/ppermute | solution.py:167
  48.6 8.1 %collective-permute-start.14 = (bf16[256,256]{1,0:T(8,128)(2,1)S(1)}, bf16[256,256]{1,0:T(8,128)(2,1)S(1)}, u32[]{:S(2)}, u32[]{:S(2)}) collective-permute-start(bf16[256,256]{1,0:T(8,128)(2,1)S(1)} %add_convert_fusion.3), channel_id=1, source_target_pairs={{0,4},{1,5},{4,6},{5,7},{6,2},{7,3},{2,0},{3,1},{8,12},{9,13},{12,... | collective-permute-start | bytes 393224 | tf_op jit(solution)/shard_map/ppermute | solution.py:167
  51.4 14.7 %copy-start.1 = (f32[768,256]{1,0:T(8,128)S(1)}, f32[768,256]{1,0:T(8,128)}, u32[]{:S(2)}) copy-start(f32[768,256]{1,0:T(8,128)} %param.15) | copy-start | bytes 2359300
  51.4 14.7 %copy-start.2 = (f32[768,256]{1,0:T(8,128)S(1)}, f32[768,256]{1,0:T(8,128)}, u32[]{:S(2)}) copy-start(f32[768,256]{1,0:T(8,128)} %param.16) | copy-start | bytes 2359300
  51.4 14.7 %copy-start.3 = (f32[768,256]{1,0:T(8,128)S(1)}, f32[768,256]{1,0:T(8,128)}, u32[]{:S(2)}) copy-start(f32[768,256]{1,0:T(8,128)} %param.17) | copy-start | bytes 2359300
  51.4 8.1 %collective-permute-start.17 = (bf16[256,256]{1,0:T(8,128)(2,1)S(1)}, bf16[256,256]{1,0:T(8,128)(2,1)S(1)}, u32[]{:S(2)}, u32[]{:S(2)}) collective-permute-start(bf16[256,256]{1,0:T(8,128)(2,1)S(1)} %add_convert_fusion.1), channel_id=1, source_target_pairs={{0,4},{1,5},{4,6},{5,7},{6,2},{7,3},{2,0},{3,1},{8,12},{9,13},{12,... | collective-permute-start | bytes 393224 | tf_op jit(solution)/shard_map/ppermute | solution.py:167
  54.2 8.1 %collective-permute-start.12 = (bf16[256,256]{1,0:T(8,128)(2,1)S(1)}, bf16[256,256]{1,0:T(8,128)(2,1)S(1)}, u32[]{:S(2)}, u32[]{:S(2)}) collective-permute-start(bf16[256,256]{1,0:T(8,128)(2,1)S(1)} %add_convert_fusion.4), channel_id=1, source_target_pairs={{0,4},{1,5},{4,6},{5,7},{6,2},{7,3},{2,0},{3,1},{8,12},{9,13},{12,... | collective-permute-start | bytes 393224 | tf_op jit(solution)/shard_map/ppermute | solution.py:171
  57.0 7.6 %collective-permute-start.15 = (bf16[256,256]{1,0:T(8,128)(2,1)S(1)}, bf16[256,256]{1,0:T(8,128)(2,1)S(1)}, u32[]{:S(2)}, u32[]{:S(2)}) collective-permute-start(bf16[256,256]{1,0:T(8,128)(2,1)S(1)} %add_convert_fusion.2), channel_id=1, source_target_pairs={{0,4},{1,5},{4,6},{5,7},{6,2},{7,3},{2,0},{3,1},{8,12},{9,13},{12,... | collective-permute-start | bytes 393224 | tf_op jit(solution)/shard_map/ppermute | solution.py:171
  59.8 6.2 %collective-permute-start.18 = (bf16[256,256]{1,0:T(8,128)(2,1)S(1)}, bf16[256,256]{1,0:T(8,128)(2,1)S(1)}, u32[]{:S(2)}, u32[]{:S(2)}) collective-permute-start(bf16[256,256]{1,0:T(8,128)(2,1)S(1)} %add_convert_fusion), channel_id=1, source_target_pairs={{0,4},{1,5},{4,6},{5,7},{6,2},{7,3},{2,0},{3,1},{8,12},{9,13},{12,... | collective-permute-start | bytes 393224 | tf_op jit(solution)/shard_map/ppermute | solution.py:171
  (2 other events, 7.7 us)

commit v8 on v6

--- a/solution.py
+++ b/solution.py
@@ -6,7 +6,7 @@
 from jax.sharding import PartitionSpec as P
 
 ADAM_STEP = 100
-GATHER_SHARES = (24, 24)
+GATHER_SHARES = (16, 16, 16)
 SCATTER_SHARES = (16, 16, 16)
 
 

time: 68.2 us -> 68.1 us (level)
  waiting for transfers between devices: 9.71 us -> 4.84 us
  starting transfers between devices: 40.9 us -> 45.1 us
    ppermute x6 -> x9, waiting for transfers between devices: 4.01 us -> 0.04 us  [inner_step(): flying = [lax.ppermute(block, 'shard', ring) for block in blocks]]
    ppermute x6 -> x9, starting transfers between devices: 16.1 us -> 19.7 us  [inner_step(): flying = [lax.ppermute(block, 'shard', ring) for block in blocks]]
    ppermute x2, waiting for transfers between devices: 1.59 us -> 0.7 us  [exchange(): lax.ppermute(total, 'replica', [(i, i ^ step) for i in range(replicas)])]
    dot_general x6 -> x9, matrix products: 2.06 us -> 2.52 us  [inner_step(): jnp.dot(both[k][:, cut], block, preferred_element_type=jnp.float32)]
  transfers between devices with their start and end apart: 20 -> 23, of which waited for: 9 -> 4; matrix products, arithmetic and copies ran while one was open for 19% -> 20% of each run, Pallas kernels for 0% -> 0%
where the time goes in v8:
time: 68.1 us; the launch traced here: 67.8 us
  starting transfers between devices  45.1 us (66%)
  matrix products  7.37 us (11%)
  other arithmetic  4.92 us (7%)
  waiting for transfers between devices  4.84 us (7%)
  local copies, waits for them, and re-layouts  3.77 us (6%)
  between operations  1.8 us (3%)
    ppermute x9, starting transfers between devices, inner_step(): flying = [lax.ppermute(block, 'shard', ring) for block in blocks]  19.7 us
    ppermute x6, starting transfers between devices, inner_step(): came = lax.ppermute(sums[j], 'shard', ring)  13.9 us
    ppermute x3, starting transfers between devices, inner_step(): sums[j] = lax.ppermute(sums[j], 'shard', ring).astype(jnp.float32) + own  7.53 us
    ppermute x3, waiting for transfers between devices, inner_step(): sums[j] = lax.ppermute(sums[j], 'shard', ring).astype(jnp.float32) + own  3.64 us
    dot_general x12, matrix products, term(): lax.dot_general(both[k][:, cuts[j]], grad_both, (((0,), (0,)), ((), ())),...  3.29 us
    ppermute x2, starting transfers between devices, exchange(): lax.ppermute(total, 'replica', [(i, i ^ step) for i in range(replicas)])  3.16 us
    dynamic_slice x2, local copies, waits for them, and re-layouts, ordered(): lax.dynamic_slice_in_dim(tokens, (2 * chip + core) * rows, rows, axis=1)  2.92 us
    dot_general x9, matrix products, inner_step(): jnp.dot(both[k][:, cut], block, preferred_element_type=jnp.float32)  2.52 us
  transfers between devices with their start and end apart: 23, of which 4 were waited for; matrix products, arithmetic and copies ran while one was open for 20% of the time, Pallas kernels for 0%

profile of v8, /device:TPU:0, one launch (start us, length us, event | category | flops | bytes accessed | tf_op | source)
XLA Modules:
  0.0 67.8 jit_solution(6733770874517853954)
XLA Ops:
  1.2 1.2 %convert_element_type.88 = bf16[768,256]{1,0:T(8,128)(2,1)S(1)} convert(f32[768,256]{1,0:T(8,128)} %param.15) | non-fusion elementwise | flops 196608 | bytes 1179648 | tf_op jit(solution)/shard_map/convert_element_type | solution.py:121
  2.4 3.7 %collective-permute-start.1 = (bf16[256,256]{1,0:T(8,128)(2,1)S(1)}, bf16[256,256]{1,0:T(8,128)(2,1)S(1)}, u32[]{:S(2)}, u32[]{:S(2)}) collective-permute-start(bf16[256,256]{1,0:T(8,128)(2,1)S(1)} %get-tuple-element.38), channel_id=1, source_target_pairs={{0,4},{1,5},{4,6},{5,7},{6,2},{7,3},{2,0},{3,1},{8,12},{9,13},{12,... | collective-permute-start | bytes 393224 | tf_op jit(solution)/shard_map/ppermute | solution.py:123
  6.0 1.6 %collective-permute-start.3 = (bf16[256,256]{1,0:T(8,128)(2,1)S(1)}, bf16[256,256]{1,0:T(8,128)(2,1)S(1)}, u32[]{:S(2)}, u32[]{:S(2)}) collective-permute-start(bf16[256,256]{1,0:T(8,128)(2,1)S(1)} %get-tuple-element.37), channel_id=1, source_target_pairs={{0,4},{1,5},{4,6},{5,7},{6,2},{7,3},{2,0},{3,1},{8,12},{9,13},{12,... | collective-permute-start | bytes 393224 | tf_op jit(solution)/shard_map/ppermute | solution.py:123
  10.5 1.6 %collective-permute-start.4 = (f32[1,6144]{1,0:T(1,128)S(1)}, f32[1,6144]{1,0:T(1,128)S(1)}, u32[]{:S(2)}, u32[]{:S(2)}) collective-permute-start(f32[1,6144]{1,0:T(1,128)S(1)} %convert_element_type.92), channel_id=1, source_target_pairs={{0,8},{8,0},{16,24},{24,16},{1,9},{9,1},{17,25},{25,17},{2,10},{10... | collective-permute-start | bytes 73736 | tf_op jit(solution)/shard_map/ppermute | solution.py:70
  12.0 2.7 %collective-permute-start.5 = (bf16[256,256]{1,0:T(8,128)(2,1)S(1)}, bf16[256,256]{1,0:T(8,128)(2,1)S(1)}, u32[]{:S(2)}, u32[]{:S(2)}) collective-permute-start(bf16[256,256]{1,0:T(8,128)(2,1)S(1)} %collective-permute-done.1), channel_id=1, source_target_pairs={{0,4},{1,5},{4,6},{5,7},{6,2},{7,3},{2,0},{3,1},{8,12},{9,13},{12,... | collective-permute-start | bytes 393224 | tf_op jit(solution)/shard_map/ppermute | solution.py:142
  14.7 1.3 %collective-permute-start.7 = (bf16[256,256]{1,0:T(8,128)(2,1)S(1)}, bf16[256,256]{1,0:T(8,128)(2,1)S(1)}, u32[]{:S(2)}, u32[]{:S(2)}) collective-permute-start(bf16[256,256]{1,0:T(8,128)(2,1)S(1)} %collective-permute-done.3), channel_id=1, source_target_pairs={{0,4},{1,5},{4,6},{5,7},{6,2},{7,3},{2,0},{3,1},{8,12},{9,13},{12,... | collective-permute-start | bytes 393224 | tf_op jit(solution)/shard_map/ppermute | solution.py:142
  16.0 2.8 %collective-permute-start.6 = (bf16[256,256]{1,0:T(8,128)(2,1)S(1)}, bf16[256,256]{1,0:T(8,128)(2,1)S(1)}, u32[]{:S(2)}, u32[]{:S(2)}) collective-permute-start(bf16[256,256]{1,0:T(8,128)(2,1)S(1)} %collective-permute-done.2), channel_id=1, source_target_pairs={{0,4},{1,5},{4,6},{5,7},{6,2},{7,3},{2,0},{3,1},{8,12},{9,13},{12,... | collective-permute-start | bytes 393224 | tf_op jit(solution)/shard_map/ppermute | solution.py:142
  18.8 1.5 %constant_dynamic-slice_fusion.7 = (bf16[256,768]{1,0:T(8,128)(2,1)S(1)}, bf16[256,768]{1,0:T(8,128)(2,1)S(1)}, bf16[256,768]{1,0:T(8,128)(2,1)S(1)}, bf16[256,768]{1,0:T(8,128)(2,1)S(1)}) fusion(bf16[256,6144]{1,0:T(8,128)(2,1)} %param.11, s32[]{:T(128)S(6)} %select_n.49, s32[]{:T(128)S(6)} %select_n.51, s32[]{:T(128)S(6)} %select_n.56, s32[]{:T(128)S(6)} %select_n.54), kind=kLoop, calls=%fused_computation.101 | loop fusion | bytes 3145744 | tf_op jit(solution)/shard_map/dynamic_slice | solution.py:118
  20.4 1.7 %collective-permute-start.8 = (bf16[256,256]{1,0:T(8,128)(2,1)S(1)}, bf16[256,256]{1,0:T(8,128)(2,1)S(1)}, u32[]{:S(2)}, u32[]{:S(2)}) collective-permute-start(bf16[256,256]{1,0:T(8,128)(2,1)S(1)} %collective-permute-done.5), channel_id=1, source_target_pairs={{0,4},{1,5},{4,6},{5,7},{6,2},{7,3},{2,0},{3,1},{8,12},{9,13},{12,... | collective-permute-start | bytes 393224 | tf_op jit(solution)/shard_map/ppermute | solution.py:142
  22.1 2.8 %collective-permute-start.10 = (bf16[256,256]{1,0:T(8,128)(2,1)S(1)}, bf16[256,256]{1,0:T(8,128)(2,1)S(1)}, u32[]{:S(2)}, u32[]{:S(2)}) collective-permute-start(bf16[256,256]{1,0:T(8,128)(2,1)S(1)} %collective-permute-done.7), channel_id=1, source_target_pairs={{0,4},{1,5},{4,6},{5,7},{6,2},{7,3},{2,0},{3,1},{8,12},{9,13},{12,... | collective-permute-start | bytes 393224 | tf_op jit(solution)/shard_map/ppermute | solution.py:142
  24.9 2.8 %collective-permute-start.9 = (bf16[256,256]{1,0:T(8,128)(2,1)S(1)}, bf16[256,256]{1,0:T(8,128)(2,1)S(1)}, u32[]{:S(2)}, u32[]{:S(2)}) collective-permute-start(bf16[256,256]{1,0:T(8,128)(2,1)S(1)} %collective-permute-done.6), channel_id=1, source_target_pairs={{0,4},{1,5},{4,6},{5,7},{6,2},{7,3},{2,0},{3,1},{8,12},{9,13},{12,... | collective-permute-start | bytes 393224 | tf_op jit(solution)/shard_map/ppermute | solution.py:142
  27.7 1.5 %constant_dynamic-slice_fusion.6 = (bf16[256,768]{1,0:T(8,128)(2,1)S(1)}, bf16[256,768]{1,0:T(8,128)(2,1)S(1)}, bf16[256,768]{1,0:T(8,128)(2,1)S(1)}, bf16[256,768]{1,0:T(8,128)(2,1)S(1)}) fusion(bf16[256,6144]{1,0:T(8,128)(2,1)} %collective-permute-done, s32[]{:T(128)S(6)} %select_n.49, s32[]{:T(128)S(6)} %select_n.56, s32[]{:T(128)S(6)} %select_n.54, ...), kind=kLoop, calls=%fused_computation.100 | loop fusion | bytes 3145744 | tf_op jit(solution)/shard_map/dynamic_slice | solution.py:118
  32.3 1.6 %collective-permute-start.22 = (f32[1,6144]{1,0:T(1,128)S(1)}, f32[1,6144]{1,0:T(1,128)S(1)}, u32[]{:S(2)}, u32[]{:S(2)}) collective-permute-start(f32[1,6144]{1,0:T(1,128)S(1)} %add.176), channel_id=1, source_target_pairs={{0,16},{8,24},{16,0},{24,8},{1,17},{9,25},{17,1},{25,9},{2,18},{10... | collective-permute-start | bytes 73736 | tf_op jit(solution)/shard_map/ppermute | solution.py:70
  37.2 3.4 %collective-permute-start.13 = (bf16[256,256]{1,0:T(8,128)(2,1)S(1)}, bf16[256,256]{1,0:T(8,128)(2,1)S(1)}, u32[]{:S(2)}, u32[]{:S(2)}) collective-permute-start(bf16[256,256]{1,0:T(8,128)(2,1)S(1)} %convolution_convert_fusion.2), channel_id=1, source_target_pairs={{0,4},{1,5},{4,6},{5,7},{6,2},{7,3},{2,0},{3,1},{8,12},{9,13},{12,... | collective-permute-start | bytes 393224 | tf_op jit(solution)/shard_map/ppermute | solution.py:167
  42.5 1.3 %collective-permute-start.19 = (bf16[256,256]{1,0:T(8,128)(2,1)S(1)}, bf16[256,256]{1,0:T(8,128)(2,1)S(1)}, u32[]{:S(2)}, u32[]{:S(2)}) collective-permute-start(bf16[256,256]{1,0:T(8,128)(2,1)S(1)} %convolution_convert_fusion), channel_id=1, source_target_pairs={{0,4},{1,5},{4,6},{5,7},{6,2},{7,3},{2,0},{3,1},{8,12},{9,13},{12,... | collective-permute-start | bytes 393224 | tf_op jit(solution)/shard_map/ppermute | solution.py:167
  44.8 3.4 %collective-permute-start.14 = (bf16[256,256]{1,0:T(8,128)(2,1)S(1)}, bf16[256,256]{1,0:T(8,128)(2,1)S(1)}, u32[]{:S(2)}, u32[]{:S(2)}) collective-permute-start(bf16[256,256]{1,0:T(8,128)(2,1)S(1)} %add_convert_fusion.5), channel_id=1, source_target_pairs={{0,4},{1,5},{4,6},{5,7},{6,2},{7,3},{2,0},{3,1},{8,12},{9,13},{12,... | collective-permute-start | bytes 393224 | tf_op jit(solution)/shard_map/ppermute | solution.py:167
  48.5 2.5 %collective-permute-start.17 = (bf16[256,256]{1,0:T(8,128)(2,1)S(1)}, bf16[256,256]{1,0:T(8,128)(2,1)S(1)}, u32[]{:S(2)}, u32[]{:S(2)}) collective-permute-start(bf16[256,256]{1,0:T(8,128)(2,1)S(1)} %add_convert_fusion.3), channel_id=1, source_target_pairs={{0,4},{1,5},{4,6},{5,7},{6,2},{7,3},{2,0},{3,1},{8,12},{9,13},{12,... | collective-permute-start | bytes 393224 | tf_op jit(solution)/shard_map/ppermute | solution.py:167
  51.3 2.5 %collective-permute-start.20 = (bf16[256,256]{1,0:T(8,128)(2,1)S(1)}, bf16[256,256]{1,0:T(8,128)(2,1)S(1)}, u32[]{:S(2)}, u32[]{:S(2)}) collective-permute-start(bf16[256,256]{1,0:T(8,128)(2,1)S(1)} %add_convert_fusion.1), channel_id=1, source_target_pairs={{0,4},{1,5},{4,6},{5,7},{6,2},{7,3},{2,0},{3,1},{8,12},{9,13},{12,... | collective-permute-start | bytes 393224 | tf_op jit(solution)/shard_map/ppermute | solution.py:167
  54.1 2.5 %collective-permute-start.15 = (bf16[256,256]{1,0:T(8,128)(2,1)S(1)}, bf16[256,256]{1,0:T(8,128)(2,1)S(1)}, u32[]{:S(2)}, u32[]{:S(2)}) collective-permute-start(bf16[256,256]{1,0:T(8,128)(2,1)S(1)} %add_convert_fusion.4), channel_id=1, source_target_pairs={{0,4},{1,5},{4,6},{5,7},{6,2},{7,3},{2,0},{3,1},{8,12},{9,13},{12,... | collective-permute-start | bytes 393224 | tf_op jit(solution)/shard_map/ppermute | solution.py:171
  56.9 2.5 %collective-permute-start.18 = (bf16[256,256]{1,0:T(8,128)(2,1)S(1)}, bf16[256,256]{1,0:T(8,128)(2,1)S(1)}, u32[]{:S(2)}, u32[]{:S(2)}) collective-permute-start(bf16[256,256]{1,0:T(8,128)(2,1)S(1)} %add_convert_fusion.2), channel_id=1, source_target_pairs={{0,4},{1,5},{4,6},{5,7},{6,2},{7,3},{2,0},{3,1},{8,12},{9,13},{12,... | collective-permute-start | bytes 393224 | tf_op jit(solution)/shard_map/ppermute | solution.py:171
  59.7 2.5 %collective-permute-start.21 = (bf16[256,256]{1,0:T(8,128)(2,1)S(1)}, bf16[256,256]{1,0:T(8,128)(2,1)S(1)}, u32[]{:S(2)}, u32[]{:S(2)}) collective-permute-start(bf16[256,256]{1,0:T(8,128)(2,1)S(1)} %add_convert_fusion), channel_id=1, source_target_pairs={{0,4},{1,5},{4,6},{5,7},{6,2},{7,3},{2,0},{3,1},{8,12},{9,13},{12,... | collective-permute-start | bytes 393224 | tf_op jit(solution)/shard_map/ppermute | solution.py:171
  62.3 2.2 %collective-permute-done.18 = bf16[256,256]{1,0:T(8,128)(2,1)S(1)} collective-permute-done((bf16[256,256]{1,0:T(8,128)(2,1)S(1)}, bf16[256,256]{1,0:T(8,128)(2,1)S(1)}, u32[]{:S(2)}, u32[]{:S(2)}) %collective-permute-start.18) | collective-permute-done | bytes 131104 | tf_op jit(solution)/shard_map/ppermute | solution.py:171
  64.5 1.4 %collective-permute-done.21 = bf16[256,256]{1,0:T(8,128)(2,1)S(1)} collective-permute-done((bf16[256,256]{1,0:T(8,128)(2,1)S(1)}, bf16[256,256]{1,0:T(8,128)(2,1)S(1)}, u32[]{:S(2)}, u32[]{:S(2)}) %collective-permute-start.21) | collective-permute-done | bytes 131104 | tf_op jit(solution)/shard_map/ppermute | solution.py:171
  66.0 1.8 %multiply_subtract_fusion = (f32[768,256]{1,0:T(8,128)}, f32[768,256]{1,0:T(8,128)}, f32[768,256]{1,0:T(8,128)}) fusion(f32[768,256]{1,0:T(8,128)S(1)} %copy-done.1, f32[256,256]{1,0:T(8,128)S(1)} %convert_add_fusion, f32[256,256]{1,0:T(8,128)S(1)} %convert_add_fusion.1, f32[256,256]{1,0:T(8,128)S(1)} %convert_add_fusion.2, f32[768,256]{1,0:T(8,128)S(1)} %copy-done.2, ...), kind=kLoop, calls=%fused_computation.37 | loop fusion | flops 3342336 | bytes 5505024 | tf_op jit(solution)/shard_map/sub | solution.py:85
  (82 shorter events, 13.3 us)
Async XLA Ops:
  0.6 33.7 %copy-start = (bf16[256,128]{1,0:T(8,128)(2,1)S(1)}, bf16[256,128]{1,0:T(8,128)(2,1)}, u32[]{:S(2)}) copy-start(bf16[256,128]{1,0:T(8,128)(2,1)} %param.14) | copy-start | bytes 196612
  0.6 27.0 %collective-permute-start = (bf16[256,6144]{1,0:T(8,128)(2,1)}, bf16[256,6144]{1,0:T(8,128)(2,1)}, u32[]{:S(2)}, u32[]{:S(2)}) collective-permute-start(bf16[256,6144]{1,0:T(8,128)(2,1)} %param.11), channel_id=1, source_target_pairs={{0,1},{1,0},{2,3},{3,2},{4,5},{5,4},{6,7},{7,6},{8,9},{9,8},{10,11... | collective-permute-start | bytes 9437192 | tf_op jit(solution)/shard_map/ppermute | solution.py:124
  2.4 8.1 %collective-permute-start.1 = (bf16[256,256]{1,0:T(8,128)(2,1)S(1)}, bf16[256,256]{1,0:T(8,128)(2,1)S(1)}, u32[]{:S(2)}, u32[]{:S(2)}) collective-permute-start(bf16[256,256]{1,0:T(8,128)(2,1)S(1)} %get-tuple-element.38), channel_id=1, source_target_pairs={{0,4},{1,5},{4,6},{5,7},{6,2},{7,3},{2,0},{3,1},{8,12},{9,13},{12,... | collective-permute-start | bytes 393224 | tf_op jit(solution)/shard_map/ppermute | solution.py:123
  6.0 8.7 %collective-permute-start.3 = (bf16[256,256]{1,0:T(8,128)(2,1)S(1)}, bf16[256,256]{1,0:T(8,128)(2,1)S(1)}, u32[]{:S(2)}, u32[]{:S(2)}) collective-permute-start(bf16[256,256]{1,0:T(8,128)(2,1)S(1)} %get-tuple-element.37), channel_id=1, source_target_pairs={{0,4},{1,5},{4,6},{5,7},{6,2},{7,3},{2,0},{3,1},{8,12},{9,13},{12,... | collective-permute-start | bytes 393224 | tf_op jit(solution)/shard_map/ppermute | solution.py:123
  7.6 8.4 %collective-permute-start.2 = (bf16[256,256]{1,0:T(8,128)(2,1)S(1)}, bf16[256,256]{1,0:T(8,128)(2,1)S(1)}, u32[]{:S(2)}, u32[]{:S(2)}) collective-permute-start(bf16[256,256]{1,0:T(8,128)(2,1)S(1)} %get-tuple-element.36), channel_id=1, source_target_pairs={{0,4},{1,5},{4,6},{5,7},{6,2},{7,3},{2,0},{3,1},{8,12},{9,13},{12,... | collective-permute-start | bytes 393224 | tf_op jit(solution)/shard_map/ppermute | solution.py:123
  10.5 9.8 %collective-permute-start.4 = (f32[1,6144]{1,0:T(1,128)S(1)}, f32[1,6144]{1,0:T(1,128)S(1)}, u32[]{:S(2)}, u32[]{:S(2)}) collective-permute-start(f32[1,6144]{1,0:T(1,128)S(1)} %convert_element_type.92), channel_id=1, source_target_pairs={{0,8},{8,0},{16,24},{24,16},{1,9},{9,1},{17,25},{25,17},{2,10},{10... | collective-permute-start | bytes 73736 | tf_op jit(solution)/shard_map/ppermute | solution.py:70
  12.0 8.3 %collective-permute-start.5 = (bf16[256,256]{1,0:T(8,128)(2,1)S(1)}, bf16[256,256]{1,0:T(8,128)(2,1)S(1)}, u32[]{:S(2)}, u32[]{:S(2)}) collective-permute-start(bf16[256,256]{1,0:T(8,128)(2,1)S(1)} %collective-permute-done.1), channel_id=1, source_target_pairs={{0,4},{1,5},{4,6},{5,7},{6,2},{7,3},{2,0},{3,1},{8,12},{9,13},{12,... | collective-permute-start | bytes 393224 | tf_op jit(solution)/shard_map/ppermute | solution.py:142
  14.7 7.3 %collective-permute-start.7 = (bf16[256,256]{1,0:T(8,128)(2,1)S(1)}, bf16[256,256]{1,0:T(8,128)(2,1)S(1)}, u32[]{:S(2)}, u32[]{:S(2)}) collective-permute-start(bf16[256,256]{1,0:T(8,128)(2,1)S(1)} %collective-permute-done.3), channel_id=1, source_target_pairs={{0,4},{1,5},{4,6},{5,7},{6,2},{7,3},{2,0},{3,1},{8,12},{9,13},{12,... | collective-permute-start | bytes 393224 | tf_op jit(solution)/shard_map/ppermute | solution.py:142
  16.0 8.8 %collective-permute-start.6 = (bf16[256,256]{1,0:T(8,128)(2,1)S(1)}, bf16[256,256]{1,0:T(8,128)(2,1)S(1)}, u32[]{:S(2)}, u32[]{:S(2)}) collective-permute-start(bf16[256,256]{1,0:T(8,128)(2,1)S(1)} %collective-permute-done.2), channel_id=1, source_target_pairs={{0,4},{1,5},{4,6},{5,7},{6,2},{7,3},{2,0},{3,1},{8,12},{9,13},{12,... | collective-permute-start | bytes 393224 | tf_op jit(solution)/shard_map/ppermute | solution.py:142
  20.4 10.6 %collective-permute-start.8 = (bf16[256,256]{1,0:T(8,128)(2,1)S(1)}, bf16[256,256]{1,0:T(8,128)(2,1)S(1)}, u32[]{:S(2)}, u32[]{:S(2)}) collective-permute-start(bf16[256,256]{1,0:T(8,128)(2,1)S(1)} %collective-permute-done.5), channel_id=1, source_target_pairs={{0,4},{1,5},{4,6},{5,7},{6,2},{7,3},{2,0},{3,1},{8,12},{9,13},{12,... | collective-permute-start | bytes 393224 | tf_op jit(solution)/shard_map/ppermute | solution.py:142
  22.1 9.6 %collective-permute-start.10 = (bf16[256,256]{1,0:T(8,128)(2,1)S(1)}, bf16[256,256]{1,0:T(8,128)(2,1)S(1)}, u32[]{:S(2)}, u32[]{:S(2)}) collective-permute-start(bf16[256,256]{1,0:T(8,128)(2,1)S(1)} %collective-permute-done.7), channel_id=1, source_target_pairs={{0,4},{1,5},{4,6},{5,7},{6,2},{7,3},{2,0},{3,1},{8,12},{9,13},{12,... | collective-permute-start | bytes 393224 | tf_op jit(solution)/shard_map/ppermute | solution.py:142
  24.9 7.1 %collective-permute-start.9 = (bf16[256,256]{1,0:T(8,128)(2,1)S(1)}, bf16[256,256]{1,0:T(8,128)(2,1)S(1)}, u32[]{:S(2)}, u32[]{:S(2)}) collective-permute-start(bf16[256,256]{1,0:T(8,128)(2,1)S(1)} %collective-permute-done.6), channel_id=1, source_target_pairs={{0,4},{1,5},{4,6},{5,7},{6,2},{7,3},{2,0},{3,1},{8,12},{9,13},{12,... | collective-permute-start | bytes 393224 | tf_op jit(solution)/shard_map/ppermute | solution.py:142
  32.2 1.7 %collective-permute-start.11 = (f32[256,256]{0,1:T(8,128)S(1)}, f32[256,256]{0,1:T(8,128)S(1)}, u32[]{:S(2)}, u32[]{:S(2)}) collective-permute-start(f32[256,256]{0,1:T(8,128)S(1)} %slice.101), channel_id=1, source_target_pairs={{0,1},{1,0},{2,3},{3,2},{4,5},{5,4},{6,7},{7,6},{8,9},{9,8},{10,11... | collective-permute-start | bytes 786440 | tf_op jit(solution)/shard_map/ppermute | solution.py:150
  32.3 3.9 %collective-permute-start.22 = (f32[1,6144]{1,0:T(1,128)S(1)}, f32[1,6144]{1,0:T(1,128)S(1)}, u32[]{:S(2)}, u32[]{:S(2)}) collective-permute-start(f32[1,6144]{1,0:T(1,128)S(1)} %add.176), channel_id=1, source_target_pairs={{0,16},{8,24},{16,0},{24,8},{1,17},{9,25},{17,1},{25,9},{2,18},{10... | collective-permute-start | bytes 73736 | tf_op jit(solution)/shard_map/ppermute | solution.py:70
  35.3 1.6 %collective-permute-start.12 = (bf16[256,256]{0,1:T(8,128)(2,1)S(1)}, bf16[256,256]{0,1:T(8,128)(2,1)S(1)}, u32[]{:S(2)}, u32[]{:S(2)}) collective-permute-start(bf16[256,256]{0,1:T(8,128)(2,1)S(1)} %fusion.25), channel_id=1, source_target_pairs={{0,1},{1,0},{2,3},{3,2},{4,5},{5,4},{6,7},{7,6},{8,9},{9,8},{10,11... | collective-permute-start | bytes 393224 | tf_op jit(solution)/shard_map/ppermute | solution.py:152
  37.2 7.3 %collective-permute-start.13 = (bf16[256,256]{1,0:T(8,128)(2,1)S(1)}, bf16[256,256]{1,0:T(8,128)(2,1)S(1)}, u32[]{:S(2)}, u32[]{:S(2)}) collective-permute-start(bf16[256,256]{1,0:T(8,128)(2,1)S(1)} %convolution_convert_fusion.2), channel_id=1, source_target_pairs={{0,4},{1,5},{4,6},{5,7},{6,2},{7,3},{2,0},{3,1},{8,12},{9,13},{12,... | collective-permute-start | bytes 393224 | tf_op jit(solution)/shard_map/ppermute | solution.py:167
  41.2 7.0 %collective-permute-start.16 = (bf16[256,256]{1,0:T(8,128)(2,1)S(1)}, bf16[256,256]{1,0:T(8,128)(2,1)S(1)}, u32[]{:S(2)}, u32[]{:S(2)}) collective-permute-start(bf16[256,256]{1,0:T(8,128)(2,1)S(1)} %convolution_convert_fusion.1), channel_id=1, source_target_pairs={{0,4},{1,5},{4,6},{5,7},{6,2},{7,3},{2,0},{3,1},{8,12},{9,13},{12,... | collective-permute-start | bytes 393224 | tf_op jit(solution)/shard_map/ppermute | solution.py:167
  42.5 8.6 %collective-permute-start.19 = (bf16[256,256]{1,0:T(8,128)(2,1)S(1)}, bf16[256,256]{1,0:T(8,128)(2,1)S(1)}, u32[]{:S(2)}, u32[]{:S(2)}) collective-permute-start(bf16[256,256]{1,0:T(8,128)(2,1)S(1)} %convolution_convert_fusion), channel_id=1, source_target_pairs={{0,4},{1,5},{4,6},{5,7},{6,2},{7,3},{2,0},{3,1},{8,12},{9,13},{12,... | collective-permute-start | bytes 393224 | tf_op jit(solution)/shard_map/ppermute | solution.py:167
  44.8 9.1 %collective-permute-start.14 = (bf16[256,256]{1,0:T(8,128)(2,1)S(1)}, bf16[256,256]{1,0:T(8,128)(2,1)S(1)}, u32[]{:S(2)}, u32[]{:S(2)}) collective-permute-start(bf16[256,256]{1,0:T(8,128)(2,1)S(1)} %add_convert_fusion.5), channel_id=1, source_target_pairs={{0,4},{1,5},{4,6},{5,7},{6,2},{7,3},{2,0},{3,1},{8,12},{9,13},{12,... | collective-permute-start | bytes 393224 | tf_op jit(solution)/shard_map/ppermute | solution.py:167
  48.5 8.1 %collective-permute-start.17 = (bf16[256,256]{1,0:T(8,128)(2,1)S(1)}, bf16[256,256]{1,0:T(8,128)(2,1)S(1)}, u32[]{:S(2)}, u32[]{:S(2)}) collective-permute-start(bf16[256,256]{1,0:T(8,128)(2,1)S(1)} %add_convert_fusion.3), channel_id=1, source_target_pairs={{0,4},{1,5},{4,6},{5,7},{6,2},{7,3},{2,0},{3,1},{8,12},{9,13},{12,... | collective-permute-start | bytes 393224 | tf_op jit(solution)/shard_map/ppermute | solution.py:167
  51.3 8.1 %collective-permute-start.20 = (bf16[256,256]{1,0:T(8,128)(2,1)S(1)}, bf16[256,256]{1,0:T(8,128)(2,1)S(1)}, u32[]{:S(2)}, u32[]{:S(2)}) collective-permute-start(bf16[256,256]{1,0:T(8,128)(2,1)S(1)} %add_convert_fusion.1), channel_id=1, source_target_pairs={{0,4},{1,5},{4,6},{5,7},{6,2},{7,3},{2,0},{3,1},{8,12},{9,13},{12,... | collective-permute-start | bytes 393224 | tf_op jit(solution)/shard_map/ppermute | solution.py:167
  54.1 8.1 %collective-permute-start.15 = (bf16[256,256]{1,0:T(8,128)(2,1)S(1)}, bf16[256,256]{1,0:T(8,128)(2,1)S(1)}, u32[]{:S(2)}, u32[]{:S(2)}) collective-permute-start(bf16[256,256]{1,0:T(8,128)(2,1)S(1)} %add_convert_fusion.4), channel_id=1, source_target_pairs={{0,4},{1,5},{4,6},{5,7},{6,2},{7,3},{2,0},{3,1},{8,12},{9,13},{12,... | collective-permute-start | bytes 393224 | tf_op jit(solution)/shard_map/ppermute | solution.py:171
  56.9 7.6 %collective-permute-start.18 = (bf16[256,256]{1,0:T(8,128)(2,1)S(1)}, bf16[256,256]{1,0:T(8,128)(2,1)S(1)}, u32[]{:S(2)}, u32[]{:S(2)}) collective-permute-start(bf16[256,256]{1,0:T(8,128)(2,1)S(1)} %add_convert_fusion.2), channel_id=1, source_target_pairs={{0,4},{1,5},{4,6},{5,7},{6,2},{7,3},{2,0},{3,1},{8,12},{9,13},{12,... | collective-permute-start | bytes 393224 | tf_op jit(solution)/shard_map/ppermute | solution.py:171
  59.7 6.2 %collective-permute-start.21 = (bf16[256,256]{1,0:T(8,128)(2,1)S(1)}, bf16[256,256]{1,0:T(8,128)(2,1)S(1)}, u32[]{:S(2)}, u32[]{:S(2)}) collective-permute-start(bf16[256,256]{1,0:T(8,128)(2,1)S(1)} %add_convert_fusion), channel_id=1, source_target_pairs={{0,4},{1,5},{4,6},{5,7},{6,2},{7,3},{2,0},{3,1},{8,12},{9,13},{12,... | collective-permute-start | bytes 393224 | tf_op jit(solution)/shard_map/ppermute | solution.py:171
  (5 other events, 49.2 us)
